TPU v7x, 128 devices: a whole 4x4x4 slice. The times are simulated.
128 devices in a mesh: row: 16 (over z, x_hi, core), col: 8 (over x_lo, y).
Axes of the slice: x: 4 (x_hi: 2, x_lo: 2; x = x_hi * 2 + x_lo), y: 4, z: 4, core: 2. Of those that a mesh axis runs over, the one named last changes fastest.
Arguments:
- layer_input: bfloat16 [4096, 1024], P('row', 'col'), may hold values from -6 to 6
- query_weight: bfloat16 [2, 1024, 1024], P(None, 'row', 'col'), may hold values from -0.1875 to 0.1875
- key_weight: bfloat16 [2, 1024, 1024], P(None, 'row', 'col'), may hold values from -0.1875 to 0.1875
- value_weight: bfloat16 [2, 1024, 1024], P(None, 'row', 'col'), may hold values from -0.1875 to 0.1875
- proj_weight: bfloat16 [2, 1024, 1024], P(None, 'row', 'col'), may hold values from -1.5 to 1.5
- up_weight: bfloat16 [2, 1024, 4096], P(None, 'row', 'col'), may hold values from -0.1875 to 0.1875
- down_weight: bfloat16 [2, 4096, 1024], P(None, 'row', 'col'), may hold values from -0.09375 to 0.09375
- query_shift: bfloat16 [2, 1024], P(None, 'col'), may hold values from -1.75 to 1.75
- value_shift: bfloat16 [2, 1024], P(None, 'col'), may hold values from -0.125 to 0.125
- proj_shift: bfloat16 [2, 1024], P(None, 'col'), may hold values from -1.75 to 1.75
- up_shift: bfloat16 [2, 4096], P(None, 'col'), may hold values from -1.75 to 1.75
- down_shift: bfloat16 [2, 1024], P(None, 'col'), may hold values from -1.75 to 1.75
- first_gain: bfloat16 [2, 1024], P(None, 'col'), may hold values from 0.5 to 1.5
- first_shift: bfloat16 [2, 1024], P(None, 'col'), may hold values from -1.75 to 1.75
- second_gain: bfloat16 [2, 1024], P(None, 'col'), may hold values from 0.5 to 1.5
- second_shift: bfloat16 [2, 1024], P(None, 'col'), may hold values from -1.75 to 1.75
- segment_ids: int32 [4096], replicated, may hold values from 0 to 5, as said below
- cotangent: bfloat16 [4096, 1024], P('row', 'col'), may hold values from -6 to 6
Outputs:
- activations: bfloat16 [4096, 1024], P('row', 'col')
- input_grad: float32 [4096, 1024], P('row', 'col')
- query_grads: float32 [2, 1024, 1024], P(None, 'row', 'col')
- key_grads: float32 [2, 1024, 1024], P(None, 'row', 'col')
- value_grads: float32 [2, 1024, 1024], P(None, 'row', 'col')
- proj_grads: float32 [2, 1024, 1024], P(None, 'row', 'col')
- up_grads: float32 [2, 1024, 4096], P(None, 'row', 'col')
- down_grads: float32 [2, 4096, 1024], P(None, 'row', 'col')
- query_shift_grads: float32 [2, 1024], P(None, 'col')
- value_shift_grads: float32 [2, 1024], P(None, 'col')
- proj_shift_grads: float32 [2, 1024], P(None, 'col')
- up_shift_grads: float32 [2, 4096], P(None, 'col')
- down_shift_grads: float32 [2, 1024], P(None, 'col')
- first_gain_grads: float32 [2, 1024], P(None, 'col')
- first_shift_grads: float32 [2, 1024], P(None, 'col')
- second_gain_grads: float32 [2, 1024], P(None, 'col')
- second_shift_grads: float32 [2, 1024], P(None, 'col')
Inputs may be any that keep to these rules, and one draw needn't show every extreme that they name: `segment_ids`: A token's document number depends only on its place within its block of 256 tokens (its index modulo 256), so every document has equally many tokens in each block; within a block the numbers never fall; document 0 holds the first 64 places of every block, and no document holds more places of a block.
All inputs are finite; a program needn't handle non-finite values.
Results may differ from a plain program's by a relative error of at most 0.035.
Values may be sent and summed in bfloat16 or wider, within the bound.
A program may use at most 128 MiB of HBM per device.

v0:
```python
from functools import partial

import jax
import jax.numpy as jnp
from jax import lax
from jax.sharding import PartitionSpec as P

D = 1024
HEADS = 16
LAYERS = 2
HEAD_DIM = 64


def matmul(left_op, right_op):
    return jnp.dot(left_op, right_op, preferred_element_type=jnp.float32)


def times_back(left_op, right_op):
    return lax.dot_general(
        left_op, right_op, (((1,), (1,)), ((), ())), preferred_element_type=jnp.float32
    )


def over_rows(left_op, right_op):
    return lax.dot_general(
        left_op, right_op, (((0,), (0,)), ((), ())), preferred_element_type=jnp.float32
    )


def spread(local_part):
    return lax.all_gather(local_part, "col", axis=1, tiled=True)


def pass_single(grad_low, full_w):
    return lax.psum_scatter(
        times_back(grad_low, full_w).astype(jnp.bfloat16), "col", scatter_dimension=1, tiled=True
    ).astype(jnp.float32)


def pass_three(query_low, key_low, value_low, full_ws):
    partial_sum = (
        times_back(query_low, full_ws[0])
        + times_back(key_low, full_ws[1])
        + times_back(value_low, full_ws[2])
    )
    return lax.psum_scatter(
        partial_sum.astype(jnp.bfloat16), "col", scatter_dimension=1, tiled=True
    ).astype(jnp.float32)


def layer_norm(summed, gain_vec, shift_vec):
    totals, squares = lax.psum((jnp.sum(summed, axis=1), jnp.sum(summed * summed, axis=1)), "col")
    average = totals / D
    variance = squares / D - average * average
    inv_spread = lax.rsqrt(variance + 1e-12)
    normed = (summed - average[:, None]) * inv_spread[:, None]
    return (normed * gain_vec + shift_vec, normed, inv_spread)


def norm_back(grad_in, normed, inv_spread, gain_vec):
    scaled = grad_in * gain_vec
    first_sum, second_sum = lax.psum(
        (jnp.sum(scaled, axis=1), jnp.sum(scaled * normed, axis=1)), "col"
    )
    grad_out = inv_spread[:, None] * (
        scaled - first_sum[:, None] / D - normed * (second_sum[:, None] / D)
    )
    return (grad_out, jnp.sum(grad_in * normed, axis=0), jnp.sum(grad_in, axis=0))


def masked_scores(queries, key_part, own_ids, id_part):
    raw_scores = jnp.einsum(
        "qhd,khd->hqk", queries, key_part, preferred_element_type=jnp.float32
    ) * HEAD_DIM ** (-0.5)
    return jnp.where((own_ids[:, None] == id_part[None, :])[None], raw_scores, -1000000000.0)


def split_blocks(key_rows, value_rows, key_ids, key_block, head_count):
    blocks = key_rows.shape[0] // key_block
    key_parts = key_rows.reshape(blocks, key_block, head_count, HEAD_DIM)
    value_parts = value_rows.reshape(blocks, key_block, head_count, HEAD_DIM)
    return (key_parts, value_parts, key_ids.reshape(blocks, key_block))


def attend_forward(queries, key_parts, value_parts, id_parts, own_ids):
    tok_rows, head_count, head_dim = queries.shape

    def stat_step(state_now, operands):
        highest, summed = state_now
        scores = masked_scores(queries, operands[0], own_ids, operands[1])
        new_high = jnp.maximum(highest, jnp.max(scores, axis=2))
        summed = summed * jnp.exp(highest - new_high) + jnp.sum(
            jnp.exp(scores - new_high[:, :, None]), axis=2
        )
        return ((new_high, summed), None)

    start_high = jnp.full((head_count, tok_rows), -1e30, jnp.float32)
    start_sum = jnp.zeros((head_count, tok_rows), jnp.float32)
    (highest, summed), unused = lax.scan(stat_step, (start_high, start_sum), (key_parts, id_parts))
    log_total = highest + jnp.log(summed)

    def out_step(out_sum, operands):
        key_part, value_part, id_part = operands
        attn_probs = jnp.exp(
            masked_scores(queries, key_part, own_ids, id_part) - log_total[:, :, None]
        )
        attn_probs = attn_probs.astype(jnp.bfloat16)
        return (
            out_sum
            + jnp.einsum(
                "hqk,khd->qhd", attn_probs, value_part, preferred_element_type=jnp.float32
            ),
            None,
        )

    start_out = jnp.zeros((tok_rows, head_count, head_dim), jnp.float32)
    attended, unused = lax.scan(out_step, start_out, (key_parts, value_parts, id_parts))
    return (attended, log_total)


def attend_backward(
    queries, key_parts, value_parts, id_parts, own_ids, log_total, out_grad, row_delta
):
    score_scale = HEAD_DIM ** (-0.5)

    def back_step(query_sum, operands):
        key_part, value_part, id_part = operands
        attn_probs = jnp.exp(
            masked_scores(queries, key_part, own_ids, id_part) - log_total[:, :, None]
        )
        value_grad = jnp.einsum(
            "hqk,qhd->khd",
            attn_probs.astype(jnp.bfloat16),
            out_grad,
            preferred_element_type=jnp.float32,
        )
        prob_grad = jnp.einsum(
            "qhd,khd->hqk", out_grad, value_part, preferred_element_type=jnp.float32
        )
        score_grad = (attn_probs * (prob_grad - row_delta[:, :, None])).astype(jnp.bfloat16)
        query_sum = (
            query_sum
            + jnp.einsum("hqk,khd->qhd", score_grad, key_part, preferred_element_type=jnp.float32)
            * score_scale
        )
        key_grad = (
            jnp.einsum("hqk,qhd->khd", score_grad, queries, preferred_element_type=jnp.float32)
            * score_scale
        )
        return (query_sum, (key_grad, value_grad))

    start_grad = jnp.zeros(queries.shape, jnp.float32)
    query_sum, (key_grads, value_grads) = lax.scan(
        back_step, start_grad, (key_parts, value_parts, id_parts)
    )
    total_rows = key_grads.shape[0] * key_grads.shape[1]
    return (query_sum, key_grads.reshape(total_rows, -1), value_grads.reshape(total_rows, -1))


def body(
    layer_input,
    query_weight,
    key_weight,
    value_weight,
    proj_weight,
    up_weight,
    down_weight,
    query_shift,
    value_shift,
    proj_shift,
    up_shift,
    down_shift,
    first_gain,
    first_shift,
    second_gain,
    second_shift,
    segment_ids,
    cotangent,
):
    tok_rows = layer_input.shape[0]
    total_rows = tok_rows * lax.axis_size("row")
    key_block = min(512, total_rows)
    head_count = HEADS // lax.axis_size("col")
    own_ids = lax.dynamic_slice_in_dim(segment_ids, lax.axis_index("row") * tok_rows, tok_rows)
    hidden = layer_input.astype(jnp.float32)
    kept_state = []
    for layer_index in range(LAYERS):
        gathered_w = (
            lax.all_gather(query_weight[layer_index], "row", axis=0, tiled=True),
            lax.all_gather(key_weight[layer_index], "row", axis=0, tiled=True),
            lax.all_gather(value_weight[layer_index], "row", axis=0, tiled=True),
            lax.all_gather(proj_weight[layer_index], "row", axis=0, tiled=True),
            lax.all_gather(up_weight[layer_index], "row", axis=0, tiled=True),
            lax.all_gather(down_weight[layer_index], "row", axis=0, tiled=True),
        )
        query_full, key_full, value_full, proj_full, up_full, down_full = gathered_w
        inputs = hidden.astype(jnp.bfloat16)
        inputs_full = spread(inputs)
        queries = (matmul(inputs_full, query_full) + query_shift[layer_index]).astype(jnp.bfloat16)
        key_rows = matmul(inputs_full, key_full).astype(jnp.bfloat16)
        value_rows = (matmul(inputs_full, value_full) + value_shift[layer_index]).astype(
            jnp.bfloat16
        )
        key_all, value_all = (
            lax.all_gather(key_rows, "row", axis=0, tiled=True),
            lax.all_gather(value_rows, "row", axis=0, tiled=True),
        )
        key_parts, value_parts, id_parts = split_blocks(
            key_all, value_all, segment_ids, key_block, head_count
        )
        head_queries = queries.reshape(tok_rows, head_count, HEAD_DIM)
        attended, log_total = attend_forward(
            head_queries, key_parts, value_parts, id_parts, own_ids
        )
        attn_low = attended.reshape(tok_rows, -1).astype(jnp.bfloat16)
        attn_full = spread(attn_low)
        projected = matmul(attn_full, proj_full) + proj_shift[layer_index]
        first_out, first_normed, first_inv = layer_norm(
            hidden + projected, first_gain[layer_index], first_shift[layer_index]
        )
        up_in = first_out.astype(jnp.bfloat16)
        up_in_full = spread(up_in)
        up_pre = matmul(up_in_full, up_full) + up_shift[layer_index]
        gated_act = jax.nn.gelu(up_pre, approximate=False).astype(jnp.bfloat16)
        gated_full = spread(gated_act)
        down_out = matmul(gated_full, down_full) + down_shift[layer_index]
        hidden, second_normed, second_inv = layer_norm(
            first_out + down_out, second_gain[layer_index], second_shift[layer_index]
        )
        kept_state.append(
            (
                gathered_w,
                inputs,
                inputs_full,
                head_queries,
                key_parts,
                value_parts,
                id_parts,
                attended,
                log_total,
                attn_low,
                attn_full,
                first_normed,
                first_inv,
                up_in,
                up_in_full,
                up_pre,
                gated_act,
                gated_full,
                second_normed,
                second_inv,
            )
        )
    activations = hidden.astype(jnp.bfloat16)
    grad_hidden = cotangent.astype(jnp.float32)
    layer_grads = [0] * LAYERS
    for layer_index in reversed(range(LAYERS)):
        (
            gathered_w,
            inputs,
            inputs_full,
            head_queries,
            key_parts,
            value_parts,
            id_parts,
            attended,
            log_total,
            attn_low,
            attn_full,
            first_normed,
            first_inv,
            up_in,
            up_in_full,
            up_pre,
            gated_act,
            gated_full,
            second_normed,
            second_inv,
        ) = kept_state[layer_index]
        query_full, key_full, value_full, proj_full, up_full, down_full = gathered_w
        second_grad, second_gain_g, second_shift_g = norm_back(
            grad_hidden, second_normed, second_inv, second_gain[layer_index]
        )
        down_low = second_grad.astype(jnp.bfloat16)
        down_shift_g = jnp.sum(down_low, axis=0, dtype=jnp.float32)
        down_w_g = over_rows(gated_full, down_low)
        gated_grad = pass_single(down_low, down_full)
        gelu_value, gelu_pull = jax.vjp(partial(jax.nn.gelu, approximate=False), up_pre)
        up_low = gelu_pull(gated_grad)[0].astype(jnp.bfloat16)
        up_shift_g = jnp.sum(up_low, axis=0, dtype=jnp.float32)
        up_w_g = over_rows(up_in_full, up_low)
        first_in_grad = second_grad + pass_single(up_low, up_full)
        first_grad, first_gain_g, first_shift_g = norm_back(
            first_in_grad, first_normed, first_inv, first_gain[layer_index]
        )
        proj_low = first_grad.astype(jnp.bfloat16)
        proj_shift_g = jnp.sum(proj_low, axis=0, dtype=jnp.float32)
        proj_w_g = over_rows(attn_full, proj_low)
        attn_grad = pass_single(proj_low, proj_full).astype(jnp.bfloat16)
        attn_grad = attn_grad.reshape(attended.shape)
        row_delta = jnp.sum(attn_grad.astype(jnp.float32) * attended, axis=2).T
        query_sum, key_all_g, value_all_g = attend_backward(
            head_queries, key_parts, value_parts, id_parts, own_ids, log_total, attn_grad, row_delta
        )
        key_sum, value_sum = (
            lax.psum_scatter(
                key_all_g.astype(jnp.bfloat16), "row", scatter_dimension=0, tiled=True
            ).astype(jnp.float32),
            lax.psum_scatter(
                value_all_g.astype(jnp.bfloat16), "row", scatter_dimension=0, tiled=True
            ).astype(jnp.float32),
        )
        query_low = query_sum.reshape(query_sum.shape[0], -1).astype(jnp.bfloat16)
        key_low = key_sum.astype(jnp.bfloat16)
        value_low = value_sum.astype(jnp.bfloat16)
        query_shift_g = jnp.sum(query_low, axis=0, dtype=jnp.float32)
        value_shift_g = jnp.sum(value_low, axis=0, dtype=jnp.float32)
        query_w_g = over_rows(inputs_full, query_low)
        key_w_g = over_rows(inputs_full, key_low)
        value_w_g = over_rows(inputs_full, value_low)
        grad_hidden = first_grad + pass_three(
            query_low, key_low, value_low, (query_full, key_full, value_full)
        )
        query_w_g, key_w_g, value_w_g, proj_w_g, up_w_g, down_w_g = (
            lax.psum_scatter(
                query_w_g.astype(jnp.bfloat16), "row", scatter_dimension=0, tiled=True
            ).astype(jnp.float32),
            lax.psum_scatter(
                key_w_g.astype(jnp.bfloat16), "row", scatter_dimension=0, tiled=True
            ).astype(jnp.float32),
            lax.psum_scatter(
                value_w_g.astype(jnp.bfloat16), "row", scatter_dimension=0, tiled=True
            ).astype(jnp.float32),
            lax.psum_scatter(
                proj_w_g.astype(jnp.bfloat16), "row", scatter_dimension=0, tiled=True
            ).astype(jnp.float32),
            lax.psum_scatter(
                up_w_g.astype(jnp.bfloat16), "row", scatter_dimension=0, tiled=True
            ).astype(jnp.float32),
            lax.psum_scatter(
                down_w_g.astype(jnp.bfloat16), "row", scatter_dimension=0, tiled=True
            ).astype(jnp.float32),
        )
        vector_sums = lax.psum(
            (
                query_shift_g,
                value_shift_g,
                proj_shift_g,
                up_shift_g,
                down_shift_g,
                first_gain_g,
                first_shift_g,
                second_gain_g,
                second_shift_g,
            ),
            "row",
        )
        layer_grads[layer_index] = (
            query_w_g,
            key_w_g,
            value_w_g,
            proj_w_g,
            up_w_g,
            down_w_g,
        ) + tuple(vector_sums)
    stacked = [
        jnp.stack([layer_grads[layer_index][member] for layer_index in range(LAYERS)])
        for member in range(15)
    ]
    return (
        activations,
        grad_hidden,
        stacked[0],
        stacked[1],
        stacked[2],
        stacked[3],
        stacked[4],
        stacked[5],
        stacked[6],
        stacked[7],
        stacked[8],
        stacked[9],
        stacked[10],
        stacked[11],
        stacked[12],
        stacked[13],
        stacked[14],
    )


def solution(mesh):
    return jax.shard_map(
        body,
        mesh=mesh,
        in_specs=(
            P("row", "col"),
            P(None, "row", "col"),
            P(None, "row", "col"),
            P(None, "row", "col"),
            P(None, "row", "col"),
            P(None, "row", "col"),
            P(None, "row", "col"),
            P(None, "col"),
            P(None, "col"),
            P(None, "col"),
            P(None, "col"),
            P(None, "col"),
            P(None, "col"),
            P(None, "col"),
            P(None, "col"),
            P(None, "col"),
            P(),
            P("row", "col"),
        ),
        out_specs=(
            P("row", "col"),
            P("row", "col"),
            P(None, "row", "col"),
            P(None, "row", "col"),
            P(None, "row", "col"),
            P(None, "row", "col"),
            P(None, "row", "col"),
            P(None, "row", "col"),
            P(None, "col"),
            P(None, "col"),
            P(None, "col"),
            P(None, "col"),
            P(None, "col"),
            P(None, "col"),
            P(None, "col"),
            P(None, "col"),
            P(None, "col"),
        ),
        check_vma=False,
    )
```

profile of v0, /device:TPU:2, one launch (start us, length us, event | category | flops | bytes accessed | tf_op | source)
XLA Modules:
  0.0 2190.7 jit_solution(10914932541320285747)
XLA Ops:
  7.3 26.0 %all_gather.72 = bf16[256,1024]{1,0:T(8,128)(2,1)S(1)} all-gather(bf16[256,128]{1,0:T(8,128)(2,1)} %param.30), channel_id=1, replica_groups=mesh['row'=16,'col'=8] {'col'}, dimensions={1}, use_global_device_ids=true | all-gather | bytes 589824 | tf_op jit(solution)/shard_map/all_gather | solution.py:31
  34.1 25.5 %all-gather = bf16[1,1024,128]{2,1,0:T(8,128)(2,1)S(1)} all-gather(bf16[1,64,128]{2,1,0:T(8,128)(2,1)S(1)} %get-tuple-element.911), channel_id=2, replica_groups=mesh['row'=16,'col'=8] {'row'}, dimensions={1}, use_global_device_ids=true | all-gather | bytes 278528 | tf_op jit(solution)/shard_map/all_gather | solution.py:191
  62.1 20.3 all-gather.1
  86.0 23.2 %all-gather.2 = bf16[1,1024,128]{2,1,0:T(8,128)(2,1)S(1)} all-gather(bf16[1,64,128]{2,1,0:T(8,128)(2,1)S(1)} %get-tuple-element.907), channel_id=4, replica_groups=mesh['row'=16,'col'=8] {'row'}, dimensions={1}, use_global_device_ids=true | all-gather | bytes 278528 | tf_op jit(solution)/shard_map/all_gather | solution.py:189
  109.2 20.5 all-gather.3
  130.2 3.9 reshape.337
  134.0 3.5 copy.135
  137.5 10.7 all-gather.25.cloned.1.call-done
  148.2 3.9 reshape.338
  152.1 3.5 copy.136
  155.6 13.3 while.78
  168.9 14.1 while.79
  183.0 29.4 %all_gather.78 = bf16[256,1024]{0,1:T(8,128)(2,1)S(1)} all-gather(bf16[256,128]{0,1:T(8,128)(2,1)S(1)} %bitcast.526), channel_id=1, replica_groups=mesh['row'=16,'col'=8] {'col'}, dimensions={1}, use_global_device_ids=true | all-gather | bytes 589824 | tf_op jit(solution)/shard_map/all_gather | solution.py:31
  213.5 19.4 all-reduce.8
  233.1 28.8 %all_gather.80 = bf16[256,1024]{0,1:T(8,128)(2,1)S(1)} all-gather(bf16[256,128]{0,1:T(8,128)(2,1)S(1)} %fusion.174), channel_id=1, replica_groups=mesh['row'=16,'col'=8] {'col'}, dimensions={1}, use_global_device_ids=true | all-gather | bytes 589824 | tf_op jit(solution)/shard_map/all_gather | solution.py:31
  261.9 4.0 multiply_convert_fusion.1
  266.0 22.6 %all-gather.6 = bf16[1,1024,128]{2,1,0:T(8,128)(2,1)S(1)} all-gather(bf16[1,64,128]{2,1,0:T(8,128)(2,1)S(1)} %get-tuple-element.910), channel_id=8, replica_groups=mesh['row'=16,'col'=8] {'row'}, dimensions={1}, use_global_device_ids=true | all-gather | bytes 278528 | tf_op jit(solution)/shard_map/all_gather | solution.py:191
  288.7 15.5 all-gather.27.cloned.1.call-done
  306.9 18.1 all-reduce.7
  325.2 28.8 %all_gather.84 = bf16[256,1024]{0,1:T(8,128)(2,1)S(1)} all-gather(bf16[256,128]{0,1:T(8,128)(2,1)S(1)} %fusion.175), channel_id=1, replica_groups=mesh['row'=16,'col'=8] {'col'}, dimensions={1}, use_global_device_ids=true | all-gather | bytes 589824 | tf_op jit(solution)/shard_map/all_gather | solution.py:31
  355.0 24.4 %all-gather.7 = bf16[1,1024,128]{2,1,0:T(8,128)(2,1)S(1)} all-gather(bf16[1,64,128]{2,1,0:T(8,128)(2,1)S(1)} %get-tuple-element.908), channel_id=9, replica_groups=mesh['row'=16,'col'=8] {'row'}, dimensions={1}, use_global_device_ids=true | all-gather | bytes 278528 | tf_op jit(solution)/shard_map/all_gather | solution.py:190
  382.1 21.1 all-gather.8
  403.2 23.8 %all-gather.9 = bf16[1,1024,128]{2,1,0:T(8,128)(2,1)} all-gather(bf16[1,64,128]{2,1,0:T(8,128)(2,1)S(1)} %get-tuple-element.904), channel_id=11, replica_groups=mesh['row'=16,'col'=8] {'row'}, dimensions={1}, use_global_device_ids=true | all-gather | bytes 278528 | tf_op jit(solution)/shard_map/all_gather | solution.py:192
  427.4 3.9 reshape.339
  434.7 10.8 all-gather.31.cloned.1.call-done
  445.5 3.9 reshape.340
  452.9 13.3 while.80
  466.2 14.1 while.81
  480.4 29.4 %all_gather.90 = bf16[256,1024]{0,1:T(8,128)(2,1)S(1)} all-gather(bf16[256,128]{0,1:T(8,128)(2,1)S(1)} %bitcast.527), channel_id=1, replica_groups=mesh['row'=16,'col'=8] {'col'}, dimensions={1}, use_global_device_ids=true | all-gather | bytes 589824 | tf_op jit(solution)/shard_map/all_gather | solution.py:31
  510.1 19.3 all-reduce.6
  529.6 28.9 %all_gather.92 = bf16[256,1024]{0,1:T(8,128)(2,1)S(1)} all-gather(bf16[256,128]{0,1:T(8,128)(2,1)S(1)} %fusion.176), channel_id=1, replica_groups=mesh['row'=16,'col'=8] {'col'}, dimensions={1}, use_global_device_ids=true | all-gather | bytes 589824 | tf_op jit(solution)/shard_map/all_gather | solution.py:31
  558.5 4.0 multiply_convert_fusion
  562.7 38.0 %all-gather.33.cloned.1.call-done = bf16[256,4096]{1,0:T(8,128)(2,1)} async-done(((bf16[256,512]{1,0:T(8,128)(2,1)}), bf16[256,4096]{1,0:T(8,128)(2,1)}) %all-gather.33.cloned.1.call-update) | async-done | bytes 2097168 | tf_op jit(solution)/shard_map/all_gather | solution.py:31
  603.4 17.1 all-reduce.5
  621.1 16.8 all-reduce.4
  640.9 41.8 %reduce-scatter.41.cloned.1.call-done = bf16[256,512]{1,0:T(8,128)(2,1)} async-done(((bf16[256,4096]{1,0:T(8,128)(2,1)}), bf16[256,512]{1,0:T(8,128)(2,1)}) %reduce-scatter.41.cloned.1.call-update) | async-done | bytes 262160 | tf_op jit(solution)/shard_map/reduce_scatter | solution.py:35
  687.3 36.5 %reduce-scatter.43.cloned.1.call-done = bf16[256,128]{0,1:T(8,128)(2,1)} async-done(((bf16[256,1024]{0,1:T(8,128)(2,1)}), bf16[256,128]{0,1:T(8,128)(2,1)}) %reduce-scatter.43.cloned.1.call-update) | async-done | bytes 65552 | tf_op jit(solution)/shard_map/reduce_scatter | solution.py:35
  725.9 17.4 all-reduce.3
  745.1 36.1 %reduce-scatter.73.cloned.1.call-done = bf16[128,256]{1,0:T(8,128)(2,1)} async-done(((bf16[1024,256]{1,0:T(8,128)(2,1)}), bf16[128,256]{1,0:T(8,128)(2,1)}) %reduce-scatter.73.cloned.1.call-update) | async-done | bytes 65552
  784.3 52.0 %while.82 = (s32[]{:T(128)}, f32[256,2,64]{0,2,1:T(8,128)S(1)}, bf16[8,512,2,64]{1,3,2,0:T(8,128)(2,1)}, bf16[8,512,2,64]{1,3,2,0:T(8,128)(2,1)}, bf16[8,512,2,6...) while((s32[]{:T(128)}, f32[256,2,64]{0,2,1:T(8,128)S(1)}, ...), condition=%wide.region_41.42_spmd.clone, body=%wide.region_40.41_spmd.clone.sunk | while | flops 169902080 | bytes 6433967 | solution.py:153
  842.9 62.8 %reduce-scatter.45.cloned.1.call-done = bf16[256,128]{0,1:T(8,128)(2,1)} async-done(((bf16[4096,128]{0,1:T(8,128)(2,1)}), bf16[256,128]{0,1:T(8,128)(2,1)}) %reduce-scatter.45.cloned.1.call-update) | async-done | bytes 65552 | tf_op jit(solution)/shard_map/reduce_scatter | solution.py:306
  906.9 68.9 %reduce-scatter.47.cloned.1.call-done = bf16[256,128]{0,1:T(8,128)(2,1)} async-done(((bf16[4096,128]{0,1:T(8,128)(2,1)}), bf16[256,128]{0,1:T(8,128)(2,1)}) %reduce-scatter.47.cloned.1.call-update) | async-done | bytes 65552 | tf_op jit(solution)/shard_map/reduce_scatter | solution.py:309
  977.9 36.5 %reduce-scatter.49.cloned.1.call-done = bf16[256,128]{0,1:T(8,128)(2,1)} async-done(((bf16[256,1024]{0,1:T(8,128)(2,1)}), bf16[256,128]{0,1:T(8,128)(2,1)}) %reduce-scatter.49.cloned.1.call-update) | async-done | bytes 65552 | tf_op jit(solution)/shard_map/reduce_scatter | solution.py:46
  1016.1 17.4 all-reduce.2
  1036.7 41.4 %reduce-scatter.51.cloned.1.call-done = bf16[256,512]{1,0:T(8,128)(2,1)} async-done(((bf16[256,4096]{1,0:T(8,128)(2,1)}), bf16[256,512]{1,0:T(8,128)(2,1)}) %reduce-scatter.51.cloned.1.call-update) | async-done | bytes 262160 | tf_op jit(solution)/shard_map/reduce_scatter | solution.py:35
  1081.1 36.4 %reduce-scatter.53.cloned.1.call-done = bf16[256,128]{0,1:T(8,128)(2,1)} async-done(((bf16[256,1024]{0,1:T(8,128)(2,1)}), bf16[256,128]{0,1:T(8,128)(2,1)}) %reduce-scatter.53.cloned.1.call-update) | async-done | bytes 65552 | tf_op jit(solution)/shard_map/reduce_scatter | solution.py:35
  1119.0 17.5 all-reduce.1
  1154.8 21.1 reduce-scatter.75.cloned.1.call-done
  1178.0 46.7 %while.83 = (s32[]{:T(128)}, f32[256,2,64]{0,2,1:T(8,128)S(1)}, bf16[8,512,2,64]{1,3,2,0:T(8,128)(2,1)S(1)}, bf16[8,512,2,64]{1,3,2,0:T(8,128)(2,1)}, bf16[8,512...) while((s32[]{:T(128)}, f32[256,2,64]{0,2,1:T(8,128)S(1)}, ...), condition=%wide.region_58.59_spmd.clone, body=%wide.region_57.58_spmd.clone.sunk | while | flops 169902080 | bytes 6433967 | solution.py:153
  1231.0 13.8 reduce-scatter.79.cloned.1.call-done
  1245.7 68.0 %reduce-scatter.83.cloned.1.call-done = bf16[64,128]{1,0:T(8,128)(2,1)} async-done(((bf16[1024,128]{1,0:T(8,128)(2,1)}), bf16[64,128]{1,0:T(8,128)(2,1)}) %reduce-scatter.83.cloned.1.call-update) | async-done | bytes 16400
  1314.5 67.5 %reduce-scatter.87.cloned.1.call-done = bf16[64,128]{1,0:T(8,128)(2,1)} async-done(((bf16[1024,128]{1,0:T(8,128)(2,1)}), bf16[64,128]{1,0:T(8,128)(2,1)}) %reduce-scatter.87.cloned.1.call-update) | async-done | bytes 16400
  1382.9 69.4 %reduce-scatter.71.cloned.1.call-done = bf16[256,128]{1,0:T(8,128)(2,1)} async-done(((bf16[4096,128]{1,0:T(8,128)(2,1)}), bf16[256,128]{1,0:T(8,128)(2,1)}) %reduce-scatter.71.cloned.1.call-update) | async-done | bytes 65552 | tf_op jit(solution)/shard_map/reduce_scatter | solution.py:340
  1452.3 69.7 %reduce-scatter.69.cloned.1.call-done = bf16[256,128]{1,0:T(8,128)(2,1)} async-done(((bf16[4096,128]{1,0:T(8,128)(2,1)}), bf16[256,128]{1,0:T(8,128)(2,1)}) %reduce-scatter.69.cloned.1.call-update) | async-done | bytes 65552 | tf_op jit(solution)/shard_map/reduce_scatter | solution.py:340
  1523.6 66.8 %reduce-scatter.63.cloned.1.call-done = bf16[64,128]{1,0:T(8,128)(2,1)} async-done(((bf16[1024,128]{1,0:T(8,128)(2,1)}), bf16[64,128]{1,0:T(8,128)(2,1)}) %reduce-scatter.63.cloned.1.call-update) | async-done | bytes 16400 | tf_op jit(solution)/shard_map/reduce_scatter | solution.py:334
  1590.4 68.2 %reduce-scatter.61.cloned.1.call-done = bf16[64,128]{1,0:T(8,128)(2,1)} async-done(((bf16[1024,128]{1,0:T(8,128)(2,1)}), bf16[64,128]{1,0:T(8,128)(2,1)}) %reduce-scatter.61.cloned.1.call-update) | async-done | bytes 16400 | tf_op jit(solution)/shard_map/reduce_scatter | solution.py:334
  1659.9 68.8 %reduce-scatter.67.cloned.1.call-done = bf16[64,512]{1,0:T(8,128)(2,1)} async-done(((bf16[1024,512]{1,0:T(8,128)(2,1)}), bf16[64,512]{1,0:T(8,128)(2,1)}) %reduce-scatter.67.cloned.1.call-update) | async-done | bytes 65552 | tf_op jit(solution)/shard_map/reduce_scatter | solution.py:337
  1728.7 69.8 %reduce-scatter.65.cloned.1.call-done = bf16[64,512]{1,0:T(8,128)(2,1)} async-done(((bf16[1024,512]{1,0:T(8,128)(2,1)}), bf16[64,512]{1,0:T(8,128)(2,1)}) %reduce-scatter.65.cloned.1.call-update) | async-done | bytes 65552 | tf_op jit(solution)/shard_map/reduce_scatter | solution.py:337
  1800.1 68.7 %reduce-scatter.55.cloned.1.call-done = bf16[256,128]{0,1:T(8,128)(2,1)} async-done(((bf16[4096,128]{0,1:T(8,128)(2,1)}), bf16[256,128]{0,1:T(8,128)(2,1)}) %reduce-scatter.55.cloned.1.call-update) | async-done | bytes 65552 | tf_op jit(solution)/shard_map/reduce_scatter | solution.py:306
  1871.2 65.4 %reduce-scatter.77.cloned.1.call-done = bf16[64,128]{1,0:T(8,128)(2,1)} async-done(((bf16[1024,128]{1,0:T(8,128)(2,1)}), bf16[64,128]{1,0:T(8,128)(2,1)}) %reduce-scatter.77.cloned.1.call-update) | async-done | bytes 16400
  1938.2 68.2 %reduce-scatter.57.cloned.1.call-done = bf16[256,128]{0,1:T(8,128)(2,1)} async-done(((bf16[4096,128]{0,1:T(8,128)(2,1)}), bf16[256,128]{0,1:T(8,128)(2,1)}) %reduce-scatter.57.cloned.1.call-update) | async-done | bytes 65552 | tf_op jit(solution)/shard_map/reduce_scatter | solution.py:309
  2010.2 65.5 %all-reduce = (f32[1,128]{1,0:T(1,128)S(1)}, f32[1,128]{1,0:T(1,128)S(1)}, f32[1,128]{1,0:T(1,128)S(1)}, f32[1,128]{1,0:T(1,128)S(1)}, f32[1,128]{1,0:T(1,128)S(...) all-reduce(f32[1,128]{1,0:T(1,128)S(1)} %stack.190, ...), channel_id=1, replica_groups=mesh['row'=16,'col'=8] {'row'}, use_global_device_ids=true, to_apply=%region_77.78 | all-reduce | flops 3072 | bytes 24576 | tf_op jit(solution)/shard_map/psum | solution.py:344
  2082.5 60.3 %reduce-scatter.85.cloned.1.call-done = bf16[64,128]{1,0:T(8,128)(2,1)} async-done(((bf16[1024,128]{1,0:T(8,128)(2,1)}), bf16[64,128]{1,0:T(8,128)(2,1)}) %reduce-scatter.85.cloned.1.call-update) | async-done | bytes 16400
  2144.4 37.4 %reduce-scatter.59.cloned.1.call-done = bf16[256,128]{0,1:T(8,128)(2,1)} async-done(((bf16[256,1024]{0,1:T(8,128)(2,1)}), bf16[256,128]{0,1:T(8,128)(2,1)}) %reduce-scatter.59.cloned.1.call-update) | async-done | bytes 65552 | tf_op jit(solution)/shard_map/reduce_scatter | solution.py:46
  (660 shorter events, 261.8 us)
Async XLA Ops:
  7.2 78.5 %copy-start.45 = (bf16[256,128]{1,0:T(8,128)(2,1)S(1)}, bf16[256,128]{1,0:T(8,128)(2,1)}, u32[]{:S(2)}) copy-start(bf16[256,128]{1,0:T(8,128)(2,1)} %param.30) | copy-start | bytes 196612
  7.2 76.9 %copy-start.49 = (bf16[2,64,512]{2,1,0:T(8,128)(2,1)S(1)}, bf16[2,64,512]{2,1,0:T(8,128)(2,1)}, u32[]{:S(2)}) copy-start(bf16[2,64,512]{2,1,0:T(8,128)(2,1)} %param.35) | copy-start | bytes 393220
  7.2 77.7 %copy-start.50 = (bf16[2,256,128]{2,1,0:T(8,128)(2,1)S(1)}, bf16[2,256,128]{2,1,0:T(8,128)(2,1)}, u32[]{:S(2)}) copy-start(bf16[2,256,128]{2,1,0:T(8,128)(2,1)} %param.36) | copy-start | bytes 393220
  7.2 78.6 %copy-start.75 = (bf16[2,128]{1,0:T(2,128)(2,1)S(1)}, bf16[2,128]{1,0:T(2,128)(2,1)}, u32[]{:S(2)}) copy-start(bf16[2,128]{1,0:T(2,128)(2,1)} %param.39) | copy-start | bytes 1540
  7.2 78.6 %copy-start.61 = (bf16[2,512]{1,0:T(2,128)(2,1)S(1)}, bf16[2,512]{1,0:T(2,128)(2,1)}, u32[]{:S(2)}) copy-start(bf16[2,512]{1,0:T(2,128)(2,1)} %param.40) | copy-start | bytes 6148
  7.2 78.6 %copy-start.54 = (s32[4096]{0:T(1024)S(1)}, s32[4096]{0:T(1024)}, u32[]{:S(2)}) copy-start(s32[4096]{0:T(1024)} %param.46) | copy-start | bytes 49156
  7.3 78.7 %copy-start.52 = (bf16[2,64,128]{2,1,0:T(8,128)(2,1)S(1)}, bf16[2,64,128]{2,1,0:T(8,128)(2,1)}, u32[]{:S(2)}) copy-start(bf16[2,64,128]{2,1,0:T(8,128)(2,1)} %param.31) | copy-start | bytes 98308
  7.3 101.9 %copy-start.76 = (bf16[2,128]{1,0:T(2,128)(2,1)S(1)}, bf16[2,128]{1,0:T(2,128)(2,1)}, u32[]{:S(2)}) copy-start(bf16[2,128]{1,0:T(2,128)(2,1)} %param.37) | copy-start | bytes 1540
  7.3 101.9 %copy-start.53 = (bf16[2,64,128]{2,1,0:T(8,128)(2,1)S(1)}, bf16[2,64,128]{2,1,0:T(8,128)(2,1)}, u32[]{:S(2)}) copy-start(bf16[2,64,128]{2,1,0:T(8,128)(2,1)} %param.34) | copy-start | bytes 98308
  7.3 122.9 %all-gather.23.cloned.1.call-start = ((), (), s32[]{:S(2)}) async-start(), calls=%async_computation.24 | async-start | bytes 1114112 | tf_op jit(solution)/shard_map/all_gather | solution.py:206
  33.4 96.4 %copy-start.77 = (bf16[2,128]{1,0:T(2,128)(2,1)S(1)}, bf16[2,128]{1,0:T(2,128)(2,1)}, u32[]{:S(2)}) copy-start(bf16[2,128]{1,0:T(2,128)(2,1)} %param.43) | copy-start | bytes 1540
  33.4 96.4 %copy-start.78 = (bf16[2,128]{1,0:T(2,128)(2,1)S(1)}, bf16[2,128]{1,0:T(2,128)(2,1)}, u32[]{:S(2)}) copy-start(bf16[2,128]{1,0:T(2,128)(2,1)} %param.42) | copy-start | bytes 1540
  61.4 86.9 %all-gather.25.cloned.1.call-start = ((), (), s32[]{:S(2)}) async-start(), calls=%async_computation.25 | async-start | bytes 1114112 | tf_op jit(solution)/shard_map/all_gather | solution.py:205
  84.1 177.8 %all-gather.35.cloned.1.call-start = ((), (), s32[]{:S(2)}) async-start(), calls=%async_computation.46 | async-start | bytes 1114112 | tf_op jit(solution)/shard_map/all_gather | solution.py:193
  84.8 203.9 %all-gather.37.cloned.1.call-start = ((), (), s32[]{:S(2)}) async-start(), calls=%async_computation.47 | async-start | bytes 1114112 | tf_op jit(solution)/shard_map/all_gather | solution.py:194
  85.6 218.6 %all-gather.27.cloned.1.call-start = ((), (), s32[]{:S(2)}) async-start(), calls=%async_computation.26 | async-start | bytes 2359296 | tf_op jit(solution)/shard_map/all_gather | solution.py:31
  129.7 82.7 %copy-start.9 = (bf16[1,1024,128]{2,1,0:T(8,128)(2,1)}, bf16[1,1024,128]{2,1,0:T(8,128)(2,1)S(1)}, u32[]{:S(2)}) copy-start(bf16[1,1024,128]{2,1,0:T(8,128)(2,1)S(1)} %all-gather.3) | copy-start | bytes 786436
  129.8 174.4 %copy-start.56 = (f32[128]{0:T(128)}, f32[128]{0:T(128)S(1)}, u32[]{:S(2)}) copy-start(f32[128]{0:T(128)S(1)} %get-tuple-element.929) | copy-start | bytes 1540
  129.8 470.9 %copy-start.58 = (f32[128]{0:T(128)}, f32[128]{0:T(128)S(1)}, u32[]{:S(2)}) copy-start(f32[128]{0:T(128)S(1)} %get-tuple-element.928) | copy-start | bytes 1540
  183.0 82.9 %copy-start.40 = (f32[256,2,64]{0,2,1:T(8,128)}, f32[256,2,64]{0,2,1:T(8,128)S(1)}, u32[]{:S(2)}) copy-start(f32[256,2,64]{0,2,1:T(8,128)S(1)} %get-tuple-element.307) | copy-start | bytes 393220
  183.0 82.9 %copy-start.73 = (f32[2,256]{1,0:T(2,128)}, f32[2,256]{1,0:T(2,128)S(1)}, u32[]{:S(2)}) copy-start(f32[2,256]{1,0:T(2,128)S(1)} %get-tuple-element.1638) | copy-start | bytes 6148
  265.9 161.4 %all-gather.29.cloned.1.call-start = ((), (), s32[]{:S(2)}) async-start(), calls=%async_computation.27 | async-start | bytes 1114112 | tf_op jit(solution)/shard_map/all_gather | solution.py:206
  288.6 65.4 %copy-start.24 = (bf16[1,1024,128]{2,1,0:T(8,128)(2,1)}, bf16[1,1024,128]{2,1,0:T(8,128)(2,1)S(1)}, u32[]{:S(2)}) copy-start(bf16[1,1024,128]{2,1,0:T(8,128)(2,1)S(1)} %all-gather.6) | copy-start | bytes 786436
  288.7 221.1 %copy-start.62 = (f32[128]{0:T(128)}, f32[128]{0:T(128)S(1)}, u32[]{:S(2)}) copy-start(f32[128]{0:T(128)S(1)} %get-tuple-element.923) | copy-start | bytes 1540
  325.0 184.7 %copy-start.55 = (f32[256]{0:T(256)}, f32[256]{0:T(256)S(1)}, u32[]{:S(2)}) copy-start(f32[256]{0:T(256)S(1)} %get-tuple-element.919) | copy-start | bytes 3076
  355.0 90.6 %all-gather.31.cloned.1.call-start = ((), (), s32[]{:S(2)}) async-start(), calls=%async_computation.28 | async-start | bytes 1114112 | tf_op jit(solution)/shard_map/all_gather | solution.py:205
  380.4 178.1 %all-gather.39.cloned.1.call-start = ((), (), s32[]{:S(2)}) async-start(), calls=%async_computation.48 | async-start | bytes 1114112 | tf_op jit(solution)/shard_map/all_gather | solution.py:193
  381.1 181.5 %all-gather.41.cloned.1.call-start = ((), (), s32[]{:S(2)}) async-start(), calls=%async_computation.49 | async-start | bytes 1114112 | tf_op jit(solution)/shard_map/all_gather | solution.py:194
  381.9 218.8 %all-gather.33.cloned.1.call-start = ((), (), s32[]{:S(2)}) async-start(), calls=%async_computation.29 | async-start | bytes 2359296 | tf_op jit(solution)/shard_map/all_gather | solution.py:31
  480.3 82.1 %copy-start.44 = (s32[8,512]{1,0:T(8,128)}, s32[8,512]{1,0:T(8,128)S(1)}, u32[]{:S(2)}) copy-start(s32[8,512]{1,0:T(8,128)S(1)} %get-tuple-element.1596) | copy-start | bytes 49156
  562.5 120.2 %reduce-scatter.41.cloned.1.call-start = ((), (), s32[]{:S(2)}) async-start(), calls=%async_computation.30 | async-start | bytes 2359296 | tf_op jit(solution)/shard_map/reduce_scatter | solution.py:35
  562.7 76.0 %copy-start.6 = (bf16[1,4096,128]{2,1,0:T(8,128)(2,1)S(1)}, bf16[1,4096,128]{2,1,0:T(8,128)(2,1)}, u32[]{:S(2)}) copy-start(bf16[1,4096,128]{2,1,0:T(8,128)(2,1)} %all-gather.41.cloned.1.call-done) | copy-start | bytes 3145732
  640.8 82.9 %copy-start.59 = (f32[128]{0:T(128)S(1)}, f32[128]{0:T(128)}, u32[]{:S(2)}) copy-start(f32[128]{0:T(128)} %copy-done.58) | copy-start | bytes 1540
  640.8 82.9 %reduce-scatter.43.cloned.1.call-start = ((), (), s32[]{:S(2)}) async-start(), calls=%async_computation.31 | async-start | bytes 589824 | tf_op jit(solution)/shard_map/reduce_scatter | solution.py:35
  687.2 94.0 %reduce-scatter.73.cloned.1.call-start = ((), (), s32[]{:S(2)}) async-start(), calls=%async_computation.50 | async-start | bytes 589824
  744.8 160.8 %reduce-scatter.45.cloned.1.call-start = ((), (), s32[]{:S(2)}) async-start(), calls=%async_computation.32 | async-start | bytes 1114112 | tf_op jit(solution)/shard_map/reduce_scatter | solution.py:306
  839.5 136.3 %reduce-scatter.47.cloned.1.call-start = ((), (), s32[]{:S(2)}) async-start(), calls=%async_computation.33 | async-start | bytes 1114112 | tf_op jit(solution)/shard_map/reduce_scatter | solution.py:309
  841.5 172.9 %reduce-scatter.49.cloned.1.call-start = ((), (), s32[]{:S(2)}) async-start(), calls=%async_computation.34 | async-start | bytes 589824 | tf_op jit(solution)/shard_map/reduce_scatter | solution.py:46
  906.9 127.6 %copy-start.5 = (bf16[1,4096,128]{2,1,0:T(8,128)(2,1)S(1)}, bf16[1,4096,128]{2,1,0:T(8,128)(2,1)}, u32[]{:S(2)}) copy-start(bf16[1,4096,128]{2,1,0:T(8,128)(2,1)} %all-gather.37.cloned.1.call-done) | copy-start | bytes 3145732
  977.9 100.3 %reduce-scatter.51.cloned.1.call-start = ((), (), s32[]{:S(2)}) async-start(), calls=%async_computation.35 | async-start | bytes 2359296 | tf_op jit(solution)/shard_map/reduce_scatter | solution.py:35
  1036.7 80.8 %copy-start.57 = (f32[128]{0:T(128)S(1)}, f32[128]{0:T(128)}, u32[]{:S(2)}) copy-start(f32[128]{0:T(128)} %copy-done.56) | copy-start | bytes 1540
  1036.7 80.8 %reduce-scatter.53.cloned.1.call-start = ((), (), s32[]{:S(2)}) async-start(), calls=%async_computation.36 | async-start | bytes 589824 | tf_op jit(solution)/shard_map/reduce_scatter | solution.py:35
  1078.1 60.0 %copy-start.10 = (bf16[1,1024,128]{2,1,0:T(8,128)(2,1)S(1)}, bf16[1,1024,128]{2,1,0:T(8,128)(2,1)}, u32[]{:S(2)}) copy-start(bf16[1,1024,128]{2,1,0:T(8,128)(2,1)} %copy-done.9) | copy-start | bytes 786436
  1081.0 94.9 %reduce-scatter.75.cloned.1.call-start = ((), (), s32[]{:S(2)}) async-start(), calls=%async_computation.51 | async-start | bytes 589824
  1139.5 105.3 %reduce-scatter.79.cloned.1.call-start = ((), (), s32[]{:S(2)}) async-start(), calls=%async_computation.53 | async-start | bytes 278528
  1140.6 173.1 %reduce-scatter.83.cloned.1.call-start = ((), (), s32[]{:S(2)}) async-start(), calls=%async_computation.55 | async-start | bytes 278528
  1141.7 240.3 %reduce-scatter.87.cloned.1.call-start = ((), (), s32[]{:S(2)}) async-start(), calls=%async_computation.57 | async-start | bytes 278528
  1142.8 309.5 %reduce-scatter.71.cloned.1.call-start = ((), (), s32[]{:S(2)}) async-start(), calls=%async_computation.45 | async-start | bytes 1114112 | tf_op jit(solution)/shard_map/reduce_scatter | solution.py:340
  1146.3 375.7 %reduce-scatter.69.cloned.1.call-start = ((), (), s32[]{:S(2)}) async-start(), calls=%async_computation.44 | async-start | bytes 1114112 | tf_op jit(solution)/shard_map/reduce_scatter | solution.py:340
  1148.2 442.2 %reduce-scatter.63.cloned.1.call-start = ((), (), s32[]{:S(2)}) async-start(), calls=%async_computation.41 | async-start | bytes 278528 | tf_op jit(solution)/shard_map/reduce_scatter | solution.py:334
  1150.4 508.2 %reduce-scatter.61.cloned.1.call-start = ((), (), s32[]{:S(2)}) async-start(), calls=%async_computation.40 | async-start | bytes 278528 | tf_op jit(solution)/shard_map/reduce_scatter | solution.py:334
  1151.5 577.2 %reduce-scatter.67.cloned.1.call-start = ((), (), s32[]{:S(2)}) async-start(), calls=%async_computation.43 | async-start | bytes 1114112 | tf_op jit(solution)/shard_map/reduce_scatter | solution.py:337
  1153.0 645.5 %reduce-scatter.65.cloned.1.call-start = ((), (), s32[]{:S(2)}) async-start(), calls=%async_computation.42 | async-start | bytes 1114112 | tf_op jit(solution)/shard_map/reduce_scatter | solution.py:337
  1154.5 714.3 %reduce-scatter.55.cloned.1.call-start = ((), (), s32[]{:S(2)}) async-start(), calls=%async_computation.37 | async-start | bytes 1114112 | tf_op jit(solution)/shard_map/reduce_scatter | solution.py:306
  1226.8 709.8 %reduce-scatter.77.cloned.1.call-start = ((), (), s32[]{:S(2)}) async-start(), calls=%async_computation.52 | async-start | bytes 278528
  1228.0 778.3 %reduce-scatter.57.cloned.1.call-start = ((), (), s32[]{:S(2)}) async-start(), calls=%async_computation.38 | async-start | bytes 1114112 | tf_op jit(solution)/shard_map/reduce_scatter | solution.py:309
  1230.1 640.7 %copy-start.19 = (bf16[1,1024,128]{2,1,0:T(8,128)(2,1)S(1)}, bf16[1,1024,128]{2,1,0:T(8,128)(2,1)}, u32[]{:S(2)}) copy-start(bf16[1,1024,128]{2,1,0:T(8,128)(2,1)} %copy-done.18) | copy-start | bytes 786436
  1230.1 850.8 %reduce-scatter.81.cloned.1.call-start = ((), (), s32[]{:S(2)}) async-start(), calls=%async_computation.54 | async-start | bytes 278528
  1869.9 138.7 %copy-start.12 = (bf16[1,1024,128]{2,1,0:T(8,128)(2,1)S(1)}, bf16[1,1024,128]{2,1,0:T(8,128)(2,1)}, u32[]{:S(2)}) copy-start(bf16[1,1024,128]{2,1,0:T(8,128)(2,1)} %copy-done.11) | copy-start | bytes 786436
  1869.9 138.7 %copy-start.47 = (bf16[256,128]{0,1:T(8,128)(2,1)S(1)}, bf16[256,128]{0,1:T(8,128)(2,1)}, u32[]{:S(2)}) copy-start(bf16[256,128]{0,1:T(8,128)(2,1)} %reduce-scatter.55.cloned.1.call-done) | copy-start | bytes 196612
  1870.7 272.1 %reduce-scatter.85.cloned.1.call-start = ((), (), s32[]{:S(2)}) async-start(), calls=%async_computation.56 | async-start | bytes 278528
  1937.4 71.4 %copy-start.23 = (bf16[1,1024,128]{2,1,0:T(8,128)(2,1)S(1)}, bf16[1,1024,128]{2,1,0:T(8,128)(2,1)}, u32[]{:S(2)}) copy-start(bf16[1,1024,128]{2,1,0:T(8,128)(2,1)} %copy-done.22) | copy-start | bytes 786436
  2008.5 173.3 %reduce-scatter.59.cloned.1.call-start = ((), (), s32[]{:S(2)}) async-start(), calls=%async_computation.39 | async-start | bytes 589824 | tf_op jit(solution)/shard_map/reduce_scatter | solution.py:46
  2008.9 172.9 %copy-start.26 = (f32[256,128]{0,1:T(8,128)S(1)}, f32[256,128]{0,1:T(8,128)}, u32[]{:S(2)}) copy-start(f32[256,128]{0,1:T(8,128)} %copy-done.25) | copy-start | bytes 393220
  (55 other events, 763.4 us)
Sparse Core Ops, SparseCore 0:
  61.5 39.9 all-gather.22
  104.5 43.6 all-gather.24
  151.3 43.6 all-gather.34
  197.8 43.6 all-gather.36
  266.1 38.0 all-gather.26
  355.1 43.4 all-gather.28
  401.6 43.8 all-gather.30
  448.6 43.6 all-gather.38
  495.3 43.6 all-gather.40
  562.6 38.0 all-gather.32
  640.9 41.6 reduce-scatter.40
  687.3 36.3 reduce-scatter.42
  745.0 36.1 reduce-scatter.72
  839.6 66.0 reduce-scatter.44
  909.8 65.9 reduce-scatter.46
  978.0 36.3 reduce-scatter.48
  1036.8 41.2 reduce-scatter.50
  1081.1 36.2 reduce-scatter.52
  1139.6 36.2 reduce-scatter.74
  1180.4 64.3 reduce-scatter.78
  1249.5 64.1 reduce-scatter.82
  1317.8 64.1 reduce-scatter.86
  1386.3 65.9 reduce-scatter.70
  1455.9 66.0 reduce-scatter.68
  1526.1 64.2 reduce-scatter.62
  1594.3 64.1 reduce-scatter.60
  1662.7 66.0 reduce-scatter.66
  1732.5 65.9 reduce-scatter.64
  1802.7 65.9 reduce-scatter.54
  1872.3 64.2 reduce-scatter.76
  1940.3 65.9 reduce-scatter.56
  2010.5 64.1 reduce-scatter.80
  2078.6 64.1 reduce-scatter.84
  2145.3 36.4 reduce-scatter.58
where the time goes:
time: 2200 us; the launch traced here: 2190 us
  waiting for transfers between devices  1320 us (60%)
  blocking collectives  561 us (26%)
  matrix products  178 us (8%)
  local copies, waits for them, and re-layouts  72.3 us (3%)
  other arithmetic  37.5 us (2%)
    unnamed x42, waiting for transfers between devices  334 us
    all_gather x6, blocking collectives, spread(): return lax.all_gather(local_part, 'col', axis=1, tiled=True)  171 us
    reduce_scatter x4, waiting for transfers between devices, pass_single(): lax.psum_scatter(times_back(grad_low, full_w).astype(jnp.bfloat16), 'col'...  156 us
    reduce_scatter x2, waiting for transfers between devices, body(): lax.psum_scatter(down_w_g.astype(jnp.bfloat16), 'row', scatter_dimension=...  139 us
    reduce_scatter x2, waiting for transfers between devices, body(): lax.psum_scatter(up_w_g.astype(jnp.bfloat16), 'row', scatter_dimension=0,...  139 us
    reduce_scatter x2, waiting for transfers between devices, body(): lax.psum_scatter(value_all_g.astype(jnp.bfloat16), 'row', scatter_dimensi...  137 us
    reduce_scatter x2, waiting for transfers between devices, body(): lax.psum_scatter(proj_w_g.astype(jnp.bfloat16), 'row', scatter_dimension=...  135 us
    reduce_scatter x2, waiting for transfers between devices, body(): lax.psum_scatter(key_all_g.astype(jnp.bfloat16), 'row', scatter_dimension...  132 us
  transfers between devices with their start and end apart: 34, of which 27 were waited for; matrix products, arithmetic and copies ran while one was open for 9% of the time, Pallas kernels for 0%

commit v1 on v0

v1 whole, which is shorter than its diff:
```python
import functools
from types import SimpleNamespace

import jax
import jax.numpy as jnp
from jax import lax
from jax.experimental import pallas as pl
from jax.experimental.pallas import tpu as pltpu
from jax.sharding import PartitionSpec as P

MESH = pl.DeviceIdType.MESH
LAYERS = 2
HEAD_DIM = 64
LANES = 128
F32 = jnp.float32
BF16 = jnp.bfloat16
PAIRS = ((0, 0), (1, 1), (1, 2), (2, 1), (2, 2), (2, 3), (3, 2), (3, 3))
KEYS_OF = {i: [(n, j) for n, (a, j) in enumerate(PAIRS) if a == i] for i in range(4)}
QUERIES_OF = {j: [(n, i) for n, (i, b) in enumerate(PAIRS) if b == j] for j in range(4)}

PROJ_B, DOWN_B, GAIN1, SHIFT1, GAIN2, SHIFT2 = range(6)
VEC_ROWS = 8


def dot(a, b):
    return jnp.dot(a, b, preferred_element_type=F32)


def dot_nt(a, b):
    return lax.dot_general(a, b, (((1,), (1,)), ((), ())), preferred_element_type=F32)


def dot_tn(a, b):
    return lax.dot_general(a, b, (((0,), (0,)), ((), ())), preferred_element_type=F32)


class Sizes:
    def __init__(self, nr, nc, tok, d, ff):
        self.nr, self.nc, self.tok, self.d, self.ff = nr, nc, tok, d, ff
        self.t = tok // nc
        self.dc, self.fc = d // nc, ff // nc
        self.dr, self.fr = d // nr, ff // nr
        self.hr = nr // nc
        self.qc = tok // 4


def scratch_of(s):
    L = LAYERS
    v = {}
    v["xf"] = ((L, s.tok, s.d), BF16)
    v["x1"] = ((L, s.tok, s.d), BF16)
    v["dff"] = ((L, s.tok, s.d), BF16)
    v["drf"] = ((L, s.tok, s.d), BF16)
    v["part"] = ((s.tok, s.d), BF16)
    v["got"] = ((s.nc, s.t, s.d), BF16)
    v["got_in"] = ((s.nc, s.tok, s.dc), BF16)
    v["act_out"] = ((s.t, s.d), BF16)
    v["act_in"] = ((s.tok, s.dc), BF16)
    v["cot"] = ((s.t, s.d), BF16)
    v["pv"] = ((L * VEC_ROWS, s.d), BF16)
    v["kv"] = ((L, s.nr, s.tok, 2 * s.dc), BF16)
    v["dkv"] = ((s.nr, s.tok, 2 * s.dc), BF16)
    v["dkv_in"] = ((L, s.nr, s.tok, 2 * s.dc), BF16)
    v["probs"] = ((L, len(PAIRS), 2 * s.qc, s.nr * s.qc), BF16)
    v["q2"] = ((L, 4, 2 * s.qc, s.dc), BF16)
    v["do2"] = ((4, 2 * s.qc, s.dc), BF16)
    v["delta"] = ((4, 2 * s.qc, 1), F32)
    v["dq2"] = ((4, 2 * s.qc, s.dc), F32)
    v["att"] = ((L, s.tok, s.dc), F32)
    v["gate"] = ((L, s.tok, s.fc), BF16)
    v["slope"] = ((L, s.tok, s.fc), F32)
    v["de"] = ((s.tok, s.fc), BF16)
    v["n1"] = ((L, s.t, s.d), F32)
    v["n2"] = ((L, s.t, s.d), F32)
    v["r1"] = ((L, s.t, 1), F32)
    v["r2"] = ((L, s.t, 1), F32)
    v["carry"] = ((s.t, s.d), F32)
    v["dqkv"] = ((s.tok, 3 * s.dc), BF16)
    v["wqkv"] = ((L, s.d, 3 * s.dc), BF16)
    v["wproj"] = ((L, s.dc, s.d), BF16)
    v["wup"] = ((L, s.d, s.fc), BF16)
    v["wdown"] = ((L, s.fc, s.d), BF16)
    v["gqkv"] = ((s.d, 3 * s.dc), BF16)
    v["gproj"] = ((s.dc, s.d), BF16)
    v["gup"] = ((s.d, s.fc), BF16)
    v["gdown"] = ((s.fc, s.d), BF16)
    v["gqkv_in"] = ((L, s.nr, s.dr, 3 * s.dc), BF16)
    v["gproj_in"] = ((L, s.nr, s.dr, s.dc), BF16)
    v["gup_in"] = ((L, s.nr, s.dr, s.fc), BF16)
    v["gdown_in"] = ((L, s.nr, s.fr, s.dc), BF16)
    v["vec"] = ((L * VEC_ROWS, s.d), F32)
    v["vec_in"] = ((s.nc, L * VEC_ROWS, s.dc), F32)
    v["own"] = ((L * 2 * VEC_ROWS, s.dc), F32)
    v["own_in"] = ((s.nr, L * 2 * VEC_ROWS, s.dc), F32)
    return v


INPUTS = ("x", "cotan", "wq", "wp", "wu", "wd", "pvec", "qkvb", "upb", "segq", "segk")
OUTPUTS = ("o_act", "o_in", "o_qkv", "o_proj", "o_up", "o_down", "o_vec")
PHASES = (
    ["x", "cotan", "pvec", "act", "gin", "vec", "own"]
    + [f"{n}{l}" for l in range(LAYERS) for n in
       ("wq", "wp", "wu", "wd", "kv", "pr", "n1", "fr", "h", "df", "dn", "dr", "dkv", "dx", "gq", "gp", "gu", "gd")]
)
PHASE = {name: index for index, name in enumerate(PHASES)}


def kernel(s, *refs):
    names = INPUTS + OUTPUTS + tuple(scratch_of(s)) + ("send", "recv")
    m = SimpleNamespace(**dict(zip(names, refs)))
    L = LAYERS
    r, c = lax.axis_index("row"), lax.axis_index("col")
    home = lax.div(r, s.hr)
    part_of_home = lax.rem(r, s.hr)
    at_home = home == c

    def remote(src, dst, phase, row, col):
        return pltpu.make_async_remote_copy(
            src_ref=src, dst_ref=dst, send_sem=m.send.at[PHASE[phase]], recv_sem=m.recv.at[PHASE[phase]],
            device_id=(row, col), device_id_type=MESH)

    def wait(sems, phase, ref):
        pltpu.make_async_copy(ref, ref, sems.at[PHASE[phase]]).wait()

    def each_col(fn):
        def step(k, carry):
            fn(lax.rem(c + k, s.nc))
            return carry
        lax.fori_loop(1, s.nc, step, 0)

    def each_row(fn):
        def step(k, carry):
            fn(lax.rem(r + k, s.nr))
            return carry
        lax.fori_loop(1, s.nr, step, 0)

    def each_row_of_home(fn):
        def step(k, carry):
            row = lax.rem(r + k, s.nr)

            @pl.when(jnp.logical_or(k > 0, jnp.logical_not(at_home)))
            def _():
                fn(row)
            return carry
        lax.fori_loop(0, s.nr, step, 0)

    def each_owner(fn):
        def step(k, carry):
            rr, cc = lax.div(k, s.nc), lax.rem(k, s.nc)
            row = c * s.hr + rr

            @pl.when(jnp.logical_or(row != r, cc != c))
            def _():
                fn(rr, row, cc)
            return carry
        lax.fori_loop(0, s.nr, step, 0)

    def wait_home(sems, phase, ref):
        @pl.when(at_home)
        def _():
            wait(sems, phase, ref.at[pl.ds(0, s.nr - 1)])

        @pl.when(jnp.logical_not(at_home))
        def _():
            wait(sems, phase, ref)

    def rows(i, n):
        return pl.ds(pl.multiple_of(i * n, n), n)

    barrier = pltpu.get_barrier_semaphore()

    def greet(row, col):
        pl.semaphore_signal(barrier, inc=1, device_id=(row, col), device_id_type=MESH)

    each_col(lambda cc: greet(r, cc))
    each_row(lambda rr: greet(rr, c))
    each_row_of_home(lambda rr: greet(rr, home))
    each_owner(lambda rr, row, cc: greet(row, cc))

    m.xf[0, :, rows(c, s.dc)] = m.x[...]
    m.cot[:, rows(c, s.dc)] = m.cotan[rows(c, s.t), :]
    m.pv[:, rows(c, s.dc)] = m.pvec[...]
    for l in range(L):
        m.wqkv[l, rows(r, s.dr), :] = m.wq[l]
        m.wup[l, rows(r, s.dr), :] = m.wu[l]

        @pl.when(at_home)
        def _():
            m.wproj[l, rows(part_of_home, s.dr), rows(c, s.dc)] = m.wp[l]
            m.wdown[l, rows(part_of_home, s.fr), rows(c, s.dc)] = m.wd[l]
    m.vec[...] = jnp.zeros(m.vec.shape, F32)
    m.own[...] = jnp.zeros(m.own.shape, F32)

    pl.semaphore_wait(barrier, s.nc - 1 + s.nr - 1 + 2 * s.nr - 2 * at_home.astype(jnp.int32))

    each_row(lambda rr: remote(m.wq.at[0], m.wqkv.at[0, rows(r, s.dr)], "wq0", rr, c).start())
    each_col(lambda cc: remote(m.x, m.xf.at[0, :, rows(c, s.dc)], "x", r, cc).start())
    each_col(lambda cc: remote(m.pvec, m.pv.at[:, rows(c, s.dc)], "pvec", r, cc).start())
    each_col(lambda cc: remote(m.cotan.at[rows(cc, s.t)], m.cot.at[:, rows(c, s.dc)], "cotan", r, cc).start())
    for l in range(L):
        if l:
            each_row(lambda rr: remote(m.wq.at[l], m.wqkv.at[l, rows(r, s.dr)], f"wq{l}", rr, c).start())
        each_row_of_home(lambda rr: remote(
            m.wp.at[l], m.wproj.at[l, rows(part_of_home, s.dr), rows(c, s.dc)], f"wp{l}", rr, home).start())
        each_row(lambda rr: remote(m.wu.at[l], m.wup.at[l, rows(r, s.dr)], f"wu{l}", rr, c).start())
        each_row_of_home(lambda rr: remote(
            m.wd.at[l], m.wdown.at[l, rows(part_of_home, s.fr), rows(c, s.dc)], f"wd{l}", rr, home).start())

    few = s.nc - 1
    wait(m.recv, "x", m.xf.at[0, :, pl.ds(0, few * s.dc)])
    wait(m.recv, "pvec", m.pv.at[:, pl.ds(0, few * s.dc)])

    def vector(l, which):
        return m.pv[l * VEC_ROWS + which : l * VEC_ROWS + which + 1, :].astype(F32)

    def share(buf, value, phase):
        buf[rows(c, s.t), :] = value
        each_col(lambda cc: remote(buf.at[rows(c, s.t)], buf.at[rows(c, s.t)], phase, r, cc).start())

    def shared(buf, phase):
        for sems in (m.recv, m.send):
            wait(sems, phase, buf.at[pl.ds(0, few * s.t)])

    def scatter(value, phase):
        m.part[...] = value.astype(BF16)
        each_col(lambda cc: remote(m.part.at[rows(cc, s.t)], m.got.at[c], phase, r, cc).start())
        m.got[c] = m.part[rows(c, s.t), :]

    def scattered(phase):
        for sems in (m.recv, m.send):
            wait(sems, phase, m.got.at[pl.ds(0, few)])
        total = m.got[0].astype(F32)
        for k in range(1, s.nc):
            total = total + m.got[k].astype(F32)
        return total

    def norm(u, l, gain, shift, n_ref, r_ref):
        mean = jnp.sum(u, axis=1, keepdims=True) / s.d
        var = jnp.sum(u * u, axis=1, keepdims=True) / s.d - mean * mean
        inv = lax.rsqrt(var + 1e-12)
        n = (u - mean) * inv
        n_ref[l] = n
        r_ref[l] = inv
        return n * vector(l, gain) + vector(l, shift)

    def norm_back(g, l, gain, shift, n_ref, r_ref):
        n = n_ref[l]
        w = g * vector(l, gain)
        first = jnp.sum(w, axis=1, keepdims=True) / s.d
        second = jnp.sum(w * n, axis=1, keepdims=True) / s.d
        at = l * VEC_ROWS
        m.vec[at + gain : at + gain + 1, :] = jnp.sum(g * n, axis=0, keepdims=True)
        m.vec[at + shift : at + shift + 1, :] = jnp.sum(g, axis=0, keepdims=True)
        return r_ref[l] * (w - first - n * second)

    low_lanes = lax.broadcasted_iota(jnp.int32, (s.qc, s.dc), 1) < HEAD_DIM

    def two_heads(block):
        block = block.astype(F32)
        return jnp.concatenate([jnp.where(low_lanes, block, 0.0), jnp.where(low_lanes, 0.0, block)], axis=0)

    def one_block(pair):
        return jnp.where(low_lanes, pair[: s.qc], pair[s.qc :])

    def keys(l, j, value):
        lanes = pl.ds(s.dc if value else 0, s.dc)
        return m.kv[l, :, pl.ds(j * s.qc, s.qc), lanes].reshape(s.nr * s.qc, s.dc)

    hidden = m.xf[0, rows(c, s.t), :].astype(F32)
    for l in range(L):
        wait(m.recv, f"wq{l}", m.wqkv.at[l, pl.ds(0, (s.nr - 1) * s.dr)])
        qkv = dot(m.xf[l], m.wqkv[l]) + m.qkvb[l : l + 1, :]
        m.kv[l, r] = qkv[:, s.dc :].astype(BF16)
        each_row(lambda rr: remote(m.kv.at[l, r], m.kv.at[l, r], f"kv{l}", rr, c).start())
        for i in range(4):
            block = qkv[i * s.qc : (i + 1) * s.qc, : s.dc].astype(BF16)
            m.q2[l, i] = (two_heads(block) * HEAD_DIM ** (-0.5)).astype(BF16)
        m.carry[...] = hidden
        wait(m.recv, f"kv{l}", m.kv.at[l, pl.ds(0, s.nr - 1)])
        wait(m.send, f"kv{l}", m.kv.at[l, pl.ds(0, s.nr - 1)])
        for i in range(4):
            queries = m.q2[l, i]
            ids = m.segq[i]
            scores = []
            for _, j in KEYS_OF[i]:
                raw = dot_nt(queries, keys(l, j, False))
                scores.append(jnp.where(ids == m.segk[j : j + 1, :], raw, -1e9))
            top = functools.reduce(jnp.maximum, [jnp.max(x, axis=1, keepdims=True) for x in scores])
            raised = [jnp.exp(x - top) for x in scores]
            inverse = 1.0 / sum(jnp.sum(x, axis=1, keepdims=True) for x in raised)
            out = jnp.zeros((2 * s.qc, s.dc), F32)
            for (n, j), x in zip(KEYS_OF[i], raised):
                prob = (x * inverse).astype(BF16)
                m.probs[l, n] = prob
                out = out + dot(prob, keys(l, j, True))
            m.att[l, i * s.qc : (i + 1) * s.qc, :] = one_block(out)
        wait_home(m.recv, f"wp{l}", m.gproj_in.at[l])
        scatter(dot(m.att[l].astype(BF16), m.wproj[l]), f"pr{l}")
        u = scattered(f"pr{l}") + vector(l, PROJ_B) + m.carry[...]
        first_out = norm(u, l, GAIN1, SHIFT1, m.n1, m.r1)
        share(m.x1.at[l], first_out.astype(BF16), f"n1{l}")
        m.carry[...] = first_out
        wait(m.recv, f"wu{l}", m.wup.at[l, pl.ds(0, (s.nr - 1) * s.dr)])
        shared(m.x1.at[l], f"n1{l}")
        pre = dot(m.x1[l], m.wup[l]) + m.upb[l : l + 1, :]
        cdf = 0.5 * (1.0 + lax.erf(pre * 0.5**0.5))
        m.gate[l] = (pre * cdf).astype(BF16)
        m.slope[l] = cdf + pre * (jnp.exp(-0.5 * pre * pre) * 0.3989422804014327)
        wait_home(m.recv, f"wd{l}", m.gdown_in.at[l])
        scatter(dot(m.gate[l], m.wdown[l]), f"fr{l}")
        u = scattered(f"fr{l}") + vector(l, DOWN_B) + m.carry[...]
        hidden = norm(u, l, GAIN2, SHIFT2, m.n2, m.r2)
        if l + 1 < L:
            share(m.xf.at[l + 1], hidden.astype(BF16), f"h{l}")
            shared(m.xf.at[l + 1], f"h{l}")

    m.act_out[...] = hidden.astype(BF16)
    each_col(lambda cc: remote(m.act_out.at[:, rows(cc, s.dc)], m.act_in.at[rows(c, s.t)], "act", r, cc).start())
    m.act_in[rows(c, s.t), :] = m.act_out[:, rows(c, s.dc)]

    wait(m.recv, "cotan", m.cot.at[:, pl.ds(0, few * s.dc)])
    grad = m.cot[...].astype(F32)
    for l in reversed(range(L)):
        at = l * VEC_ROWS
        own = l * 2 * VEC_ROWS
        dz = norm_back(grad, l, GAIN2, SHIFT2, m.n2, m.r2)
        m.carry[...] = dz
        low = dz.astype(BF16)
        share(m.dff.at[l], low, f"df{l}")
        m.vec[at + DOWN_B : at + DOWN_B + 1, :] = jnp.sum(low.astype(F32), axis=0, keepdims=True)
        shared(m.dff.at[l], f"df{l}")
        de = (dot_nt(m.dff[l], m.wdown[l]) * m.slope[l]).astype(BF16)
        m.de[...] = de
        scatter(dot_nt(de, m.wup[l]), f"dn{l}")
        sums = jnp.sum(de.astype(F32), axis=0, keepdims=True)
        for k in range(s.fc // LANES):
            m.own[own + k : own + k + 1, :] = sums[:, k * LANES : (k + 1) * LANES]
        if l + 1 < L:
            wait_home(m.send, f"gd{l + 1}", m.gdown_in.at[l])
            wait(m.send, f"gu{l + 1}", m.gup_in.at[l, pl.ds(0, s.nr - 1)])
        m.gdown[...] = dot_tn(m.gate[l], m.dff[l]).astype(BF16)
        each_owner(lambda rr, row, cc: remote(
            m.gdown.at[rows(rr, s.fr), rows(cc, s.dc)], m.gdown_in.at[l, r], f"gd{l}", row, cc).start())

        @pl.when(at_home)
        def _():
            m.gdown_in[l, r] = m.gdown[rows(part_of_home, s.fr), rows(c, s.dc)]
        m.gup[...] = dot_tn(m.x1[l], m.de[...]).astype(BF16)
        each_row(lambda rr: remote(m.gup.at[rows(rr, s.dr)], m.gup_in.at[l, r], f"gu{l}", rr, c).start())
        m.gup_in[l, r] = m.gup[rows(r, s.dr), :]
        grad = scattered(f"dn{l}") + m.carry[...]
        du = norm_back(grad, l, GAIN1, SHIFT1, m.n1, m.r1)
        m.carry[...] = du
        low = du.astype(BF16)
        share(m.drf.at[l], low, f"dr{l}")
        m.vec[at + PROJ_B : at + PROJ_B + 1, :] = jnp.sum(low.astype(F32), axis=0, keepdims=True)
        shared(m.drf.at[l], f"dr{l}")
        dout = dot_nt(m.drf[l], m.wproj[l]).astype(BF16)
        for i in range(4):
            block = two_heads(dout[i * s.qc : (i + 1) * s.qc, :])
            kept = m.att[l, i * s.qc : (i + 1) * s.qc, :]
            m.do2[i] = block.astype(BF16)
            m.delta[i] = jnp.sum(block * jnp.concatenate([kept, kept], axis=0), axis=1, keepdims=True)
            m.dq2[i] = jnp.zeros((2 * s.qc, s.dc), F32)
        if l + 1 < L:
            wait(m.send, f"dkv{l + 1}", m.dkv.at[pl.ds(0, s.nr - 1)])
        for j in range(4):
            key_grad = jnp.zeros((s.nr * s.qc, s.dc), F32)
            value_grad = jnp.zeros((s.nr * s.qc, s.dc), F32)
            for n, i in QUERIES_OF[j]:
                prob = m.probs[l, n]
                prob_grad = dot_nt(m.do2[i], keys(l, j, True))
                score_grad = (prob.astype(F32) * (prob_grad - m.delta[i])).astype(BF16)
                m.dq2[i] += dot(score_grad, keys(l, j, False))
                key_grad = key_grad + dot_tn(score_grad, m.q2[l, i])
                value_grad = value_grad + dot_tn(prob, m.do2[i])
            shape = (s.nr, s.qc, s.dc)
            m.dkv[:, pl.ds(j * s.qc, s.qc), pl.ds(0, s.dc)] = key_grad.astype(BF16).reshape(shape)
            m.dkv[:, pl.ds(j * s.qc, s.qc), pl.ds(s.dc, s.dc)] = value_grad.astype(BF16).reshape(shape)
        each_row(lambda rr: remote(m.dkv.at[rr], m.dkv_in.at[l, r], f"dkv{l}", rr, c).start())
        m.dkv_in[l, r] = m.dkv[r]
        for i in range(4):
            m.dqkv[i * s.qc : (i + 1) * s.qc, : s.dc] = (one_block(m.dq2[i]) * HEAD_DIM ** (-0.5)).astype(BF16)
        if l + 1 < L:
            wait_home(m.send, f"gp{l + 1}", m.gproj_in.at[l])
            wait(m.send, f"gq{l + 1}", m.gqkv_in.at[l, pl.ds(0, s.nr - 1)])
        m.gproj[...] = dot_tn(m.att[l].astype(BF16), m.drf[l]).astype(BF16)
        each_owner(lambda rr, row, cc: remote(
            m.gproj.at[rows(rr, s.dr), rows(cc, s.dc)], m.gproj_in.at[l, r], f"gp{l}", row, cc).start())

        @pl.when(at_home)
        def _():
            m.gproj_in[l, r] = m.gproj[rows(part_of_home, s.dr), rows(c, s.dc)]
        wait(m.recv, f"dkv{l}", m.dkv_in.at[l, pl.ds(0, s.nr - 1)])
        total = m.dkv_in[l, 0].astype(F32)
        for k in range(1, s.nr):
            total = total + m.dkv_in[l, k].astype(F32)
        m.dqkv[:, s.dc :] = total.astype(BF16)
        back = dot_nt(m.dqkv[...], m.wqkv[l])
        if l:
            scatter(back, f"dx{l}")
        else:
            m.part[...] = back.astype(BF16)
            m.part[rows(c, s.t), :] = (m.part[rows(c, s.t), :].astype(F32) + m.carry[...]).astype(BF16)
            each_col(lambda cc: remote(m.part.at[:, rows(cc, s.dc)], m.got_in.at[c], "gin", r, cc).start())
            m.got_in[c] = m.part[:, rows(c, s.dc)]
        sums = jnp.sum(m.dqkv[...].astype(F32), axis=0, keepdims=True)
        m.own[own + 4 : own + 5, :] = sums[:, : s.dc]
        m.own[own + 5 : own + 6, :] = sums[:, 2 * s.dc :]
        m.gqkv[...] = dot_tn(m.xf[l], m.dqkv[...]).astype(BF16)
        each_row(lambda rr: remote(m.gqkv.at[rows(rr, s.dr)], m.gqkv_in.at[l, r], f"gq{l}", rr, c).start())
        m.gqkv_in[l, r] = m.gqkv[rows(r, s.dr), :]
        if l:
            grad = scattered(f"dx{l}") + m.carry[...]

    each_col(lambda cc: remote(m.vec.at[:, rows(cc, s.dc)], m.vec_in.at[c], "vec", r, cc).start())
    m.vec_in[c] = m.vec[:, rows(c, s.dc)]
    wait(m.recv, "vec", m.vec_in.at[pl.ds(0, few)])
    total = m.vec_in[0]
    for k in range(1, s.nc):
        total = total + m.vec_in[k]
    for l in range(L):
        own = l * 2 * VEC_ROWS + VEC_ROWS
        m.own[own : own + VEC_ROWS, :] = total[l * VEC_ROWS : (l + 1) * VEC_ROWS]
    m.own_in[r] = m.own[...]
    each_row(lambda rr: remote(m.own, m.own_in.at[r], "own", rr, c).start())

    def sum_up(buf, l, out):
        total = buf[l, 0].astype(F32)
        for k in range(1, s.nr):
            total = total + buf[l, k].astype(F32)
        out[l] = total

    for l in reversed(range(L)):
        wait_home(m.recv, f"gd{l}", m.gdown_in.at[l])
        sum_up(m.gdown_in, l, m.o_down)
        wait(m.recv, f"gu{l}", m.gup_in.at[l, pl.ds(0, s.nr - 1)])
        sum_up(m.gup_in, l, m.o_up)
        wait_home(m.recv, f"gp{l}", m.gproj_in.at[l])
        sum_up(m.gproj_in, l, m.o_proj)
        if l == 0:
            wait(m.recv, "gin", m.got_in.at[pl.ds(0, few)])
            total = m.got_in[0].astype(F32)
            for k in range(1, s.nc):
                total = total + m.got_in[k].astype(F32)
            m.o_in[...] = total
            wait(m.recv, "act", m.act_in.at[pl.ds(0, few * s.t)])
            m.o_act[...] = m.act_in[...]
        wait(m.recv, f"gq{l}", m.gqkv_in.at[l, pl.ds(0, s.nr - 1)])
        sum_up(m.gqkv_in, l, m.o_qkv)
    wait(m.recv, "own", m.own_in.at[pl.ds(0, s.nr - 1)])
    total = m.own_in[0]
    for k in range(1, s.nr):
        total = total + m.own_in[k]
    m.o_vec[...] = total

    wait(m.send, "x", m.xf.at[0, :, pl.ds(0, few * s.dc)])
    wait(m.send, "pvec", m.pv.at[:, pl.ds(0, few * s.dc)])
    wait(m.send, "cotan", m.cot.at[:, pl.ds(0, few * s.dc)])
    wait(m.send, "act", m.act_in.at[pl.ds(0, few * s.t)])
    wait(m.send, "gin", m.got_in.at[pl.ds(0, few)])
    wait(m.send, "vec", m.vec_in.at[pl.ds(0, few)])
    wait(m.send, "own", m.own_in.at[pl.ds(0, s.nr - 1)])
    for l in range(L):
        wait(m.send, f"wq{l}", m.wqkv.at[l, pl.ds(0, (s.nr - 1) * s.dr)])
        wait(m.send, f"wu{l}", m.wup.at[l, pl.ds(0, (s.nr - 1) * s.dr)])
        wait_home(m.send, f"wp{l}", m.gproj_in.at[l])
        wait_home(m.send, f"wd{l}", m.gdown_in.at[l])
    wait(m.send, "dkv0", m.dkv.at[pl.ds(0, s.nr - 1)])
    wait_home(m.send, "gd0", m.gdown_in.at[0])
    wait(m.send, "gu0", m.gup_in.at[0, pl.ds(0, s.nr - 1)])
    wait_home(m.send, "gp0", m.gproj_in.at[0])
    wait(m.send, "gq0", m.gqkv_in.at[0, pl.ds(0, s.nr - 1)])


def body(s, layer_input, query_weight, key_weight, value_weight, proj_weight, up_weight, down_weight, query_shift,
         value_shift, proj_shift, up_shift, down_shift, first_gain, first_shift, second_gain, second_shift, segment_ids,
         cotangent):
    L = LAYERS
    wq = jnp.concatenate([query_weight, key_weight, value_weight], axis=2)
    zero = jnp.zeros_like(proj_shift)
    pvec = jnp.stack([proj_shift, down_shift, first_gain, first_shift, second_gain, second_shift, zero, zero], axis=1)
    pvec = pvec.reshape(L * VEC_ROWS, s.dc)
    qkvb = jnp.concatenate([query_shift, jnp.zeros_like(query_shift), value_shift], axis=1).astype(F32)
    upb = up_shift.astype(F32)
    places = segment_ids[: s.tok].reshape(4, 1, s.qc)
    segq = jnp.tile(places, (1, 2, 1)).reshape(4, 2 * s.qc, 1)
    segk = jnp.tile(places, (1, s.nr, 1)).reshape(4, s.nr * s.qc)
    shapes = scratch_of(s)
    out_shape = (
        jax.ShapeDtypeStruct((s.tok, s.dc), BF16),
        jax.ShapeDtypeStruct((s.tok, s.dc), F32),
        jax.ShapeDtypeStruct((L, s.dr, 3 * s.dc), F32),
        jax.ShapeDtypeStruct((L, s.dr, s.dc), F32),
        jax.ShapeDtypeStruct((L, s.dr, s.fc), F32),
        jax.ShapeDtypeStruct((L, s.fr, s.dc), F32),
        jax.ShapeDtypeStruct((L * 2 * VEC_ROWS, s.dc), F32),
    )
    vmem = pl.BlockSpec(memory_space=pltpu.VMEM)
    o_act, o_in, o_qkv, o_proj, o_up, o_down, o_vec = pl.pallas_call(
        functools.partial(kernel, s),
        out_shape=out_shape,
        in_specs=[vmem] * len(INPUTS),
        out_specs=[vmem] * len(OUTPUTS),
        scratch_shapes=[pltpu.VMEM(shape, dtype) for shape, dtype in shapes.values()]
        + [pltpu.SemaphoreType.DMA((len(PHASES),))] * 2,
        compiler_params=pltpu.CompilerParams(
            collective_id=0, has_side_effects=True, vmem_limit_bytes=60 * 2**20),
        name="encoder",
    )(layer_input, cotangent, wq, proj_weight, up_weight, down_weight, pvec, qkvb, upb, segq, segk)
    own = o_vec.reshape(L, 2 * VEC_ROWS, s.dc)
    up_rows = s.fc // LANES
    vectors = own[:, VEC_ROWS:]
    return (
        o_act, o_in, o_qkv[:, :, : s.dc], o_qkv[:, :, s.dc : 2 * s.dc], o_qkv[:, :, 2 * s.dc :], o_proj, o_up, o_down,
        own[:, 4], own[:, 5], vectors[:, PROJ_B], own[:, :up_rows].reshape(L, s.fc), vectors[:, DOWN_B],
        vectors[:, GAIN1], vectors[:, SHIFT1], vectors[:, GAIN2], vectors[:, SHIFT2],
    )


def build(mesh, tok, d, ff):
    s = Sizes(mesh.shape["row"], mesh.shape["col"], tok, d, ff)
    return jax.shard_map(
        functools.partial(body, s),
        mesh=mesh,
        in_specs=(P("row", "col"),) + (P(None, "row", "col"),) * 6 + (P(None, "col"),) * 9 + (P(), P("row", "col")),
        out_specs=(P("row", "col"),) * 2 + (P(None, "row", "col"),) * 6 + (P(None, "col"),) * 9,
        check_vma=False,
    )


def solution(mesh):
    return build(mesh, 256, 1024, 4096)
```

time: 2200 us -> 489 us (0.22)
  waiting for transfers between devices: 1320 us -> 0 us
  blocking collectives: 561 us -> 0 us
  Pallas kernels: 0 us -> 471 us
  matrix products: 178 us -> 0 us
  local copies, waits for them, and re-layouts: 72.3 us -> 14.6 us
  other arithmetic: 37.5 us -> 1.83 us
    reduce_scatter x16 -> x0, waiting for transfers between devices: 911 us -> none  [the longest x4 156 us: pass_single(): lax.psum_scatter(times_back(grad_low, full_w).astype(jnp.bfloat16), 'col'...]
    pallas_call x0 -> x1, Pallas kernels: none -> 471 us  [body(): pl.pallas_call(functools.partial(kernel, s), out_shape=out_shape, in_spec...]
    all_gather x14 -> x0, blocking collectives: 353 us -> none  [the longest x6 171 us: spread(): return lax.all_gather(local_part, 'col', axis=1, tiled=True)]
    unnamed x42 -> x0, waiting for transfers between devices: 334 us -> none
    psum x9 -> x0, blocking collectives: 209 us -> none  [the longest x4 73.9 us: layer_norm(): lax.psum((jnp.sum(summed, axis=1), jnp.sum(summed * summed, axis=1)), 'col')]
    dot_general x148 -> x0, matrix products: 178 us -> none  [the longest x32 41.6 us: masked_scores(): jnp.einsum('qhd,khd->hqk', queries, key_part, preferred_element_type=jnp....]
    all_gather x10 -> x0, waiting for transfers between devices: 75.1 us -> none  [the longest x2 53.5 us: spread(): return lax.all_gather(local_part, 'col', axis=1, tiled=True)]
    unnamed x196 -> x43, local copies, waits for them, and re-layouts: 35 us -> 9.39 us
  transfers between devices with their start and end apart: 34 -> 0, of which waited for: 27 -> 0; matrix products, arithmetic and copies ran while one was open for 9% -> 0% of each run, Pallas kernels for 0% -> 0%
where the time goes in v1:
time: 489 us; the launch traced here: 488 us
  Pallas kernels  471 us (96%)
  local copies, waits for them, and re-layouts  14.6 us (3%)
    pallas_call x1, Pallas kernels, body(): pl.pallas_call(functools.partial(kernel, s), out_shape=out_shape, in_spec...  471 us

profile of v1, /device:TPU:2, one launch (start us, length us, event | category | flops | bytes accessed | tf_op | source)
XLA Modules:
  0.0 488.1 jit_solution(11890372869402061500)
XLA Ops:
  0.7 0.0 copy-start.12
  0.7 0.6 copy-done.12
  1.3 0.0 copy-start.13
  1.3 0.6 copy-done.13
  2.0 0.0 copy-start.14
  2.0 0.6 copy-done.14
  2.6 0.0 copy-start.15
  2.6 0.6 copy-done.15
  3.3 0.0 copy-start.16
  3.3 0.6 copy-done.16
  3.9 0.0 copy-start.17
  4.0 0.6 copy-done.17
  4.6 0.0 slice-start
  4.6 0.7 slice-done
  5.3 0.1 tile.16
  5.4 0.0 copy-start.10
  5.4 0.0 copy-start.11
  5.4 0.6 stack.31
  6.0 0.0 copy-start.9
  6.0 0.0 copy-done.10
  6.0 0.0 copy-done.11
  6.0 0.0 copy-start.7
  6.0 0.6 maximum_convert_fusion.refs_7_
  6.6 0.0 copy-done.9
  6.7 0.6 convert_element_type.7.refs_8_
  7.3 0.0 copy-start.6
  7.3 0.0 copy-start.5
  7.3 0.7 tile.20.refs_10_
  8.0 0.0 copy-done.7
  8.0 0.1 copy-done.6
  8.0 0.0 copy-done.5
  8.0 0.7 pad_maximum_fusion.refs_2_
  8.7 0.9 tile.21.refs_9_
  9.6 471.0 %encoder.1 = (bf16[256,128]{1,0:T(8,128)(2,1)}, f32[256,128]{1,0:T(8,128)}, f32[2,64,384]{2,1,0:T(8,128)}, f32[2,64,128]{2,1,0:T(8,128)}, f32[2,64,512]{2,1,0:T(...) custom-call(bf16[256,128]{1,0:T(8,128)(2,1)} %refs_0_.1, bf16[256,128]{1,0:T(8,128)(2,1)} %refs_1_.1, ...), custom_call_target="tpu_custom_call" | custom-call | tf_op jit(solution)/shard_map/encoder/pallas_call | solution.py:500
  480.6 0.0 copy-start.8
  480.6 0.8 slice_bitcast_fusion
  481.4 0.0 copy-done.8
  481.4 0.6 fusion.1
  482.0 0.6 copy.74
  482.6 0.0 copy-start.4
  482.6 0.0 copy-start.3
  482.6 1.6 fusion
  484.2 0.0 copy-start.2
  484.2 0.0 copy-done.4
  484.2 0.0 copy-start.1
  484.2 0.6 copy.80
  484.8 0.3 copy-done.2
  485.1 0.7 copy.81
  485.8 0.0 copy-done.3
  485.8 0.6 copy.82
  486.4 0.0 copy-done.1
  486.4 0.0 copy-start
  486.4 0.7 copy.83
  487.1 0.3 copy-done
  487.4 0.7 copy.84
  (11 shorter events, 0.0 us)
Async XLA Ops:
  0.7 0.7 copy-start.12
  1.3 0.7 copy-start.13
  2.0 0.7 copy-start.14
  2.6 0.7 copy-start.15
  3.3 0.7 copy-start.16
  3.9 0.7 copy-start.17
  4.6 0.7 slice-start
  5.4 0.7 copy-start.10
  5.4 0.7 copy-start.11
  6.0 0.7 copy-start.9
  6.0 1.9 copy-start.7
  7.3 0.8 copy-start.6
  7.3 0.8 copy-start.5
  480.6 0.8 copy-start.8
  482.6 1.6 copy-start.4
  482.6 3.2 copy-start.3
  484.2 0.9 copy-start.2
  484.2 2.2 copy-start.1
  486.4 1.0 copy-start

commit v2 on v1

v2 whole, which is shorter than its diff:
```python
import functools
from types import SimpleNamespace

import jax
import jax.numpy as jnp
from jax import lax
from jax.experimental import pallas as pl
from jax.experimental.pallas import tpu as pltpu
from jax.sharding import PartitionSpec as P

MESH = pl.DeviceIdType.MESH
LAYERS = 2
HEAD_DIM = 64
LANES = 128
F32 = jnp.float32
BF16 = jnp.bfloat16
PAIRS = ((0, 0), (1, 1), (1, 2), (2, 1), (2, 2), (2, 3), (3, 2), (3, 3))
KEYS_OF = {i: [(n, j) for n, (a, j) in enumerate(PAIRS) if a == i] for i in range(4)}
QUERIES_OF = {j: [(n, i) for n, (i, b) in enumerate(PAIRS) if b == j] for j in range(4)}

PROJ_B, DOWN_B, GAIN1, SHIFT1, GAIN2, SHIFT2 = range(6)
VEC_ROWS = 8


def dot(a, b):
    return jnp.dot(a, b, preferred_element_type=F32)


def dot_nt(a, b):
    return lax.dot_general(a, b, (((1,), (1,)), ((), ())), preferred_element_type=F32)


def dot_tn(a, b):
    return lax.dot_general(a, b, (((0,), (0,)), ((), ())), preferred_element_type=F32)


class Sizes:
    def __init__(self, nr, nc, tok, d, ff):
        self.nr, self.nc, self.tok, self.d, self.ff = nr, nc, tok, d, ff
        self.t = tok // nc
        self.dc, self.fc = d // nc, ff // nc
        self.dr, self.fr = d // nr, ff // nr
        self.nzx = nr // 2
        self.qc = tok // 4


def scratch_of(s):
    L = LAYERS
    v = {}
    v["xf"] = ((L, s.tok, s.d), BF16)
    v["x1"] = ((L, s.tok, s.d), BF16)
    v["dff"] = ((L, s.tok, s.d), BF16)
    v["drf"] = ((L, s.tok, s.d), BF16)
    v["part"] = ((s.tok, s.d), BF16)
    v["got"] = ((s.nc, s.t, s.d), BF16)
    v["got_in"] = ((s.nc, s.tok, s.dc), BF16)
    v["act_out"] = ((s.t, s.d), BF16)
    v["act_in"] = ((s.tok, s.dc), BF16)
    v["cot"] = ((s.t, s.d), BF16)
    v["pv"] = ((L * VEC_ROWS, s.d), F32)
    v["kv"] = ((L, s.nzx, 2, s.tok, 2 * s.dc), BF16)
    v["dkv"] = ((s.nzx, 2, s.tok, 2 * s.dc), BF16)
    v["dkv_c"] = ((L, s.nzx, s.tok, 2 * s.dc), BF16)
    v["dkv_in"] = ((L, s.nzx, s.tok, 2 * s.dc), BF16)
    v["probs"] = ((L, len(PAIRS), 2 * s.qc, s.nr * s.qc), BF16)
    v["q2"] = ((L, 4, 2 * s.qc, s.dc), BF16)
    v["do2"] = ((4, 2 * s.qc, s.dc), BF16)
    v["delta"] = ((4, 2 * s.qc, 1), F32)
    v["dq2"] = ((4, 2 * s.qc, s.dc), F32)
    v["att"] = ((L, s.tok, s.dc), F32)
    v["gate"] = ((L, s.tok, s.fc), BF16)
    v["slope"] = ((L, s.tok, s.fc), F32)
    v["de"] = ((s.tok, s.fc), BF16)
    v["n1"] = ((L, s.t, s.d), F32)
    v["n2"] = ((L, s.t, s.d), F32)
    v["r1"] = ((L, s.t, 1), F32)
    v["r2"] = ((L, s.t, 1), F32)
    v["carry"] = ((s.t, s.d), F32)
    v["dqkv"] = ((s.tok, 3 * s.dc), BF16)
    v["wqkv"] = ((L, s.nzx, 2, s.dr, 3 * s.dc), BF16)
    v["wup"] = ((L, s.nzx, 2, s.dr, s.fc), BF16)
    v["wproj"] = ((L, s.dc, s.d), BF16)
    v["wdown"] = ((L, s.fc, s.d), BF16)
    v["wp_own"] = ((L, s.dr, s.dc), BF16)
    v["wd_own"] = ((L, s.fr, s.dc), BF16)
    v["gqkv"] = ((s.nzx, 2, s.dr, 3 * s.dc), BF16)
    v["gup"] = ((s.nzx, 2, s.dr, s.fc), BF16)
    v["gproj"] = ((s.dc, s.d), BF16)
    v["gdown"] = ((s.fc, s.d), BF16)
    v["gqkv_c"] = ((L, s.nzx, s.dr, 3 * s.dc), BF16)
    v["gup_c"] = ((L, s.nzx, s.dr, s.fc), BF16)
    v["gproj_c"] = ((L, s.dr, s.d), BF16)
    v["gdown_c"] = ((L, s.fr, s.d), BF16)
    v["gqkv_in"] = ((L, s.nzx, s.dr, 3 * s.dc), BF16)
    v["gup_in"] = ((L, s.nzx, s.dr, s.fc), BF16)
    v["gproj_in"] = ((L, s.nzx, s.dr, s.dc), BF16)
    v["gdown_in"] = ((L, s.nzx, s.fr, s.dc), BF16)
    v["gproj_out"] = ((L, s.dr, s.dc), BF16)
    v["gdown_out"] = ((L, s.fr, s.dc), BF16)
    v["gproj_fin"] = ((L, s.dr, s.dc), BF16)
    v["gdown_fin"] = ((L, s.fr, s.dc), BF16)
    v["vec"] = ((L * VEC_ROWS, s.d), F32)
    v["vec_in"] = ((s.nc, L * VEC_ROWS, s.dc), F32)
    v["own"] = ((L * 2 * VEC_ROWS, s.dc), F32)
    v["own_in"] = ((s.nr, L * 2 * VEC_ROWS, s.dc), F32)
    return v


INPUTS = ("x", "cotan", "wq", "wk", "wv", "wp", "wu", "wd", "qb", "vb", "pb", "upb", "db", "g1", "s1", "g2", "s2", "segq",
          "segk")
OUTPUTS = ("o_act", "o_in", "o_q", "o_k", "o_v", "o_proj", "o_up", "o_down", "o_vec")
PHASES = (
    ["x", "cotan", "pvec", "act", "gin", "vec", "own", "wpt", "wdt"]
    + [f"{n}{l}" for l in range(LAYERS) for n in ("pr", "n1", "fr", "h", "df", "dn", "dr", "dx", "gpt", "gdt")]
    + [f"{n}{l}{e}" for l in range(LAYERS) for n in ("wq", "wp", "wu", "wd", "kv", "dkv", "gq", "gp", "gu", "gd")
       for e in ("", "c")]
)
PHASE = {name: index for index, name in enumerate(PHASES)}


def kernel(s, *refs):
    names = INPUTS + OUTPUTS + tuple(scratch_of(s)) + ("send", "recv")
    m = SimpleNamespace(**dict(zip(names, refs)))
    L = LAYERS
    r, c = lax.axis_index("row"), lax.axis_index("col")
    zx, k = lax.div(r, 2), lax.rem(r, 2)
    other = zx * 2 + 1 - k
    at_home = zx == c
    chips, few = s.nzx - 1, s.nc - 1

    def remote(src, dst, phase, row, col):
        return pltpu.make_async_remote_copy(
            src_ref=src, dst_ref=dst, send_sem=m.send.at[PHASE[phase]], recv_sem=m.recv.at[PHASE[phase]],
            device_id=(row, col), device_id_type=MESH)

    def wait(sems, phase, ref):
        pltpu.make_async_copy(ref, ref, sems.at[PHASE[phase]]).wait()

    def each_col(fn):
        def step(q, carry):
            fn(lax.rem(c + q, s.nc))
            return carry
        lax.fori_loop(1, s.nc, step, 0)

    def each_row(fn):
        def step(q, carry):
            fn(lax.rem(r + q, s.nr))
            return carry
        lax.fori_loop(1, s.nr, step, 0)

    def each_chip(fn):
        def step(q, carry):
            fn(lax.rem(zx + q, s.nzx))
            return carry
        lax.fori_loop(1, s.nzx, step, 0)

    def rows(i, n):
        return pl.ds(pl.multiple_of(i * n, n), n)

    barrier = pltpu.get_barrier_semaphore()

    def greet(row, col):
        pl.semaphore_signal(barrier, inc=1, device_id=(row, col), device_id_type=MESH)

    swap_row, swap_col = c * 2 + k, zx
    each_col(lambda cc: greet(r, cc))
    each_row(lambda rr: greet(rr, c))

    @pl.when(jnp.logical_not(at_home))
    def _():
        greet(swap_row, swap_col)

    def weight(name, l):
        if name in ("wq", "wu", "kv"):
            ref = {"wq": m.wqkv, "wu": m.wup, "kv": m.kv}[name]
            return (lambda i, kk: ref.at[l, i, kk]), (lambda kk: ref.at[l, :, kk]), ref.at[l, pl.ds(0, chips), 0]
        ref, n = {"wp": (m.wproj, s.dr), "wd": (m.wdown, s.fr)}[name]
        return ((lambda i, kk: ref.at[l, rows(kk, n), rows(i, s.dc)]), (lambda kk: ref.at[l, rows(kk, n)]),
                ref.at[l, pl.ds(0, n), pl.ds(0, chips * s.dc)])

    def gather(name, l):
        piece = weight(name, l)[0](zx, k)
        each_chip(lambda i: remote(piece, piece, f"{name}{l}", i * 2 + k, c).start())

    def pass_on(name, l):
        _, half, many = weight(name, l)
        wait(m.recv, f"{name}{l}", many)
        remote(half(k), half(k), f"{name}{l}c", other, c).start()

    def gathered(name, l):
        wait(m.recv, f"{name}{l}c", weight(name, l)[1](1 - k))

    def sent_gather(name, l):
        _, half, many = weight(name, l)
        wait(m.send, f"{name}{l}", many)
        wait(m.send, f"{name}{l}c", half(k))

    def partial_sum(name, l):
        if name in ("gq", "gu", "dkv"):
            full, mid, got = {"gq": (m.gqkv, m.gqkv_c, m.gqkv_in), "gu": (m.gup, m.gup_c, m.gup_in),
                              "dkv": (m.dkv, m.dkv_c, m.dkv_in)}[name]
            return (lambda kk: full.at[:, kk]), mid, (lambda i: mid.at[l, i]), got
        full, mid, got, n = {"gp": (m.gproj, m.gproj_c, m.gproj_in, s.dr),
                             "gd": (m.gdown, m.gdown_c, m.gdown_in, s.fr)}[name]
        return (lambda kk: full.at[rows(kk, n)]), mid, (lambda i: mid.at[l, :, rows(i, s.dc)]), got

    def reduce_start(name, l):
        half, mid, _, _ = partial_sum(name, l)
        remote(half(1 - k), mid.at[l], f"{name}{l}c", other, c).start()

    def reduce_mid(name, l):
        half, mid, piece, got = partial_sum(name, l)
        wait(m.recv, f"{name}{l}c", mid.at[l])
        mid[l] = (half(k)[...].astype(F32) + mid[l].astype(F32)).astype(BF16)
        each_chip(lambda i: remote(piece(i), got.at[l, zx], f"{name}{l}", i * 2 + k, c).start())
        got[l, zx] = piece(zx)[...]

    def reduce_end(name, l):
        got = partial_sum(name, l)[3]
        wait(m.recv, f"{name}{l}", got.at[l, pl.ds(0, chips)])
        total = got[l, 0].astype(F32)
        for i in range(1, s.nzx):
            total = total + got[l, i].astype(F32)
        return total

    def sent_half(name, l):
        half, mid, _, _ = partial_sum(name, l)
        wait(m.send, f"{name}{l}c", mid.at[l])

    def sent_pieces(name, l):
        got = partial_sum(name, l)[3]
        wait(m.send, f"{name}{l}", got.at[l, pl.ds(0, chips)])

    m.xf[0, :, rows(c, s.dc)] = m.x[...]
    m.cot[:, rows(c, s.dc)] = m.cotan[rows(c, s.t), :]
    m.pv[:, rows(c, s.dc)] = jnp.zeros((L * VEC_ROWS, s.dc), F32)
    for l in range(L):
        for which, ref in enumerate((m.pb, m.db, m.g1, m.s1, m.g2, m.s2)):
            m.pv[l * VEC_ROWS + which : l * VEC_ROWS + which + 1, rows(c, s.dc)] = ref[l : l + 1, :].astype(F32)
        for which, ref in enumerate((m.wq, m.wk, m.wv)):
            m.wqkv[l, zx, k, :, which * s.dc : (which + 1) * s.dc] = ref[l]
        m.wup[l, zx, k] = m.wu[l]

    pl.semaphore_wait(barrier, s.nc - 1 + s.nr - 1 + 1 - at_home.astype(jnp.int32))

    gather("wq", 0)
    each_col(lambda cc: remote(m.x, m.xf.at[0, :, rows(c, s.dc)], "x", r, cc).start())

    @pl.when(jnp.logical_not(at_home))
    def _():
        remote(m.wp, m.wp_own, "wpt", swap_row, swap_col).start()
        remote(m.wd, m.wd_own, "wdt", swap_row, swap_col).start()
    mine = m.pv.at[:, rows(c, s.dc)]
    each_col(lambda cc: remote(mine, mine, "pvec", r, cc).start())
    each_col(lambda cc: remote(m.cotan.at[rows(cc, s.t)], m.cot.at[:, rows(c, s.dc)], "cotan", r, cc).start())
    m.vec[...] = jnp.zeros(m.vec.shape, F32)
    m.own[...] = jnp.zeros(m.own.shape, F32)

    def vector(l, which):
        return m.pv[l * VEC_ROWS + which : l * VEC_ROWS + which + 1, :]

    def share(buf, value, phase):
        buf[rows(c, s.t), :] = value
        each_col(lambda cc: remote(buf.at[rows(c, s.t)], buf.at[rows(c, s.t)], phase, r, cc).start())

    def shared(buf, phase):
        for sems in (m.recv, m.send):
            wait(sems, phase, buf.at[pl.ds(0, few * s.t)])

    def scatter(value, phase):
        m.part[...] = value.astype(BF16)
        each_col(lambda cc: remote(m.part.at[rows(cc, s.t)], m.got.at[c], phase, r, cc).start())
        m.got[c] = m.part[rows(c, s.t), :]

    def scattered(phase):
        for sems in (m.recv, m.send):
            wait(sems, phase, m.got.at[pl.ds(0, few)])
        total = m.got[0].astype(F32)
        for i in range(1, s.nc):
            total = total + m.got[i].astype(F32)
        return total

    def norm(u, l, gain, shift, n_ref, r_ref):
        mean = jnp.sum(u, axis=1, keepdims=True) / s.d
        var = jnp.sum(u * u, axis=1, keepdims=True) / s.d - mean * mean
        inv = lax.rsqrt(var + 1e-12)
        n = (u - mean) * inv
        n_ref[l] = n
        r_ref[l] = inv
        return n * vector(l, gain) + vector(l, shift)

    def norm_back(g, l, gain, shift, n_ref, r_ref):
        n = n_ref[l]
        w = g * vector(l, gain)
        first = jnp.sum(w, axis=1, keepdims=True) / s.d
        second = jnp.sum(w * n, axis=1, keepdims=True) / s.d
        at = l * VEC_ROWS
        m.vec[at + gain : at + gain + 1, :] = jnp.sum(g * n, axis=0, keepdims=True)
        m.vec[at + shift : at + shift + 1, :] = jnp.sum(g, axis=0, keepdims=True)
        return r_ref[l] * (w - first - n * second)

    low_lanes = lax.broadcasted_iota(jnp.int32, (s.qc, s.dc), 1) < HEAD_DIM

    def two_heads(block):
        block = block.astype(F32)
        return jnp.concatenate([jnp.where(low_lanes, block, 0.0), jnp.where(low_lanes, 0.0, block)], axis=0)

    def one_block(pair):
        return jnp.where(low_lanes, pair[: s.qc], pair[s.qc :])

    def keys(l, j, value):
        lanes = pl.ds(s.dc if value else 0, s.dc)
        return m.kv[l, :, :, pl.ds(j * s.qc, s.qc), lanes].reshape(s.nr * s.qc, s.dc)

    def swapped(l):
        m.wproj[l, rows(k, s.dr), rows(zx, s.dc)] = m.wp_own[l]
        m.wdown[l, rows(k, s.fr), rows(zx, s.dc)] = m.wd_own[l]

    pass_on("wq", 0)
    wait(m.recv, "x", m.xf.at[0, :, pl.ds(0, few * s.dc)])
    wait(m.recv, "pvec", m.pv.at[:, pl.ds(0, few * s.dc)])

    @pl.when(at_home)
    def _():
        m.wp_own[...] = m.wp[...]
        m.wd_own[...] = m.wd[...]

    @pl.when(jnp.logical_not(at_home))
    def _():
        wait(m.recv, "wpt", m.wp_own)
        wait(m.recv, "wdt", m.wd_own)
    swapped(0)
    hidden = m.xf[0, rows(c, s.t), :].astype(F32)
    for l in range(L):
        gathered("wq", l)
        qkv = dot(m.xf[l], m.wqkv[l].reshape(s.d, 3 * s.dc))
        keep = (qkv[:, 2 * s.dc :] + m.vb[l : l + 1, :].astype(F32)).astype(BF16)
        m.kv[l, zx, k, :, : s.dc] = qkv[:, s.dc : 2 * s.dc].astype(BF16)
        m.kv[l, zx, k, :, s.dc :] = keep
        gather("kv", l)
        if l == 0:
            gather("wp", 0)
        for i in range(4):
            block = (qkv[i * s.qc : (i + 1) * s.qc, : s.dc] + m.qb[l : l + 1, :].astype(F32)).astype(BF16)
            m.q2[l, i] = (two_heads(block) * HEAD_DIM ** (-0.5)).astype(BF16)
        m.carry[...] = hidden
        pass_on("kv", l)
        if l == 0:
            gather("wu", 0)
            gather("wd", 0)
            pass_on("wp", 0)
        else:
            pass_on("wu", 1)
            pass_on("wd", 1)
        gathered("kv", l)
        for i in range(4):
            queries = m.q2[l, i]
            ids = m.segq[i]
            scores = []
            for _, j in KEYS_OF[i]:
                raw = dot_nt(queries, keys(l, j, False))
                scores.append(jnp.where(ids == m.segk[j : j + 1, :], raw, -1e9))
            top = functools.reduce(jnp.maximum, [jnp.max(x, axis=1, keepdims=True) for x in scores])
            raised = [jnp.exp(x - top) for x in scores]
            inverse = 1.0 / sum(jnp.sum(x, axis=1, keepdims=True) for x in raised)
            out = jnp.zeros((2 * s.qc, s.dc), F32)
            for (n, j), x in zip(KEYS_OF[i], raised):
                prob = (x * inverse).astype(BF16)
                m.probs[l, n] = prob
                out = out + dot(prob, keys(l, j, True))
            m.att[l, i * s.qc : (i + 1) * s.qc, :] = one_block(out)
        gathered("wp", l)
        scatter(dot(m.att[l].astype(BF16), m.wproj[l]), f"pr{l}")
        if l == 0:
            pass_on("wu", 0)
            pass_on("wd", 0)
            swapped(1)
        u = scattered(f"pr{l}") + vector(l, PROJ_B) + m.carry[...]
        first_out = norm(u, l, GAIN1, SHIFT1, m.n1, m.r1)
        share(m.x1.at[l], first_out.astype(BF16), f"n1{l}")
        m.carry[...] = first_out
        if l == 0:
            gather("wq", 1)
            gather("wp", 1)
        gathered("wu", l)
        shared(m.x1.at[l], f"n1{l}")
        pre = dot(m.x1[l], m.wup[l].reshape(s.d, s.fc)) + m.upb[l : l + 1, :].astype(F32)
        cdf = 0.5 * (1.0 + lax.erf(pre * 0.5**0.5))
        m.gate[l] = (pre * cdf).astype(BF16)
        m.slope[l] = cdf + pre * (jnp.exp(-0.5 * pre * pre) * 0.3989422804014327)
        gathered("wd", l)
        scatter(dot(m.gate[l], m.wdown[l]), f"fr{l}")
        if l == 0:
            pass_on("wq", 1)
            pass_on("wp", 1)
        u = scattered(f"fr{l}") + vector(l, DOWN_B) + m.carry[...]
        hidden = norm(u, l, GAIN2, SHIFT2, m.n2, m.r2)
        if l == 0:
            share(m.xf.at[1], hidden.astype(BF16), "h0")
            gather("wu", 1)
            gather("wd", 1)
            shared(m.xf.at[1], "h0")

    m.act_out[...] = hidden.astype(BF16)
    each_col(lambda cc: remote(m.act_out.at[:, rows(cc, s.dc)], m.act_in.at[rows(c, s.t)], "act", r, cc).start())
    m.act_in[rows(c, s.t), :] = m.act_out[:, rows(c, s.dc)]

    def swap_back(l, name, total):
        out, fin, phase = {"gp": (m.gproj_out, m.gproj_fin, f"gpt{l}"), "gd": (m.gdown_out, m.gdown_fin, f"gdt{l}")}[name]
        out[l] = total.astype(BF16)

        @pl.when(jnp.logical_not(at_home))
        def _():
            remote(out.at[l], fin.at[l], phase, swap_row, swap_col).start()

        @pl.when(at_home)
        def _():
            fin[l] = out[l]

    def swap_end(l, name, out):
        fin, phase = {"gp": (m.gproj_fin, f"gpt{l}"), "gd": (m.gdown_fin, f"gdt{l}")}[name]

        @pl.when(jnp.logical_not(at_home))
        def _():
            wait(m.recv, phase, fin.at[l])
        out[l] = fin[l].astype(F32)

    wait(m.recv, "cotan", m.cot.at[:, pl.ds(0, few * s.dc)])
    grad = m.cot[...].astype(F32)
    for l in reversed(range(L)):
        at = l * VEC_ROWS
        own = l * 2 * VEC_ROWS
        dz = norm_back(grad, l, GAIN2, SHIFT2, m.n2, m.r2)
        m.carry[...] = dz
        low = dz.astype(BF16)
        share(m.dff.at[l], low, f"df{l}")
        m.vec[at + DOWN_B : at + DOWN_B + 1, :] = jnp.sum(low.astype(F32), axis=0, keepdims=True)
        if l + 1 < L:
            reduce_mid("gq", l + 1)
            swap_back(l + 1, "gp", reduce_end("gp", l + 1))
        shared(m.dff.at[l], f"df{l}")
        de = (dot_nt(m.dff[l], m.wdown[l]) * m.slope[l]).astype(BF16)
        m.de[...] = de
        scatter(dot_nt(de, m.wup[l].reshape(s.d, s.fc)), f"dn{l}")
        sums = jnp.sum(de.astype(F32), axis=0, keepdims=True)
        for i in range(s.fc // LANES):
            m.own[own + i : own + i + 1, :] = sums[:, i * LANES : (i + 1) * LANES]
        if l + 1 < L:
            sent_half("gd", l + 1)
            sent_half("gu", l + 1)
        m.gdown[...] = dot_tn(m.gate[l], m.dff[l]).astype(BF16)
        reduce_start("gd", l)
        m.gup[...] = dot_tn(m.x1[l], m.de[...]).astype(BF16).reshape(m.gup.shape)
        reduce_start("gu", l)
        grad = scattered(f"dn{l}") + m.carry[...]
        du = norm_back(grad, l, GAIN1, SHIFT1, m.n1, m.r1)
        m.carry[...] = du
        low = du.astype(BF16)
        share(m.drf.at[l], low, f"dr{l}")
        m.vec[at + PROJ_B : at + PROJ_B + 1, :] = jnp.sum(low.astype(F32), axis=0, keepdims=True)
        reduce_mid("gd", l)
        reduce_mid("gu", l)
        shared(m.drf.at[l], f"dr{l}")
        if l == 0:
            each_col(lambda cc: remote(m.vec.at[:, rows(cc, s.dc)], m.vec_in.at[c], "vec", r, cc).start())
            m.vec_in[c] = m.vec[:, rows(c, s.dc)]
        dout = dot_nt(m.drf[l], m.wproj[l]).astype(BF16)
        for i in range(4):
            block = two_heads(dout[i * s.qc : (i + 1) * s.qc, :])
            kept = m.att[l, i * s.qc : (i + 1) * s.qc, :]
            m.do2[i] = block.astype(BF16)
            m.delta[i] = jnp.sum(block * jnp.concatenate([kept, kept], axis=0), axis=1, keepdims=True)
            m.dq2[i] = jnp.zeros((2 * s.qc, s.dc), F32)
        if l + 1 < L:
            sent_half("dkv", l + 1)
        for j in range(4):
            key_grad = jnp.zeros((s.nr * s.qc, s.dc), F32)
            value_grad = jnp.zeros((s.nr * s.qc, s.dc), F32)
            for n, i in QUERIES_OF[j]:
                prob = m.probs[l, n]
                prob_grad = dot_nt(m.do2[i], keys(l, j, True))
                score_grad = (prob.astype(F32) * (prob_grad - m.delta[i])).astype(BF16)
                m.dq2[i] += dot(score_grad, keys(l, j, False))
                key_grad = key_grad + dot_tn(score_grad, m.q2[l, i])
                value_grad = value_grad + dot_tn(prob, m.do2[i])
            shape = (s.nzx, 2, s.qc, s.dc)
            m.dkv[:, :, pl.ds(j * s.qc, s.qc), pl.ds(0, s.dc)] = key_grad.astype(BF16).reshape(shape)
            m.dkv[:, :, pl.ds(j * s.qc, s.qc), pl.ds(s.dc, s.dc)] = value_grad.astype(BF16).reshape(shape)
        reduce_start("dkv", l)
        for i in range(4):
            m.dqkv[i * s.qc : (i + 1) * s.qc, : s.dc] = (one_block(m.dq2[i]) * HEAD_DIM ** (-0.5)).astype(BF16)
        reduce_mid("dkv", l)
        if l + 1 < L:
            sent_half("gp", l + 1)
            sent_half("gq", l + 1)
        m.gproj[...] = dot_tn(m.att[l].astype(BF16), m.drf[l]).astype(BF16)
        reduce_start("gp", l)
        swap_back(l, "gd", reduce_end("gd", l))
        m.o_up[l] = reduce_end("gu", l)
        reduce_mid("gp", l)
        if l + 1 < L:
            swap_end(l + 1, "gd", m.o_down)
            swap_end(l + 1, "gp", m.o_proj)
            total = reduce_end("gq", l + 1)
            for which, out in enumerate((m.o_q, m.o_k, m.o_v)):
                out[l + 1] = total[:, which * s.dc : (which + 1) * s.dc]
        if l == 0:
            wait(m.recv, "vec", m.vec_in.at[pl.ds(0, few)])
            total = m.vec_in[0]
            for i in range(1, s.nc):
                total = total + m.vec_in[i]
            for i in range(L):
                to = i * 2 * VEC_ROWS + VEC_ROWS
                m.own[to : to + VEC_ROWS, :] = total[i * VEC_ROWS : (i + 1) * VEC_ROWS]
        m.dqkv[:, s.dc :] = reduce_end("dkv", l).astype(BF16)
        back = dot_nt(m.dqkv[...], m.wqkv[l].reshape(s.d, 3 * s.dc))
        if l:
            scatter(back, f"dx{l}")
        else:
            m.part[...] = back.astype(BF16)
            m.part[rows(c, s.t), :] = (m.part[rows(c, s.t), :].astype(F32) + m.carry[...]).astype(BF16)
            each_col(lambda cc: remote(m.part.at[:, rows(cc, s.dc)], m.got_in.at[c], "gin", r, cc).start())
            m.got_in[c] = m.part[:, rows(c, s.dc)]
        m.gqkv[...] = dot_tn(m.xf[l], m.dqkv[...]).astype(BF16).reshape(m.gqkv.shape)
        reduce_start("gq", l)
        sums = jnp.sum(m.dqkv[...].astype(F32), axis=0, keepdims=True)
        m.own[own + 4 : own + 5, :] = sums[:, : s.dc]
        m.own[own + 5 : own + 6, :] = sums[:, 2 * s.dc :]
        if l:
            grad = scattered(f"dx{l}") + m.carry[...]

    m.own_in[r] = m.own[...]
    each_row(lambda rr: remote(m.own, m.own_in.at[r], "own", rr, c).start())
    reduce_mid("gq", 0)
    swap_back(0, "gp", reduce_end("gp", 0))
    swap_end(0, "gd", m.o_down)
    wait(m.recv, "act", m.act_in.at[pl.ds(0, few * s.t)])
    m.o_act[...] = m.act_in[...]
    wait(m.recv, "gin", m.got_in.at[pl.ds(0, few)])
    total = m.got_in[0].astype(F32)
    for i in range(1, s.nc):
        total = total + m.got_in[i].astype(F32)
    m.o_in[...] = total
    wait(m.recv, "own", m.own_in.at[pl.ds(0, s.nr - 1)])
    total = m.own_in[0]
    for i in range(1, s.nr):
        total = total + m.own_in[i]
    m.o_vec[...] = total
    total = reduce_end("gq", 0)
    for which, out in enumerate((m.o_q, m.o_k, m.o_v)):
        out[0] = total[:, which * s.dc : (which + 1) * s.dc]
    swap_end(0, "gp", m.o_proj)

    wait(m.send, "x", m.xf.at[0, :, pl.ds(0, few * s.dc)])
    wait(m.send, "pvec", m.pv.at[:, pl.ds(0, few * s.dc)])
    wait(m.send, "cotan", m.cot.at[:, pl.ds(0, few * s.dc)])
    wait(m.send, "act", m.act_in.at[pl.ds(0, few * s.t)])
    wait(m.send, "gin", m.got_in.at[pl.ds(0, few)])
    wait(m.send, "vec", m.vec_in.at[pl.ds(0, few)])
    wait(m.send, "own", m.own_in.at[pl.ds(0, s.nr - 1)])

    @pl.when(jnp.logical_not(at_home))
    def _():
        wait(m.send, "wpt", m.wp_own)
        wait(m.send, "wdt", m.wd_own)
        for l in range(L):
            wait(m.send, f"gpt{l}", m.gproj_fin.at[l])
            wait(m.send, f"gdt{l}", m.gdown_fin.at[l])
    for l in range(L):
        for name in ("wq", "wp", "wu", "wd", "kv"):
            sent_gather(name, l)
        for name in ("gq", "gp", "gu", "gd", "dkv"):
            sent_pieces(name, l)
    for name in ("gq", "gp", "gu", "gd", "dkv"):
        sent_half(name, 0)


def body(s, layer_input, query_weight, key_weight, value_weight, proj_weight, up_weight, down_weight, query_shift,
         value_shift, proj_shift, up_shift, down_shift, first_gain, first_shift, second_gain, second_shift, segment_ids,
         cotangent):
    L = LAYERS
    places = segment_ids[: s.tok].reshape(4, 1, s.qc)
    segq = jnp.tile(places, (1, 2, 1)).reshape(4, 2 * s.qc, 1)
    segk = jnp.tile(places, (1, s.nr, 1)).reshape(4, s.nr * s.qc)
    shapes = scratch_of(s)
    square = jax.ShapeDtypeStruct((L, s.dr, s.dc), F32)
    out_shape = (
        jax.ShapeDtypeStruct((s.tok, s.dc), BF16),
        jax.ShapeDtypeStruct((s.tok, s.dc), F32),
        square, square, square, square,
        jax.ShapeDtypeStruct((L, s.dr, s.fc), F32),
        jax.ShapeDtypeStruct((L, s.fr, s.dc), F32),
        jax.ShapeDtypeStruct((L * 2 * VEC_ROWS, s.dc), F32),
    )
    vmem = pl.BlockSpec(memory_space=pltpu.VMEM)
    *arrays, o_vec = pl.pallas_call(
        functools.partial(kernel, s),
        out_shape=out_shape,
        in_specs=[vmem] * len(INPUTS),
        out_specs=[vmem] * len(OUTPUTS),
        scratch_shapes=[pltpu.VMEM(shape, dtype) for shape, dtype in shapes.values()]
        + [pltpu.SemaphoreType.DMA((len(PHASES),))] * 2,
        compiler_params=pltpu.CompilerParams(
            collective_id=0, has_side_effects=True, vmem_limit_bytes=60 * 2**20),
        name="encoder",
    )(layer_input, cotangent, query_weight, key_weight, value_weight, proj_weight, up_weight, down_weight, query_shift,
      value_shift, proj_shift, up_shift, down_shift, first_gain, first_shift, second_gain, second_shift, segq, segk)
    own = o_vec.reshape(L, 2 * VEC_ROWS, s.dc)
    up_rows = s.fc // LANES
    vectors = own[:, VEC_ROWS:]
    return (
        *arrays, own[:, 4], own[:, 5], vectors[:, PROJ_B], own[:, :up_rows].reshape(L, s.fc), vectors[:, DOWN_B],
        vectors[:, GAIN1], vectors[:, SHIFT1], vectors[:, GAIN2], vectors[:, SHIFT2],
    )


def build(mesh, tok, d, ff):
    s = Sizes(mesh.shape["row"], mesh.shape["col"], tok, d, ff)
    return jax.shard_map(
        functools.partial(body, s),
        mesh=mesh,
        in_specs=(P("row", "col"),) + (P(None, "row", "col"),) * 6 + (P(None, "col"),) * 9 + (P(), P("row", "col")),
        out_specs=(P("row", "col"),) * 2 + (P(None, "row", "col"),) * 6 + (P(None, "col"),) * 9,
        check_vma=False,
    )


def solution(mesh):
    return build(mesh, 256, 1024, 4096)
```

time: 489 us -> 276 us (0.56)
  Pallas kernels: 471 us -> 260 us
    pallas_call x1, Pallas kernels: 471 us -> 260 us  [body(): pl.pallas_call(functools.partial(kernel, s), out_shape=out_shape, in_spec...]
where the time goes in v2:
time: 276 us; the launch traced here: 273 us
  Pallas kernels  260 us (94%)
  local copies, waits for them, and re-layouts  12 us (4%)
    pallas_call x1, Pallas kernels, body(): pl.pallas_call(functools.partial(kernel, s), out_shape=out_shape, in_spec...  260 us
    unnamed x24, local copies, waits for them, and re-layouts  8.14 us

profile of v2, /device:TPU:2, one launch (start us, length us, event | category | flops | bytes accessed | tf_op | source)
XLA Modules:
  0.0 272.9 jit_solution(3507370092922731567)
XLA Ops:
  0.7 0.0 slice-start
  0.7 0.7 slice-done
  1.3 0.1 tile.16
  1.4 0.7 tile.20.refs_18_
  2.1 0.9 tile.21.refs_17_
  3.0 260.2 %encoder.1 = (bf16[256,128]{1,0:T(8,128)(2,1)}, f32[256,128]{1,0:T(8,128)}, f32[2,64,128]{2,1,0:T(8,128)}, f32[2,64,128]{2,1,0:T(8,128)}, f32[2,64,128]{2,1,0:T(...) custom-call(bf16[256,128]{1,0:T(8,128)(2,1)} %refs_0_.1, ...), custom_call_target="tpu_custom_call" | custom-call | tf_op jit(solution)/shard_map/encoder/pallas_call | solution.py:596
  263.3 0.0 copy-start.2
  263.3 0.7 slice_bitcast_fusion
  264.0 1.5 fusion
  265.5 0.6 copy.62
  266.1 1.5 copy.71
  267.6 0.0 copy-done.2
  267.6 0.0 copy-start.6
  267.6 0.0 copy-start.5
  267.6 0.0 copy-start.4
  267.6 0.7 copy.72
  268.3 0.2 copy-done.6
  268.4 0.0 copy-start.1
  268.4 0.6 copy.73
  269.1 0.0 copy-done.5
  269.1 0.6 copy.74
  269.7 0.0 copy-done.4
  269.7 0.0 copy-start.3
  269.7 0.6 copy.75
  270.3 0.2 copy-done.3
  270.6 0.6 copy.76
  271.2 0.0 copy-done.1
  271.2 0.0 copy-start
  271.2 0.7 copy.77
  271.9 0.3 copy-done
  272.2 0.7 copy.78
  (2 shorter events, 0.0 us)
Async XLA Ops:
  0.7 0.7 slice-start
  263.3 4.3 %copy-start.2 = (f32[256,128]{1,0:T(8,128)S(1)}, f32[256,128]{1,0:T(8,128)}, u32[]{:S(2)}) copy-start(f32[256,128]{1,0:T(8,128)} %get-tuple-element.61) | copy-start | bytes 393220
  267.6 0.8 copy-start.6
  267.6 1.5 copy-start.5
  267.6 2.1 copy-start.4
  268.4 2.8 %copy-start.1 = (f32[2,64,512]{2,1,0:T(8,128)S(1)}, f32[2,64,512]{2,1,0:T(8,128)}, u32[]{:S(2)}) copy-start(f32[2,64,512]{2,1,0:T(8,128)} %get-tuple-element.66) | copy-start | bytes 786436
  269.7 0.9 copy-start.3
  271.2 1.0 copy-start

commit v3 on v2

v3 whole, which is shorter than its diff:
```python
import functools
from types import SimpleNamespace

import jax
import jax.numpy as jnp
from jax import lax
from jax.experimental import pallas as pl
from jax.experimental.pallas import tpu as pltpu
from jax.sharding import PartitionSpec as P

MESH = pl.DeviceIdType.MESH
LAYERS = 2
HEAD_DIM = 64
LANES = 128
F32 = jnp.float32
BF16 = jnp.bfloat16
PAIRS = ((0, 0), (1, 1), (1, 2), (2, 1), (2, 2), (2, 3), (3, 2), (3, 3))
KEYS_OF = {i: [(n, j) for n, (a, j) in enumerate(PAIRS) if a == i] for i in range(4)}
QUERIES_OF = {j: [(n, i) for n, (i, b) in enumerate(PAIRS) if b == j] for j in range(4)}

PROJ_B, DOWN_B, GAIN1, SHIFT1, GAIN2, SHIFT2 = range(6)
VEC_ROWS = 8


def dot(a, b):
    return jnp.dot(a, b, preferred_element_type=F32)


def dot_nt(a, b):
    return lax.dot_general(a, b, (((1,), (1,)), ((), ())), preferred_element_type=F32)


def dot_tn(a, b):
    return lax.dot_general(a, b, (((0,), (0,)), ((), ())), preferred_element_type=F32)


class Sizes:
    def __init__(self, nr, nc, tok, d, ff):
        self.nr, self.nc, self.tok, self.d, self.ff = nr, nc, tok, d, ff
        self.half = tok // 2
        self.t = self.half // nc
        self.dc, self.fc = d // nc, ff // nc
        self.dr, self.fr = d // nr, ff // nr
        self.nz = nr // 4
        self.nzx = nr // 2
        self.qc = tok // 4


def scratch_of(s):
    L = LAYERS
    v = {}
    v["xf"] = ((L, 2, s.half, s.d), BF16)
    v["x1"] = ((L, 2, s.half, s.d), BF16)
    v["dff"] = ((L, 2, s.half, s.d), BF16)
    v["drf"] = ((L, 2, s.half, s.d), BF16)
    v["part"] = ((2, s.half, s.d), BF16)
    v["got"] = ((2, s.nc, s.t, s.d), BF16)
    v["got_in"] = ((2, s.nc, s.half, s.dc), BF16)
    v["act_out"] = ((2, s.t, s.d), BF16)
    v["act_in"] = ((2, s.half, s.dc), BF16)
    v["cot"] = ((2, s.t, s.d), BF16)
    v["pv"] = ((L * VEC_ROWS, s.d), F32)
    v["kv"] = ((L, s.nzx, 2, s.tok, 2 * s.dc), BF16)
    v["dkv"] = ((2, s.nzx, 2, s.half, 2 * s.dc), BF16)
    v["dkv_c"] = ((L, 2, s.nzx, s.half, 2 * s.dc), BF16)
    v["dkv_in"] = ((L, 2, s.nzx, s.half, 2 * s.dc), BF16)
    v["probs"] = ((L, len(PAIRS), 2 * s.qc, s.nr * s.qc), BF16)
    v["q2"] = ((L, 4, 2 * s.qc, s.dc), BF16)
    v["do2"] = ((4, 2 * s.qc, s.dc), BF16)
    v["delta"] = ((4, 2 * s.qc, 1), F32)
    v["dq2"] = ((4, 2 * s.qc, s.dc), F32)
    v["att"] = ((L, s.tok, s.dc), F32)
    v["gate"] = ((L, 2, s.half, s.fc), BF16)
    v["slope"] = ((L, 2, s.half, s.fc), F32)
    v["de"] = ((2, s.half, s.fc), BF16)
    v["n1"] = ((L, 2, s.t, s.d), F32)
    v["n2"] = ((L, 2, s.t, s.d), F32)
    v["r1"] = ((L, 2, s.t, 1), F32)
    v["r2"] = ((L, 2, s.t, 1), F32)
    v["carry"] = ((2, s.t, s.d), F32)
    v["dqkv"] = ((s.tok, 3 * s.dc), BF16)
    v["wqkv"] = ((L, s.nzx, 2, s.dr, 3 * s.dc), BF16)
    v["wup"] = ((L, s.nzx, 2, s.dr, s.fc), BF16)
    v["wproj"] = ((L, s.dc, s.d), BF16)
    v["wdown"] = ((L, s.fc, s.d), BF16)
    v["wp_own"] = ((L, s.dr, s.dc), BF16)
    v["wd_own"] = ((L, s.fr, s.dc), BF16)
    v["gqkv"] = ((s.nzx, 2, s.dr, 3 * s.dc), BF16)
    v["gup"] = ((s.nzx, 2, s.dr, s.fc), BF16)
    v["gproj"] = ((s.dc, s.d), BF16)
    v["gdown"] = ((s.fc, s.d), BF16)
    v["gqkv_c"] = ((L, s.nzx, s.dr, 3 * s.dc), BF16)
    v["gup_c"] = ((L, s.nzx, s.dr, s.fc), BF16)
    v["gproj_c"] = ((L, s.dr, s.d), BF16)
    v["gdown_c"] = ((L, s.fr, s.d), BF16)
    v["gqkv_in"] = ((L, s.nzx, s.dr, 3 * s.dc), BF16)
    v["gup_in"] = ((L, s.nzx, s.dr, s.fc), BF16)
    v["gproj_in"] = ((L, s.dr, s.d), BF16)
    for name, shape in (("gq", (s.dr, 3 * s.dc)), ("gp", (s.dr, s.dc)), ("gu", (s.dr, s.fc)), ("gd", (s.fr, s.dc))):
        v[f"t_{name}"] = (shape, F32)
        v[f"t_{name}_out"] = ((L,) + shape, BF16)
        v[f"t_{name}_in"] = ((L,) + shape, BF16)
    v["gdown_in"] = ((L, s.fr, s.d), BF16)
    v["gproj_out"] = ((L, s.dr, s.dc), BF16)
    v["gdown_out"] = ((L, s.fr, s.dc), BF16)
    v["gproj_fin"] = ((L, s.dr, s.dc), BF16)
    v["gdown_fin"] = ((L, s.fr, s.dc), BF16)
    v["vec"] = ((L * VEC_ROWS, s.d), F32)
    v["vec_in"] = ((s.nc, L * VEC_ROWS, s.dc), F32)
    v["own"] = ((L * 2 * VEC_ROWS, s.dc), F32)
    v["own_in"] = ((s.nr, L * 2 * VEC_ROWS, s.dc), F32)
    return v


INPUTS = ("x", "cotan", "wq", "wk", "wv", "wp", "wu", "wd", "qb", "vb", "pb", "upb", "db", "g1", "s1", "g2", "s2", "segq",
          "segk")
OUTPUTS = ("o_act", "o_in", "o_q", "o_k", "o_v", "o_proj", "o_up", "o_down", "o_vec")
ROW_PHASES = ("wq", "wp", "wu", "wd", "kva", "kvb", "dkva", "dkvb", "gq", "gp", "gu", "gd")
PHASES = (
    ["x", "cotan", "pvec", "act", "vec", "own", "wpt", "wdt"]
    + [f"{n}{l}" for l in range(LAYERS) for n in ("gpt", "gdt")]
    + [f"{n}{l}{a}" for l in range(LAYERS) for n in ("pr", "n1", "fr", "h", "df", "dn", "dr", "dx") for a in range(2)]
    + [f"{n}{l}{e}" for l in range(LAYERS) for n in ROW_PHASES
       for e in ("", "c", "x")]
)
IN_STEPS = ("wp0", "wu0", "wd0", "wq1", "wp1", "wu1", "wd1", "gu0", "gd0", "gp0", "gq1", "gp1", "gu1", "gd1")
KV = {"kva": 0, "kvb": 1}
DKV = {"dkva": 0, "dkvb": 1}
PHASE = {name: index for index, name in enumerate(PHASES)}


def kernel(s, *refs):
    names = INPUTS + OUTPUTS + tuple(scratch_of(s)) + ("send", "recv")
    m = SimpleNamespace(**dict(zip(names, refs)))
    L = LAYERS
    r, c = lax.axis_index("row"), lax.axis_index("col")
    zx, k = lax.div(r, 2), lax.rem(r, 2)
    z, x = lax.div(zx, 2), lax.rem(zx, 2)
    across = z * 2 + 1 - x
    other = zx * 2 + 1 - k
    at_home = zx == c
    chips, few = s.nzx - 1, s.nc - 1

    def remote(src, dst, phase, row, col):
        return pltpu.make_async_remote_copy(
            src_ref=src, dst_ref=dst, send_sem=m.send.at[PHASE[phase]], recv_sem=m.recv.at[PHASE[phase]],
            device_id=(row, col), device_id_type=MESH)

    def wait(sems, phase, ref):
        pltpu.make_async_copy(ref, ref, sems.at[PHASE[phase]]).wait()

    def each_col(fn):
        def step(q, carry):
            fn(lax.rem(c + q, s.nc))
            return carry
        lax.fori_loop(1, s.nc, step, 0)

    def each_row(fn):
        def step(q, carry):
            fn(lax.rem(r + q, s.nr))
            return carry
        lax.fori_loop(1, s.nr, step, 0)

    def each_chip(fn):
        def step(q, carry):
            fn(lax.rem(zx + q, s.nzx))
            return carry
        lax.fori_loop(1, s.nzx, step, 0)

    def each_z(fn):
        def step(q, carry):
            fn(lax.rem(z + q, s.nz))
            return carry
        lax.fori_loop(1, s.nz, step, 0)

    def rows(i, n):
        return pl.ds(pl.multiple_of(i * n, n), n)

    barrier = pltpu.get_barrier_semaphore()

    def greet(row, col):
        pl.semaphore_signal(barrier, inc=1, device_id=(row, col), device_id_type=MESH)

    swap_row, swap_col = c * 2 + k, zx
    each_col(lambda cc: greet(r, cc))
    each_row(lambda rr: greet(rr, c))

    @pl.when(jnp.logical_not(at_home))
    def _():
        greet(swap_row, swap_col)

    def weight(name, l):
        chips = s.nzx - (2 if f"{name}{l}" in IN_STEPS else 1)
        if name in KV:
            span = pl.ds(KV[name] * s.half, s.half)
            return ((lambda i, kk: m.kv.at[l, i, kk, span]), (lambda kk: m.kv.at[l, :, kk, span]),
                    m.kv.at[l, pl.ds(0, chips), 0, span] if chips else None)
        if name in ("wq", "wu"):
            ref = {"wq": m.wqkv, "wu": m.wup}[name]
            return (lambda i, kk: ref.at[l, i, kk]), (lambda kk: ref.at[l, :, kk]), \
                ref.at[l, pl.ds(0, chips), 0] if chips else None
        ref, n = {"wp": (m.wproj, s.dr), "wd": (m.wdown, s.fr)}[name]
        return ((lambda i, kk: ref.at[l, rows(kk, n), rows(i, s.dc)]), (lambda kk: ref.at[l, rows(kk, n)]),
                ref.at[l, pl.ds(0, n), pl.ds(0, chips * s.dc)] if chips else None)

    def gather(name, l):
        piece = weight(name, l)[0](zx, k)
        if f"{name}{l}" not in IN_STEPS:
            each_chip(lambda i: remote(piece, piece, f"{name}{l}", i * 2 + k, c).start())
            return
        remote(piece, piece, f"{name}{l}x", across * 2 + k, c).start()
        each_z(lambda i: remote(piece, piece, f"{name}{l}", (i * 2 + x) * 2 + k, c).start())

    def forward(name, l):
        piece = weight(name, l)[0](across, k)
        wait(m.recv, f"{name}{l}x", piece)
        each_z(lambda i: remote(piece, piece, f"{name}{l}", (i * 2 + x) * 2 + k, c).start())

    def pass_on(name, l):
        _, half, many = weight(name, l)
        if many is not None:
            wait(m.recv, f"{name}{l}", many)
        remote(half(k), half(k), f"{name}{l}c", other, c).start()

    def gathered(name, l):
        wait(m.recv, f"{name}{l}c", weight(name, l)[1](1 - k))

    def sent_gather(name, l):
        piece, half, many = weight(name, l)
        if many is not None:
            wait(m.send, f"{name}{l}", many)
        if f"{name}{l}" in IN_STEPS:
            wait(m.send, f"{name}{l}x", piece(zx, k))
        wait(m.send, f"{name}{l}c", half(k))

    def partial_sum(name, l):
        if name in DKV:
            a = DKV[name]
            mid, got = m.dkv_c.at[l, a], m.dkv_in.at[l, a]
            return (lambda kk: m.dkv.at[a, :, kk]), mid, (lambda i: mid.at[i]), got
        if name in ("gq", "gu"):
            full, mid, got = {"gq": (m.gqkv, m.gqkv_c.at[l], m.gqkv_in.at[l]),
                              "gu": (m.gup, m.gup_c.at[l], m.gup_in.at[l])}[name]
            return (lambda kk: full.at[:, kk]), mid, (lambda i: mid.at[i]), got
        full, mid, got, n = {"gp": (m.gproj, m.gproj_c.at[l], m.gproj_in.at[l], s.dr),
                             "gd": (m.gdown, m.gdown_c.at[l], m.gdown_in.at[l], s.fr)}[name]
        return (lambda kk: full.at[rows(kk, n)]), mid, (lambda i: mid.at[:, rows(i, s.dc)]), got

    def reduce_start(name, l):
        half, mid, _, _ = partial_sum(name, l)
        remote(half(1 - k), mid, f"{name}{l}c", other, c).start()

    def both(name, mid, i):
        if name in ("gp", "gd"):
            return mid.at[:, rows(i, 2 * s.dc)]
        return mid.at[pl.ds(2 * i, 2)]

    def m_pair(name, got, i):
        if name in ("gp", "gd"):
            return got.at[:, rows(i, 2 * s.dc)]
        return got.at[pl.ds(2 * i, 2)]

    def reduce_turn(name, l):
        _, mid, piece, got = partial_sum(name, l)
        if s.nz > 1:
            wait(m.recv, f"{name}{l}", m_all(name, got))
        sums = []
        for which in (x, 1 - x):
            total = piece(z * 2 + which)[...].astype(F32)
            for q in range(1, s.nz):
                i = lax.rem(z + q, s.nz) * 2 + which
                arrived = got[:, rows(i, s.dc)] if name in ("gp", "gd") else got[i]
                total = total + arrived.astype(F32)
            sums.append(total)
        kept, out, back = turned(name, l)
        kept[...] = sums[0]
        out[...] = sums[1].astype(BF16)
        remote(out, back, f"{name}{l}x", across * 2 + k, c).start()

    def turned(name, l):
        return {"gq": (m.t_gq, m.t_gq_out.at[l], m.t_gq_in.at[l]), "gp": (m.t_gp, m.t_gp_out.at[l], m.t_gp_in.at[l]),
                "gu": (m.t_gu, m.t_gu_out.at[l], m.t_gu_in.at[l]), "gd": (m.t_gd, m.t_gd_out.at[l], m.t_gd_in.at[l])}[name]

    def m_all(name, got):
        if name in ("gp", "gd"):
            return got.at[:, pl.ds(0, 2 * (s.nz - 1) * s.dc)]
        return got.at[pl.ds(0, 2 * (s.nz - 1))]

    def reduce_mid(name, l):
        half, mid, piece, got = partial_sum(name, l)
        wait(m.recv, f"{name}{l}c", mid)
        mid[...] = (half(k)[...].astype(F32) + mid[...].astype(F32)).astype(BF16)
        if f"{name}{l}" in IN_STEPS:
            each_z(lambda i: remote(both(name, mid, i), m_pair(name, got, z), f"{name}{l}", (i * 2 + x) * 2 + k, c).start())
            return
        each_chip(lambda i: remote(piece(i), got.at[zx], f"{name}{l}", i * 2 + k, c).start())
        got[zx] = piece(zx)[...]

    def reduce_end(name, l):
        if f"{name}{l}" in IN_STEPS:
            kept, _, back = turned(name, l)
            wait(m.recv, f"{name}{l}x", back)
            return kept[...] + back[...].astype(F32)
        got = partial_sum(name, l)[3]
        wait(m.recv, f"{name}{l}", got.at[pl.ds(0, chips)])
        total = got[0].astype(F32)
        for i in range(1, s.nzx):
            total = total + got[i].astype(F32)
        return total

    def sent_half(name, l):
        wait(m.send, f"{name}{l}c", partial_sum(name, l)[1])

    def sent_pieces(name, l):
        if f"{name}{l}" in IN_STEPS:
            if s.nz > 1:
                wait(m.send, f"{name}{l}", m_all(name, partial_sum(name, l)[3]))
            wait(m.send, f"{name}{l}x", turned(name, l)[1])
            return
        wait(m.send, f"{name}{l}", partial_sum(name, l)[3].at[pl.ds(0, chips)])

    m.xf[0, :, :, rows(c, s.dc)] = m.x[...]
    m.cot[:, :, rows(c, s.dc)] = m.cotan[:, rows(c, s.t), :]
    m.pv[:, rows(c, s.dc)] = jnp.zeros((L * VEC_ROWS, s.dc), F32)
    for l in range(L):
        for which, ref in enumerate((m.pb, m.db, m.g1, m.s1, m.g2, m.s2)):
            m.pv[l * VEC_ROWS + which : l * VEC_ROWS + which + 1, rows(c, s.dc)] = ref[l : l + 1, :].astype(F32)
        for which, ref in enumerate((m.wq, m.wk, m.wv)):
            m.wqkv[l, zx, k, :, which * s.dc : (which + 1) * s.dc] = ref[l]
        m.wup[l, zx, k] = m.wu[l]

    pl.semaphore_wait(barrier, s.nc - 1 + s.nr - 1 + 1 - at_home.astype(jnp.int32))

    gather("wq", 0)
    each_col(lambda cc: remote(m.x, m.xf.at[0, :, :, rows(c, s.dc)], "x", r, cc).start())

    @pl.when(jnp.logical_not(at_home))
    def _():
        remote(m.wp, m.wp_own, "wpt", swap_row, swap_col).start()
        remote(m.wd, m.wd_own, "wdt", swap_row, swap_col).start()
    mine = m.pv.at[:, rows(c, s.dc)]
    each_col(lambda cc: remote(mine, mine, "pvec", r, cc).start())
    each_col(lambda cc: remote(
        m.cotan.at[:, rows(cc, s.t)], m.cot.at[:, :, rows(c, s.dc)], "cotan", r, cc).start())
    m.vec[...] = jnp.zeros(m.vec.shape, F32)
    m.own[...] = jnp.zeros(m.own.shape, F32)

    def vector(l, which):
        return m.pv[l * VEC_ROWS + which : l * VEC_ROWS + which + 1, :]

    def share(buf, value, phase):
        buf[rows(c, s.t), :] = value
        each_col(lambda cc: remote(buf.at[rows(c, s.t)], buf.at[rows(c, s.t)], phase, r, cc).start())

    def shared(buf, phase):
        for sems in (m.recv, m.send):
            wait(sems, phase, buf.at[pl.ds(0, few * s.t)])

    def scatter(a, value, phase):
        m.part[a] = value.astype(BF16)
        each_col(lambda cc: remote(m.part.at[a, rows(cc, s.t)], m.got.at[a, c], phase, r, cc).start())
        m.got[a, c] = m.part[a, rows(c, s.t), :]

    def scattered(a, phase):
        for sems in (m.recv, m.send):
            wait(sems, phase, m.got.at[a, pl.ds(0, few)])
        total = m.got[a, 0].astype(F32)
        for i in range(1, s.nc):
            total = total + m.got[a, i].astype(F32)
        return total

    def norm(u, l, a, gain, shift, n_ref, r_ref):
        mean = jnp.sum(u, axis=1, keepdims=True) / s.d
        var = jnp.sum(u * u, axis=1, keepdims=True) / s.d - mean * mean
        inv = lax.rsqrt(var + 1e-12)
        n = (u - mean) * inv
        n_ref[l, a] = n
        r_ref[l, a] = inv
        return n * vector(l, gain) + vector(l, shift)

    def add_row(ref, at, value):
        ref[at : at + 1, :] += jnp.sum(value, axis=0, keepdims=True)

    def norm_back(g, l, a, gain, shift, n_ref, r_ref):
        n = n_ref[l, a]
        w = g * vector(l, gain)
        first = jnp.sum(w, axis=1, keepdims=True) / s.d
        second = jnp.sum(w * n, axis=1, keepdims=True) / s.d
        add_row(m.vec, l * VEC_ROWS + gain, g * n)
        add_row(m.vec, l * VEC_ROWS + shift, g)
        return r_ref[l, a] * (w - first - n * second)

    low_lanes = lax.broadcasted_iota(jnp.int32, (s.qc, s.dc), 1) < HEAD_DIM

    def two_heads(block):
        block = block.astype(F32)
        return jnp.concatenate([jnp.where(low_lanes, block, 0.0), jnp.where(low_lanes, 0.0, block)], axis=0)

    def one_block(pair):
        return jnp.where(low_lanes, pair[: s.qc], pair[s.qc :])

    def keys(l, j, value):
        lanes = pl.ds(s.dc if value else 0, s.dc)
        return m.kv[l, :, :, pl.ds(j * s.qc, s.qc), lanes].reshape(s.nr * s.qc, s.dc)

    def swapped(l):
        m.wproj[l, rows(k, s.dr), rows(zx, s.dc)] = m.wp_own[l]
        m.wdown[l, rows(k, s.fr), rows(zx, s.dc)] = m.wd_own[l]

    pass_on("wq", 0)
    wait(m.recv, "x", m.xf.at[0, :, :, pl.ds(0, few * s.dc)])
    wait(m.recv, "pvec", m.pv.at[:, pl.ds(0, few * s.dc)])

    @pl.when(at_home)
    def _():
        m.wp_own[...] = m.wp[...]
        m.wd_own[...] = m.wd[...]

    @pl.when(jnp.logical_not(at_home))
    def _():
        wait(m.recv, "wpt", m.wp_own)
        wait(m.recv, "wdt", m.wd_own)
    swapped(0)

    def attend(l, i):
        queries = m.q2[l, i]
        ids = m.segq[i]
        scores = []
        for _, j in KEYS_OF[i]:
            raw = dot_nt(queries, keys(l, j, False))
            scores.append(jnp.where(ids == m.segk[j : j + 1, :], raw, -1e9))
        top = functools.reduce(jnp.maximum, [jnp.max(x, axis=1, keepdims=True) for x in scores])
        raised = [jnp.exp(x - top) for x in scores]
        inverse = 1.0 / sum(jnp.sum(x, axis=1, keepdims=True) for x in raised)
        out = jnp.zeros((2 * s.qc, s.dc), F32)
        for (n, j), x in zip(KEYS_OF[i], raised):
            prob = (x * inverse).astype(BF16)
            m.probs[l, n] = prob
            out = out + dot(prob, keys(l, j, True))
        m.att[l, i * s.qc : (i + 1) * s.qc, :] = one_block(out)

    def span(a):
        return pl.ds(a * s.half, s.half)

    for l in range(L):
        for a in range(2):
            if l:
                shared(m.xf.at[l, a], f"h{l - 1}{a}")
            elif a == 0:
                gathered("wq", 0)
                for b in range(2):
                    m.carry[b] = m.xf[0, b, rows(c, s.t), :].astype(F32)
            if l and a == 0:
                gathered("wq", l)
            qkv = dot(m.xf[l, a], m.wqkv[l].reshape(s.d, 3 * s.dc))
            keep = (qkv[:, 2 * s.dc :] + m.vb[l : l + 1, :].astype(F32)).astype(BF16)
            m.kv[l, zx, k, span(a), : s.dc] = qkv[:, s.dc : 2 * s.dc].astype(BF16)
            m.kv[l, zx, k, span(a), s.dc :] = keep
            gather("kva" if a == 0 else "kvb", l)
            for i in range(2):
                block = (qkv[i * s.qc : (i + 1) * s.qc, : s.dc] + m.qb[l : l + 1, :].astype(F32)).astype(BF16)
                m.q2[l, 2 * a + i] = (two_heads(block) * HEAD_DIM ** (-0.5)).astype(BF16)
        if l == 0:
            gather("wp", 0)
        if l == 0:
            forward("wp", 0)
        pass_on("kva", l)
        pass_on("kvb", l)
        if l == 0:
            gather("wu", 0)
            gather("wd", 0)
            pass_on("wp", 0)
        else:
            pass_on("wu", 1)
            pass_on("wd", 1)
        gathered("kva", l)
        attend(l, 0)
        gathered("kvb", l)
        attend(l, 1)
        gathered("wp", l)
        scatter(0, dot(m.att[l, span(0), :].astype(BF16), m.wproj[l]), f"pr{l}0")
        attend(l, 2)
        attend(l, 3)
        scatter(1, dot(m.att[l, span(1), :].astype(BF16), m.wproj[l]), f"pr{l}1")
        if l == 0:
            forward("wu", 0)
            forward("wd", 0)
            swapped(1)
        for a in range(2):
            u = scattered(a, f"pr{l}{a}") + vector(l, PROJ_B) + m.carry[a]
            first_out = norm(u, l, a, GAIN1, SHIFT1, m.n1, m.r1)
            share(m.x1.at[l, a], first_out.astype(BF16), f"n1{l}{a}")
            m.carry[a] = first_out
        if l == 0:
            pass_on("wu", 0)
            pass_on("wd", 0)
            gather("wq", 1)
            gather("wp", 1)
        gathered("wu", l)
        for a in range(2):
            shared(m.x1.at[l, a], f"n1{l}{a}")
            pre = dot(m.x1[l, a], m.wup[l].reshape(s.d, s.fc)) + m.upb[l : l + 1, :].astype(F32)
            cdf = 0.5 * (1.0 + lax.erf(pre * 0.5**0.5))
            m.gate[l, a] = (pre * cdf).astype(BF16)
            if a == 0:
                gathered("wd", l)
            scatter(a, dot(m.gate[l, a], m.wdown[l]), f"fr{l}{a}")
            m.slope[l, a] = cdf + pre * (jnp.exp(-0.5 * pre * pre) * 0.3989422804014327)
        if l == 0:
            forward("wq", 1)
            forward("wp", 1)
            gather("wu", 1)
            gather("wd", 1)
        for a in range(2):
            u = scattered(a, f"fr{l}{a}") + vector(l, DOWN_B) + m.carry[a]
            hidden = norm(u, l, a, GAIN2, SHIFT2, m.n2, m.r2)
            if l == 0:
                share(m.xf.at[1, a], hidden.astype(BF16), f"h0{a}")
                m.carry[a] = hidden
            else:
                m.act_out[a] = hidden.astype(BF16)
        if l == 0:
            pass_on("wq", 1)
            pass_on("wp", 1)
            forward("wu", 1)
            forward("wd", 1)

    def swap_back(l, name, total):
        out, fin, phase = {"gp": (m.gproj_out, m.gproj_fin, f"gpt{l}"), "gd": (m.gdown_out, m.gdown_fin, f"gdt{l}")}[name]
        out[l] = total.astype(BF16)

        @pl.when(jnp.logical_not(at_home))
        def _():
            remote(out.at[l], fin.at[l], phase, swap_row, swap_col).start()

        @pl.when(at_home)
        def _():
            fin[l] = out[l]

    def swap_end(l, name, out):
        fin, phase = {"gp": (m.gproj_fin, f"gpt{l}"), "gd": (m.gdown_fin, f"gdt{l}")}[name]

        @pl.when(jnp.logical_not(at_home))
        def _():
            wait(m.recv, phase, fin.at[l])
        out[l] = fin[l].astype(F32)

    def attend_back(l, j):
        key_grad = jnp.zeros((s.nr * s.qc, s.dc), F32)
        value_grad = jnp.zeros((s.nr * s.qc, s.dc), F32)
        for n, i in QUERIES_OF[j]:
            prob = m.probs[l, n]
            prob_grad = dot_nt(m.do2[i], keys(l, j, True))
            score_grad = (prob.astype(F32) * (prob_grad - m.delta[i])).astype(BF16)
            m.dq2[i] += dot(score_grad, keys(l, j, False))
            key_grad = key_grad + dot_tn(score_grad, m.q2[l, i])
            value_grad = value_grad + dot_tn(prob, m.do2[i])
        shape = (s.nzx, 2, s.qc, s.dc)
        place = pl.ds(j % 2 * s.qc, s.qc)
        m.dkv[j // 2, :, :, place, pl.ds(0, s.dc)] = key_grad.astype(BF16).reshape(shape)
        m.dkv[j // 2, :, :, place, pl.ds(s.dc, s.dc)] = value_grad.astype(BF16).reshape(shape)

    wait(m.recv, "cotan", m.cot.at[:, :, pl.ds(0, few * s.dc)])
    for l in reversed(range(L)):
        at = l * VEC_ROWS
        own = l * 2 * VEC_ROWS
        for a in range(2):
            if l + 1 < L:
                grad = scattered(a, f"dx{l + 1}{a}") + m.carry[a]
            else:
                grad = m.cot[a].astype(F32)
            dz = norm_back(grad, l, a, GAIN2, SHIFT2, m.n2, m.r2)
            m.carry[a] = dz
            low = dz.astype(BF16)
            share(m.dff.at[l, a], low, f"df{l}{a}")
            add_row(m.vec, at + DOWN_B, low.astype(F32))
        if l + 1 == L:
            each_col(lambda cc: remote(
                m.act_out.at[:, :, rows(cc, s.dc)], m.act_in.at[:, rows(c, s.t)], "act", r, cc).start())
            m.act_in[:, rows(c, s.t), :] = m.act_out[:, :, rows(c, s.dc)]
        else:
            reduce_mid("gq", l + 1)
            reduce_turn("gp", l + 1)
        for a in range(2):
            shared(m.dff.at[l, a], f"df{l}{a}")
            de = (dot_nt(m.dff[l, a], m.wdown[l]) * m.slope[l, a]).astype(BF16)
            m.de[a] = de
            scatter(a, dot_nt(de, m.wup[l].reshape(s.d, s.fc)), f"dn{l}{a}")
            sums = jnp.sum(de.astype(F32), axis=0, keepdims=True)
            for i in range(s.fc // LANES):
                m.own[own + i : own + i + 1, :] += sums[:, i * LANES : (i + 1) * LANES]
        if l + 1 < L:
            reduce_turn("gq", l + 1)
            swap_back(l + 1, "gp", reduce_end("gp", l + 1))
            sent_half("gd", l + 1)
            sent_half("gu", l + 1)
        m.gdown[...] = dot_tn(m.gate[l].reshape(s.tok, s.fc), m.dff[l].reshape(s.tok, s.d)).astype(BF16)
        reduce_start("gd", l)
        for a in range(2):
            grad = scattered(a, f"dn{l}{a}") + m.carry[a]
            du = norm_back(grad, l, a, GAIN1, SHIFT1, m.n1, m.r1)
            m.carry[a] = du
            low = du.astype(BF16)
            share(m.drf.at[l, a], low, f"dr{l}{a}")
            add_row(m.vec, at + PROJ_B, low.astype(F32))
        m.gup[...] = dot_tn(m.x1[l].reshape(s.tok, s.d), m.de[...].reshape(s.tok, s.fc)).astype(BF16).reshape(m.gup.shape)
        reduce_start("gu", l)
        reduce_mid("gd", l)
        if l == 0:
            each_col(lambda cc: remote(m.vec.at[:, rows(cc, s.dc)], m.vec_in.at[c], "vec", r, cc).start())
            m.vec_in[c] = m.vec[:, rows(c, s.dc)]
        if l + 1 < L:
            sent_half("dkva", l + 1)
            sent_half("dkvb", l + 1)
        for a in range(2):
            shared(m.drf.at[l, a], f"dr{l}{a}")
            dout = dot_nt(m.drf[l, a], m.wproj[l]).astype(BF16)
            for b in range(2):
                i = 2 * a + b
                block = two_heads(dout[b * s.qc : (b + 1) * s.qc, :])
                kept = m.att[l, i * s.qc : (i + 1) * s.qc, :]
                m.do2[i] = block.astype(BF16)
                m.delta[i] = jnp.sum(block * jnp.concatenate([kept, kept], axis=0), axis=1, keepdims=True)
                m.dq2[i] = jnp.zeros((2 * s.qc, s.dc), F32)
            if a == 0:
                attend_back(l, 0)
                reduce_mid("gu", l)
        attend_back(l, 1)
        reduce_start("dkva", l)
        attend_back(l, 2)
        reduce_mid("dkva", l)
        attend_back(l, 3)
        reduce_start("dkvb", l)
        for i in range(4):
            m.dqkv[i * s.qc : (i + 1) * s.qc, : s.dc] = (one_block(m.dq2[i]) * HEAD_DIM ** (-0.5)).astype(BF16)
        reduce_mid("dkvb", l)
        reduce_turn("gd", l)
        if l + 1 < L:
            sent_half("gp", l + 1)
            sent_half("gq", l + 1)
        m.gproj[...] = dot_tn(m.att[l].astype(BF16), m.drf[l].reshape(s.tok, s.d)).astype(BF16)
        reduce_start("gp", l)
        reduce_turn("gu", l)
        if l == 0:
            wait(m.recv, "vec", m.vec_in.at[pl.ds(0, few)])
            total = m.vec_in[0]
            for i in range(1, s.nc):
                total = total + m.vec_in[i]
            for i in range(L):
                to = i * 2 * VEC_ROWS + VEC_ROWS
                m.own[to : to + VEC_ROWS, :] = total[i * VEC_ROWS : (i + 1) * VEC_ROWS]
        for a in range(2):
            m.dqkv[span(a), s.dc :] = reduce_end("dkva" if a == 0 else "dkvb", l).astype(BF16)
            back = dot_nt(m.dqkv[span(a), :], m.wqkv[l].reshape(s.d, 3 * s.dc))
            if l:
                scatter(a, back, f"dx{l}{a}")
            else:
                m.part[a] = back.astype(BF16)
                mine = m.part[a, rows(c, s.t), :].astype(F32) + m.carry[a]
                m.part[a, rows(c, s.t), :] = mine.astype(BF16)
                each_col(lambda cc: remote(m.part.at[a, :, rows(cc, s.dc)], m.got_in.at[a, c], f"dx0{a}", r, cc).start())
                m.got_in[a, c] = m.part[a, :, rows(c, s.dc)]
        m.gqkv[...] = dot_tn(m.xf[l].reshape(s.tok, s.d), m.dqkv[...]).astype(BF16).reshape(m.gqkv.shape)
        reduce_start("gq", l)
        sums = jnp.sum(m.dqkv[...].astype(F32), axis=0, keepdims=True)
        m.own[own + 4 : own + 5, :] = sums[:, : s.dc]
        m.own[own + 5 : own + 6, :] = sums[:, 2 * s.dc :]
        reduce_mid("gp", l)
        swap_back(l, "gd", reduce_end("gd", l))
        m.o_up[l] = reduce_end("gu", l)
        if l + 1 < L:
            swap_end(l + 1, "gd", m.o_down)
            swap_end(l + 1, "gp", m.o_proj)
            total = reduce_end("gq", l + 1)
            for which, out in enumerate((m.o_q, m.o_k, m.o_v)):
                out[l + 1] = total[:, which * s.dc : (which + 1) * s.dc]

    m.own_in[r] = m.own[...]
    each_row(lambda rr: remote(m.own, m.own_in.at[r], "own", rr, c).start())
    reduce_mid("gq", 0)
    reduce_turn("gp", 0)
    swap_end(0, "gd", m.o_down)
    wait(m.recv, "act", m.act_in.at[:, pl.ds(0, few * s.t)])
    m.o_act[...] = m.act_in[...]
    for a in range(2):
        wait(m.recv, f"dx0{a}", m.got_in.at[a, pl.ds(0, few)])
        total = m.got_in[a, 0].astype(F32)
        for i in range(1, s.nc):
            total = total + m.got_in[a, i].astype(F32)
        m.o_in[a] = total
    swap_back(0, "gp", reduce_end("gp", 0))
    wait(m.recv, "own", m.own_in.at[pl.ds(0, s.nr - 1)])
    total = m.own_in[0]
    for i in range(1, s.nr):
        total = total + m.own_in[i]
    m.o_vec[...] = total
    total = reduce_end("gq", 0)
    for which, out in enumerate((m.o_q, m.o_k, m.o_v)):
        out[0] = total[:, which * s.dc : (which + 1) * s.dc]
    swap_end(0, "gp", m.o_proj)

    wait(m.send, "x", m.xf.at[0, :, :, pl.ds(0, few * s.dc)])
    wait(m.send, "pvec", m.pv.at[:, pl.ds(0, few * s.dc)])
    wait(m.send, "cotan", m.cot.at[:, :, pl.ds(0, few * s.dc)])
    wait(m.send, "act", m.act_in.at[:, pl.ds(0, few * s.t)])
    for a in range(2):
        wait(m.send, f"dx0{a}", m.got_in.at[a, pl.ds(0, few)])
    wait(m.send, "vec", m.vec_in.at[pl.ds(0, few)])
    wait(m.send, "own", m.own_in.at[pl.ds(0, s.nr - 1)])

    @pl.when(jnp.logical_not(at_home))
    def _():
        wait(m.send, "wpt", m.wp_own)
        wait(m.send, "wdt", m.wd_own)
        for l in range(L):
            wait(m.send, f"gpt{l}", m.gproj_fin.at[l])
            wait(m.send, f"gdt{l}", m.gdown_fin.at[l])
    for l in range(L):
        for name in ("wq", "wp", "wu", "wd", "kva", "kvb"):
            sent_gather(name, l)
        for name in ("gq", "gp", "gu", "gd", "dkva", "dkvb"):
            sent_pieces(name, l)
    for name in ("gq", "gp", "gu", "gd", "dkva", "dkvb"):
        sent_half(name, 0)


def body(s, layer_input, query_weight, key_weight, value_weight, proj_weight, up_weight, down_weight, query_shift,
         value_shift, proj_shift, up_shift, down_shift, first_gain, first_shift, second_gain, second_shift, segment_ids,
         cotangent):
    L = LAYERS
    places = segment_ids[: s.tok].reshape(4, 1, s.qc)
    segq = jnp.tile(places, (1, 2, 1)).reshape(4, 2 * s.qc, 1)
    segk = jnp.tile(places, (1, s.nr, 1)).reshape(4, s.nr * s.qc)
    shapes = scratch_of(s)
    halves = (2, s.half, s.dc)
    square = jax.ShapeDtypeStruct((L, s.dr, s.dc), F32)
    out_shape = (
        jax.ShapeDtypeStruct((2, s.half, s.dc), BF16),
        jax.ShapeDtypeStruct((2, s.half, s.dc), F32),
        square, square, square, square,
        jax.ShapeDtypeStruct((L, s.dr, s.fc), F32),
        jax.ShapeDtypeStruct((L, s.fr, s.dc), F32),
        jax.ShapeDtypeStruct((L * 2 * VEC_ROWS, s.dc), F32),
    )
    vmem = pl.BlockSpec(memory_space=pltpu.VMEM)
    o_act, o_in, *arrays, o_vec = pl.pallas_call(
        functools.partial(kernel, s),
        out_shape=out_shape,
        in_specs=[vmem] * len(INPUTS),
        out_specs=[vmem] * len(OUTPUTS),
        scratch_shapes=[pltpu.VMEM(shape, dtype) for shape, dtype in shapes.values()]
        + [pltpu.SemaphoreType.DMA((len(PHASES),))] * 2,
        compiler_params=pltpu.CompilerParams(
            collective_id=0, has_side_effects=True, vmem_limit_bytes=60 * 2**20),
        name="encoder",
    )(layer_input.reshape(halves), cotangent.reshape(halves), query_weight, key_weight, value_weight, proj_weight, up_weight, down_weight, query_shift,
      value_shift, proj_shift, up_shift, down_shift, first_gain, first_shift, second_gain, second_shift, segq, segk)
    own = o_vec.reshape(L, 2 * VEC_ROWS, s.dc)
    up_rows = s.fc // LANES
    vectors = own[:, VEC_ROWS:]
    return (
        o_act.reshape(s.tok, s.dc), o_in.reshape(s.tok, s.dc), *arrays, own[:, 4], own[:, 5], vectors[:, PROJ_B], own[:, :up_rows].reshape(L, s.fc), vectors[:, DOWN_B],
        vectors[:, GAIN1], vectors[:, SHIFT1], vectors[:, GAIN2], vectors[:, SHIFT2],
    )


def build(mesh, tok, d, ff):
    s = Sizes(mesh.shape["row"], mesh.shape["col"], tok, d, ff)
    return jax.shard_map(
        functools.partial(body, s),
        mesh=mesh,
        in_specs=(P("row", "col"),) + (P(None, "row", "col"),) * 6 + (P(None, "col"),) * 9 + (P(), P("row", "col")),
        out_specs=(P("row", "col"),) * 2 + (P(None, "row", "col"),) * 6 + (P(None, "col"),) * 9,
        check_vma=False,
    )


def solution(mesh):
    return build(mesh, 256, 1024, 4096)
```

time: 276 us -> 241 us (0.87)
  Pallas kernels: 260 us -> 228 us
    pallas_call x1, Pallas kernels: 260 us -> 228 us  [body(): pl.pallas_call(functools.partial(kernel, s), out_shape=out_shape, in_spec...]
where the time goes in v3:
time: 241 us
  Pallas kernels  228 us (95%)
  local copies, waits for them, and re-layouts  12 us (5%)
    pallas_call x1, Pallas kernels, body(): pl.pallas_call(functools.partial(kernel, s), out_shape=out_shape, in_spec...  228 us
    unnamed x24, local copies, waits for them, and re-layouts  8.14 us

profile of v3, /device:TPU:2, one launch (start us, length us, event | category | flops | bytes accessed | tf_op | source)
XLA Modules:
  0.0 240.7 jit_solution(12660557040736168530)
XLA Ops:
  0.7 0.0 slice-start
  0.7 0.7 slice-done
  1.3 0.1 tile.16
  1.4 0.7 tile.20.refs_18_
  2.1 0.9 tile.21.refs_17_
  3.0 228.0 %encoder.1 = (bf16[2,128,128]{2,1,0:T(8,128)(2,1)}, f32[2,128,128]{2,1,0:T(8,128)}, f32[2,64,128]{2,1,0:T(8,128)}, f32[2,64,128]{2,1,0:T(8,128)}, f32[2,64,128]{...) custom-call(bf16[2,128,128]{2,1,0:T(8,128)(2,1)} %bitcast.41, ...), custom_call_target="tpu_custom_call" | custom-call | tf_op jit(solution)/shard_map/encoder/pallas_call | solution.py:746
  231.0 0.0 copy-start.2
  231.0 0.7 slice_bitcast_fusion
  231.8 1.5 fusion
  233.3 0.6 copy.62
  233.9 1.5 copy.71
  235.3 0.0 copy-done.2
  235.3 0.0 copy-start.6
  235.3 0.0 copy-start.5
  235.3 0.0 copy-start.4
  235.3 0.7 copy.72
  236.0 0.2 copy-done.6
  236.2 0.0 copy-start.1
  236.2 0.6 copy.73
  236.8 0.0 copy-done.5
  236.8 0.6 copy.74
  237.4 0.0 copy-done.4
  237.4 0.0 copy-start.3
  237.4 0.6 copy.75
  238.1 0.2 copy-done.3
  238.3 0.6 copy.76
  238.9 0.0 copy-done.1
  238.9 0.0 copy-start
  238.9 0.7 copy.77
  239.6 0.3 copy-done
  240.0 0.7 copy.78
  (2 shorter events, 0.0 us)
Async XLA Ops:
  0.7 0.7 slice-start
  231.0 4.3 %copy-start.2 = (f32[2,128,128]{2,1,0:T(8,128)S(1)}, f32[2,128,128]{2,1,0:T(8,128)}, u32[]{:S(2)}) copy-start(f32[2,128,128]{2,1,0:T(8,128)} %get-tuple-element.27) | copy-start | bytes 393220
  235.3 0.8 copy-start.6
  235.3 1.5 copy-start.5
  235.3 2.1 copy-start.4
  236.2 2.8 %copy-start.1 = (f32[2,64,512]{2,1,0:T(8,128)S(1)}, f32[2,64,512]{2,1,0:T(8,128)}, u32[]{:S(2)}) copy-start(f32[2,64,512]{2,1,0:T(8,128)} %get-tuple-element.66) | copy-start | bytes 786436
  237.4 0.9 copy-start.3
  238.9 1.0 copy-start

commit v4 on v3

v4 whole, which is shorter than its diff:
```python
import functools
from types import SimpleNamespace

import jax
import jax.numpy as jnp
from jax import lax
from jax.experimental import pallas as pl
from jax.experimental.pallas import tpu as pltpu
from jax.sharding import PartitionSpec as P

MESH = pl.DeviceIdType.MESH
LAYERS = 2
HEAD_DIM = 64
LANES = 128
F32 = jnp.float32
BF16 = jnp.bfloat16
PAIRS = ((0, 0), (1, 1), (1, 2), (2, 1), (2, 2), (2, 3), (3, 2), (3, 3))
KEYS_OF = {i: [(n, j) for n, (a, j) in enumerate(PAIRS) if a == i] for i in range(4)}
QUERIES_OF = {j: [(n, i) for n, (i, b) in enumerate(PAIRS) if b == j] for j in range(4)}

PROJ_B, DOWN_B, GAIN1, SHIFT1, GAIN2, SHIFT2 = range(6)
VEC_ROWS = 8


def dot(a, b):
    return jnp.dot(a, b, preferred_element_type=F32)


def dot_nt(a, b):
    return lax.dot_general(a, b, (((1,), (1,)), ((), ())), preferred_element_type=F32)


def dot_tn(a, b):
    return lax.dot_general(a, b, (((0,), (0,)), ((), ())), preferred_element_type=F32)


class Sizes:
    def __init__(self, nr, nc, tok, d, ff):
        self.nr, self.nc, self.tok, self.d, self.ff = nr, nc, tok, d, ff
        self.half = tok // 2
        self.t = self.half // nc
        self.dc, self.fc = d // nc, ff // nc
        self.dr, self.fr = d // nr, ff // nr
        self.nz = nr // 4
        self.nzx = nr // 2
        self.qc = tok // 4


def scratch_of(s):
    L = LAYERS
    v = SimpleNamespace()
    v.xf = ((L, 2, s.half, s.d), BF16)
    v.x1 = ((L, 2, s.half, s.d), BF16)
    v.dff = ((L, 2, s.half, s.d), BF16)
    v.drf = ((L, 2, s.half, s.d), BF16)
    v.part = ((2, s.half, s.d), BF16)
    v.got = ((2, s.nc, s.t, s.d), BF16)
    v.got_in = ((2, s.nc, s.half, s.dc), BF16)
    v.act_out = ((2, s.t, s.d), BF16)
    v.act_in = ((2, s.half, s.dc), BF16)
    v.cot = ((2, s.t, s.d), BF16)
    v.pv = ((L * VEC_ROWS, s.d), F32)
    v.kv = ((L, s.nzx, 2, s.tok, 2 * s.dc), BF16)
    v.dkv = ((2, s.nzx, 2, s.half, 2 * s.dc), BF16)
    v.dkv_c = ((L, 2, s.nzx, s.half, 2 * s.dc), BF16)
    v.dkv_in = ((L, 2, s.nzx, s.half, 2 * s.dc), BF16)
    v.probs = ((L, len(PAIRS), 2 * s.qc, s.nr * s.qc), BF16)
    v.q2 = ((L, 4, 2 * s.qc, s.dc), BF16)
    v.do2 = ((4, 2 * s.qc, s.dc), BF16)
    v.delta = ((4, 2 * s.qc, 1), F32)
    v.dq2 = ((4, 2 * s.qc, s.dc), F32)
    v.att = ((L, s.tok, s.dc), F32)
    v.gate = ((L, 2, s.half, s.fc), BF16)
    v.slope = ((L, 2, s.half, s.fc), F32)
    v.de = ((2, s.half, s.fc), BF16)
    v.n1 = ((L, 2, s.t, s.d), F32)
    v.n2 = ((L, 2, s.t, s.d), F32)
    v.r1 = ((L, 2, s.t, 1), F32)
    v.r2 = ((L, 2, s.t, 1), F32)
    v.carry = ((2, s.t, s.d), F32)
    v.dqkv = ((s.tok, 3 * s.dc), BF16)
    v.wqkv = ((L, s.nzx, 2, s.dr, 3 * s.dc), BF16)
    v.wup = ((L, s.nzx, 2, s.dr, s.fc), BF16)
    v.wproj = ((L, s.dc, s.d), BF16)
    v.wdown = ((L, s.fc, s.d), BF16)
    v.wp_own = ((L, s.dr, s.dc), BF16)
    v.wd_own = ((L, s.fr, s.dc), BF16)
    v.gqkv = ((s.nzx, 2, s.dr, 3 * s.dc), BF16)
    v.gup = ((s.nzx, 2, s.dr, s.fc), BF16)
    v.gproj = ((s.dc, s.d), BF16)
    v.gdown = ((s.fc, s.d), BF16)
    v.gqkv_c = ((L, s.nzx, s.dr, 3 * s.dc), BF16)
    v.gup_c = ((L, s.nzx, s.dr, s.fc), BF16)
    v.gproj_c = ((L, s.dr, s.d), BF16)
    v.gdown_c = ((L, s.fr, s.d), BF16)
    v.gqkv_in = ((L, s.nzx, s.dr, 3 * s.dc), BF16)
    v.gup_in = ((L, s.nzx, s.dr, s.fc), BF16)
    v.gproj_in = ((L, s.dr, s.d), BF16)
    v.t_gq, v.t_gp = ((s.dr, 3 * s.dc), F32), ((s.dr, s.dc), F32)
    v.t_gu, v.t_gd = ((s.dr, s.fc), F32), ((s.fr, s.dc), F32)
    v.t_gq_out = v.t_gq_in = ((L, s.dr, 3 * s.dc), BF16)
    v.t_gp_out = v.t_gp_in = ((L, s.dr, s.dc), BF16)
    v.t_gu_out = v.t_gu_in = ((L, s.dr, s.fc), BF16)
    v.t_gd_out = v.t_gd_in = ((L, s.fr, s.dc), BF16)
    v.gdown_in = ((L, s.fr, s.d), BF16)
    v.gproj_out = ((L, s.dr, s.dc), BF16)
    v.gdown_out = ((L, s.fr, s.dc), BF16)
    v.gproj_fin = ((L, s.dr, s.dc), BF16)
    v.gdown_fin = ((L, s.fr, s.dc), BF16)
    v.vec = ((L * VEC_ROWS, s.d), F32)
    v.vec_in = ((s.nc, L * VEC_ROWS, s.dc), F32)
    v.segq = ((4, 2 * s.qc, 1), jnp.int32)
    v.segk = ((4, s.nr * s.qc), jnp.int32)
    v.own = ((L * 2 * VEC_ROWS, s.dc), F32)
    v.own_in = ((s.nr, L * 2 * VEC_ROWS, s.dc), F32)
    return vars(v)


INPUTS = tuple(dict(x=0, cotan=0, wq=0, wk=0, wv=0, wp=0, wu=0, wd=0, qb=0, vb=0, pb=0, upb=0, db=0, g1=0, s1=0, g2=0, s2=0,
                    places=0))
OUTPUTS = tuple(dict(o_act=0, o_in=0, o_q=0, o_k=0, o_v=0, o_proj=0, o_up=0, o_down=0, o_vec=0))

(X_IN, COTAN, PVEC, ACT, VEC, OWN, WPT, WDT, GPT, GDT, PR, N1, FR, H, DF, DN, DR, DX,
 WQ, WP, WU, WD, KVA, KVB, DKVA, DKVB, GQ, GP, GU, GD) = range(30)
CORE, ACROSS = 1, 2
IN_STEPS = {(n, l) for n in (WP, WU, WD, KVA, KVB, GP, GU, GD) for l in range(LAYERS)} | {(WQ, 1), (GQ, 1)}
KV = {KVA: 0, KVB: 1}
DKV = {DKVA: 0, DKVB: 1}
KEYS = (
    [(n, 0, 0) for n in range(X_IN, GPT)]
    + [(n, l, 0) for n in range(GPT, PR) for l in range(LAYERS)]
    + [(n, l, a) for n in range(PR, WQ) for l in range(LAYERS) for a in range(2)]
    + [(n, l, step) for n in range(WQ, GD + 1) for l in range(LAYERS) for step in range(3)]
)
PHASE = {key: index for index, key in enumerate(KEYS)}


def kernel(s, *refs):
    names = INPUTS + OUTPUTS + tuple(scratch_of(s)) + ("send", "recv")
    m = SimpleNamespace(**dict(zip(names, refs)))
    L = LAYERS
    r, c = lax.axis_index("row"), lax.axis_index("col")
    zx, k = lax.div(r, 2), lax.rem(r, 2)
    z, x = lax.div(zx, 2), lax.rem(zx, 2)
    across = z * 2 + 1 - x
    other = zx * 2 + 1 - k
    at_home = zx == c
    chips, few = s.nzx - 1, s.nc - 1

    def remote(src, dst, phase, row, col):
        return pltpu.make_async_remote_copy(
            src_ref=src, dst_ref=dst, send_sem=m.send.at[PHASE[phase]], recv_sem=m.recv.at[PHASE[phase]],
            device_id=(row, col), device_id_type=MESH)

    def wait(sems, phase, ref):
        pltpu.make_async_copy(ref, ref, sems.at[PHASE[phase]]).wait()

    def each_col(fn):
        def step(q, carry):
            fn(lax.rem(c + q, s.nc))
            return carry
        lax.fori_loop(1, s.nc, step, 0)

    def each_row(fn):
        def step(q, carry):
            fn(lax.rem(r + q, s.nr))
            return carry
        lax.fori_loop(1, s.nr, step, 0)

    def each_chip(fn):
        def step(q, carry):
            fn(lax.rem(zx + q, s.nzx))
            return carry
        lax.fori_loop(1, s.nzx, step, 0)

    def each_z(fn):
        def step(q, carry):
            fn(lax.rem(z + q, s.nz))
            return carry
        lax.fori_loop(1, s.nz, step, 0)

    def rows(i, n):
        return pl.ds(pl.multiple_of(i * n, n), n)

    barrier = pltpu.get_barrier_semaphore()

    def greet(row, col):
        pl.semaphore_signal(barrier, inc=1, device_id=(row, col), device_id_type=MESH)

    swap_row, swap_col = c * 2 + k, zx
    each_col(lambda cc: greet(r, cc))
    each_row(lambda rr: greet(rr, c))

    @pl.when(jnp.logical_not(at_home))
    def _():
        greet(swap_row, swap_col)

    def weight(name, l):
        chips = s.nzx - (2 if (name, l) in IN_STEPS else 1)
        if name in KV:
            span = pl.ds(KV[name] * s.half, s.half)
            return ((lambda i, kk: m.kv.at[l, i, kk, span]), (lambda kk: m.kv.at[l, :, kk, span]),
                    m.kv.at[l, pl.ds(0, chips), 0, span] if chips else None)
        if name in (WQ, WU):
            ref = {WQ: m.wqkv, WU: m.wup}[name]
            return (lambda i, kk: ref.at[l, i, kk]), (lambda kk: ref.at[l, :, kk]), \
                ref.at[l, pl.ds(0, chips), 0] if chips else None
        ref, n = {WP: (m.wproj, s.dr), WD: (m.wdown, s.fr)}[name]
        return ((lambda i, kk: ref.at[l, rows(kk, n), rows(i, s.dc)]), (lambda kk: ref.at[l, rows(kk, n)]),
                ref.at[l, pl.ds(0, n), pl.ds(0, chips * s.dc)] if chips else None)

    def gather(name, l):
        piece = weight(name, l)[0](zx, k)
        if (name, l) not in IN_STEPS:
            each_chip(lambda i: remote(piece, piece, (name, l, 0), i * 2 + k, c).start())
            return
        remote(piece, piece, (name, l, ACROSS), across * 2 + k, c).start()
        each_z(lambda i: remote(piece, piece, (name, l, 0), (i * 2 + x) * 2 + k, c).start())

    def forward(name, l):
        piece = weight(name, l)[0](across, k)
        wait(m.recv, (name, l, ACROSS), piece)
        each_z(lambda i: remote(piece, piece, (name, l, 0), (i * 2 + x) * 2 + k, c).start())

    def pass_on(name, l):
        _, half, many = weight(name, l)
        if many is not None:
            wait(m.recv, (name, l, 0), many)
        remote(half(k), half(k), (name, l, CORE), other, c).start()

    def gathered(name, l):
        wait(m.recv, (name, l, CORE), weight(name, l)[1](1 - k))

    def sent_gather(name, l):
        piece, half, many = weight(name, l)
        if many is not None:
            wait(m.send, (name, l, 0), many)
        if (name, l) in IN_STEPS:
            wait(m.send, (name, l, ACROSS), piece(zx, k))
        wait(m.send, (name, l, CORE), half(k))

    def partial_sum(name, l):
        if name in DKV:
            a = DKV[name]
            mid, got = m.dkv_c.at[l, a], m.dkv_in.at[l, a]
            return (lambda kk: m.dkv.at[a, :, kk]), mid, (lambda i: mid.at[i]), got
        if name in (GQ, GU):
            full, mid, got = {GQ: (m.gqkv, m.gqkv_c.at[l], m.gqkv_in.at[l]),
                              GU: (m.gup, m.gup_c.at[l], m.gup_in.at[l])}[name]
            return (lambda kk: full.at[:, kk]), mid, (lambda i: mid.at[i]), got
        full, mid, got, n = {GP: (m.gproj, m.gproj_c.at[l], m.gproj_in.at[l], s.dr),
                             GD: (m.gdown, m.gdown_c.at[l], m.gdown_in.at[l], s.fr)}[name]
        return (lambda kk: full.at[rows(kk, n)]), mid, (lambda i: mid.at[:, rows(i, s.dc)]), got

    def reduce_start(name, l):
        half, mid, _, _ = partial_sum(name, l)
        remote(half(1 - k), mid, (name, l, CORE), other, c).start()

    def both(name, mid, i):
        if name in (GP, GD):
            return mid.at[:, rows(i, 2 * s.dc)]
        return mid.at[pl.ds(2 * i, 2)]

    def m_pair(name, got, i):
        if name in (GP, GD):
            return got.at[:, rows(i, 2 * s.dc)]
        return got.at[pl.ds(2 * i, 2)]

    def reduce_turn(name, l):
        _, mid, piece, got = partial_sum(name, l)
        if s.nz > 1:
            wait(m.recv, (name, l, 0), m_all(name, got))
        sums = []
        for which in (x, 1 - x):
            total = piece(z * 2 + which)[...].astype(F32)
            for q in range(1, s.nz):
                i = lax.rem(z + q, s.nz) * 2 + which
                arrived = got[:, rows(i, s.dc)] if name in (GP, GD) else got[i]
                total = total + arrived.astype(F32)
            sums.append(total)
        kept, out, back = turned(name, l)
        kept[...] = sums[0]
        out[...] = sums[1].astype(BF16)
        remote(out, back, (name, l, ACROSS), across * 2 + k, c).start()

    def turned(name, l):
        return {GQ: (m.t_gq, m.t_gq_out.at[l], m.t_gq_in.at[l]), GP: (m.t_gp, m.t_gp_out.at[l], m.t_gp_in.at[l]),
                GU: (m.t_gu, m.t_gu_out.at[l], m.t_gu_in.at[l]), GD: (m.t_gd, m.t_gd_out.at[l], m.t_gd_in.at[l])}[name]

    def m_all(name, got):
        if name in (GP, GD):
            return got.at[:, pl.ds(0, 2 * (s.nz - 1) * s.dc)]
        return got.at[pl.ds(0, 2 * (s.nz - 1))]

    def reduce_mid(name, l):
        half, mid, piece, got = partial_sum(name, l)
        wait(m.recv, (name, l, CORE), mid)
        mid[...] = (half(k)[...].astype(F32) + mid[...].astype(F32)).astype(BF16)
        if (name, l) in IN_STEPS:
            each_z(lambda i: remote(both(name, mid, i), m_pair(name, got, z), (name, l, 0), (i * 2 + x) * 2 + k, c).start())
            return
        each_chip(lambda i: remote(piece(i), got.at[zx], (name, l, 0), i * 2 + k, c).start())
        got[zx] = piece(zx)[...]

    def reduce_end(name, l):
        if (name, l) in IN_STEPS:
            kept, _, back = turned(name, l)
            wait(m.recv, (name, l, ACROSS), back)
            return kept[...] + back[...].astype(F32)
        got = partial_sum(name, l)[3]
        wait(m.recv, (name, l, 0), got.at[pl.ds(0, chips)])
        total = got[0].astype(F32)
        for i in range(1, s.nzx):
            total = total + got[i].astype(F32)
        return total

    def sent_half(name, l):
        wait(m.send, (name, l, CORE), partial_sum(name, l)[1])

    def sent_pieces(name, l):
        if (name, l) in IN_STEPS:
            if s.nz > 1:
                wait(m.send, (name, l, 0), m_all(name, partial_sum(name, l)[3]))
            wait(m.send, (name, l, ACROSS), turned(name, l)[1])
            return
        wait(m.send, (name, l, 0), partial_sum(name, l)[3].at[pl.ds(0, chips)])

    m.xf[0, :, :, rows(c, s.dc)] = m.x[...]
    m.cot[:, :, rows(c, s.dc)] = m.cotan[:, rows(c, s.t), :]
    m.pv[:, rows(c, s.dc)] = jnp.zeros((L * VEC_ROWS, s.dc), F32)
    for l in range(L):
        for which, ref in enumerate((m.pb, m.db, m.g1, m.s1, m.g2, m.s2)):
            m.pv[l * VEC_ROWS + which : l * VEC_ROWS + which + 1, rows(c, s.dc)] = ref[l : l + 1, :].astype(F32)
        for which, ref in enumerate((m.wq, m.wk, m.wv)):
            m.wqkv[l, zx, k, :, which * s.dc : (which + 1) * s.dc] = ref[l]
        m.wup[l, zx, k] = m.wu[l]

    pl.semaphore_wait(barrier, s.nc - 1 + s.nr - 1 + 1 - at_home.astype(jnp.int32))

    gather(WQ, 0)
    each_col(lambda cc: remote(m.x, m.xf.at[0, :, :, rows(c, s.dc)], (X_IN, 0, 0), r, cc).start())

    @pl.when(jnp.logical_not(at_home))
    def _():
        remote(m.wp, m.wp_own, (WPT, 0, 0), swap_row, swap_col).start()
        remote(m.wd, m.wd_own, (WDT, 0, 0), swap_row, swap_col).start()
    mine = m.pv.at[:, rows(c, s.dc)]
    each_col(lambda cc: remote(mine, mine, (PVEC, 0, 0), r, cc).start())
    each_col(lambda cc: remote(
        m.cotan.at[:, rows(cc, s.t)], m.cot.at[:, :, rows(c, s.dc)], (COTAN, 0, 0), r, cc).start())
    square = (s.qc, s.qc)
    diagonal = lax.broadcasted_iota(jnp.int32, square, 0) == lax.broadcasted_iota(jnp.int32, square, 1)
    for i in range(4):
        numbers = m.places[i : i + 1, :]
        column = jnp.sum(jnp.where(diagonal, numbers[:, : s.qc], 0), axis=1, keepdims=True)
        m.segq[i] = jnp.concatenate([column, column], axis=0)
        m.segk[i : i + 1, :] = jnp.concatenate([numbers] * (s.nr * s.qc // numbers.shape[1]), axis=1)
    m.vec[...] = jnp.zeros(m.vec.shape, F32)
    m.own[...] = jnp.zeros(m.own.shape, F32)

    def vector(l, which):
        return m.pv[l * VEC_ROWS + which : l * VEC_ROWS + which + 1, :]

    def share(buf, value, phase):
        buf[rows(c, s.t), :] = value
        each_col(lambda cc: remote(buf.at[rows(c, s.t)], buf.at[rows(c, s.t)], phase, r, cc).start())

    def shared(buf, phase):
        for sems in (m.recv, m.send):
            wait(sems, phase, buf.at[pl.ds(0, few * s.t)])

    def scatter(a, value, phase):
        m.part[a] = value.astype(BF16)
        each_col(lambda cc: remote(m.part.at[a, rows(cc, s.t)], m.got.at[a, c], phase, r, cc).start())
        m.got[a, c] = m.part[a, rows(c, s.t), :]

    def scattered(a, phase):
        for sems in (m.recv, m.send):
            wait(sems, phase, m.got.at[a, pl.ds(0, few)])
        total = m.got[a, 0].astype(F32)
        for i in range(1, s.nc):
            total = total + m.got[a, i].astype(F32)
        return total

    def norm(u, l, a, gain, shift, n_ref, r_ref):
        mean = jnp.sum(u, axis=1, keepdims=True) / s.d
        var = jnp.sum(u * u, axis=1, keepdims=True) / s.d - mean * mean
        inv = lax.rsqrt(var + 1e-12)
        n = (u - mean) * inv
        n_ref[l, a] = n
        r_ref[l, a] = inv
        return n * vector(l, gain) + vector(l, shift)

    def add_row(ref, at, value):
        ref[at : at + 1, :] += jnp.sum(value, axis=0, keepdims=True)

    def norm_back(g, l, a, gain, shift, n_ref, r_ref):
        n = n_ref[l, a]
        w = g * vector(l, gain)
        first = jnp.sum(w, axis=1, keepdims=True) / s.d
        second = jnp.sum(w * n, axis=1, keepdims=True) / s.d
        add_row(m.vec, l * VEC_ROWS + gain, g * n)
        add_row(m.vec, l * VEC_ROWS + shift, g)
        return r_ref[l, a] * (w - first - n * second)

    low_lanes = lax.broadcasted_iota(jnp.int32, (s.qc, s.dc), 1) < HEAD_DIM

    def two_heads(block):
        block = block.astype(F32)
        return jnp.concatenate([jnp.where(low_lanes, block, 0.0), jnp.where(low_lanes, 0.0, block)], axis=0)

    def one_block(pair):
        return jnp.where(low_lanes, pair[: s.qc], pair[s.qc :])

    def keys(l, j, value):
        lanes = pl.ds(s.dc if value else 0, s.dc)
        return m.kv[l, :, :, pl.ds(j * s.qc, s.qc), lanes].reshape(s.nr * s.qc, s.dc)

    def swapped(l):
        m.wproj[l, rows(k, s.dr), rows(zx, s.dc)] = m.wp_own[l]
        m.wdown[l, rows(k, s.fr), rows(zx, s.dc)] = m.wd_own[l]

    pass_on(WQ, 0)
    wait(m.recv, (X_IN, 0, 0), m.xf.at[0, :, :, pl.ds(0, few * s.dc)])
    wait(m.recv, (PVEC, 0, 0), m.pv.at[:, pl.ds(0, few * s.dc)])

    @pl.when(at_home)
    def _():
        m.wp_own[...] = m.wp[...]
        m.wd_own[...] = m.wd[...]

    @pl.when(jnp.logical_not(at_home))
    def _():
        wait(m.recv, (WPT, 0, 0), m.wp_own)
        wait(m.recv, (WDT, 0, 0), m.wd_own)
    swapped(0)

    def attend(l, i):
        queries = m.q2[l, i]
        ids = m.segq[i]
        scores = []
        for _, j in KEYS_OF[i]:
            raw = dot_nt(queries, keys(l, j, False))
            scores.append(jnp.where(ids == m.segk[j : j + 1, :], raw, -1e9))
        top = functools.reduce(jnp.maximum, [jnp.max(x, axis=1, keepdims=True) for x in scores])
        raised = [jnp.exp(x - top) for x in scores]
        inverse = 1.0 / sum(jnp.sum(x, axis=1, keepdims=True) for x in raised)
        out = jnp.zeros((2 * s.qc, s.dc), F32)
        for (n, j), x in zip(KEYS_OF[i], raised):
            prob = (x * inverse).astype(BF16)
            m.probs[l, n] = prob
            out = out + dot(prob, keys(l, j, True))
        m.att[l, i * s.qc : (i + 1) * s.qc, :] = one_block(out)

    def span(a):
        return pl.ds(a * s.half, s.half)

    for l in range(L):
        for a in range(2):
            if l:
                shared(m.xf.at[l, a], (H, l - 1, a))
            elif a == 0:
                gathered(WQ, 0)
                for b in range(2):
                    m.carry[b] = m.xf[0, b, rows(c, s.t), :].astype(F32)
            if l and a == 0:
                gathered(WQ, l)
            qkv = dot(m.xf[l, a], m.wqkv[l].reshape(s.d, 3 * s.dc))
            keep = (qkv[:, 2 * s.dc :] + m.vb[l : l + 1, :].astype(F32)).astype(BF16)
            m.kv[l, zx, k, span(a), : s.dc] = qkv[:, s.dc : 2 * s.dc].astype(BF16)
            m.kv[l, zx, k, span(a), s.dc :] = keep
            gather(KVA if a == 0 else KVB, l)
            for i in range(2):
                block = (qkv[i * s.qc : (i + 1) * s.qc, : s.dc] + m.qb[l : l + 1, :].astype(F32)).astype(BF16)
                m.q2[l, 2 * a + i] = (two_heads(block) * HEAD_DIM ** (-0.5)).astype(BF16)
        if l == 0:
            gather(WP, 0)
        if l == 0:
            forward(WP, 0)
        forward(KVA, l)
        forward(KVB, l)
        pass_on(KVA, l)
        pass_on(KVB, l)
        if l == 0:
            gather(WU, 0)
            gather(WD, 0)
            pass_on(WP, 0)
        else:
            pass_on(WU, 1)
            pass_on(WD, 1)
        gathered(KVA, l)
        attend(l, 0)
        gathered(KVB, l)
        attend(l, 1)
        gathered(WP, l)
        scatter(0, dot(m.att[l, span(0), :].astype(BF16), m.wproj[l]), (PR, l, 0))
        attend(l, 2)
        attend(l, 3)
        scatter(1, dot(m.att[l, span(1), :].astype(BF16), m.wproj[l]), (PR, l, 1))
        if l == 0:
            forward(WU, 0)
            forward(WD, 0)
            swapped(1)
        for a in range(2):
            u = scattered(a, (PR, l, a)) + vector(l, PROJ_B) + m.carry[a]
            first_out = norm(u, l, a, GAIN1, SHIFT1, m.n1, m.r1)
            share(m.x1.at[l, a], first_out.astype(BF16), (N1, l, a))
            m.carry[a] = first_out
        if l == 0:
            pass_on(WU, 0)
            pass_on(WD, 0)
            gather(WQ, 1)
            gather(WP, 1)
        gathered(WU, l)
        for a in range(2):
            shared(m.x1.at[l, a], (N1, l, a))
            pre = dot(m.x1[l, a], m.wup[l].reshape(s.d, s.fc)) + m.upb[l : l + 1, :].astype(F32)
            cdf = 0.5 * (1.0 + lax.erf(pre * 0.5**0.5))
            m.gate[l, a] = (pre * cdf).astype(BF16)
            if a == 0:
                gathered(WD, l)
            scatter(a, dot(m.gate[l, a], m.wdown[l]), (FR, l, a))
            m.slope[l, a] = cdf + pre * (jnp.exp(-0.5 * pre * pre) * 0.3989422804014327)
        if l == 0:
            forward(WQ, 1)
            forward(WP, 1)
            gather(WU, 1)
            gather(WD, 1)
        for a in range(2):
            u = scattered(a, (FR, l, a)) + vector(l, DOWN_B) + m.carry[a]
            hidden = norm(u, l, a, GAIN2, SHIFT2, m.n2, m.r2)
            if l == 0:
                share(m.xf.at[1, a], hidden.astype(BF16), (H, 0, a))
                m.carry[a] = hidden
            else:
                m.act_out[a] = hidden.astype(BF16)
        if l == 0:
            pass_on(WQ, 1)
            pass_on(WP, 1)
            forward(WU, 1)
            forward(WD, 1)

    def swap_back(l, name, total):
        out, fin, phase = {GP: (m.gproj_out, m.gproj_fin, (GPT, l, 0)), GD: (m.gdown_out, m.gdown_fin, (GDT, l, 0))}[name]
        out[l] = total.astype(BF16)

        @pl.when(jnp.logical_not(at_home))
        def _():
            remote(out.at[l], fin.at[l], phase, swap_row, swap_col).start()

        @pl.when(at_home)
        def _():
            fin[l] = out[l]

    def swap_end(l, name, out):
        fin, phase = {GP: (m.gproj_fin, (GPT, l, 0)), GD: (m.gdown_fin, (GDT, l, 0))}[name]

        @pl.when(jnp.logical_not(at_home))
        def _():
            wait(m.recv, phase, fin.at[l])
        out[l] = fin[l].astype(F32)

    def attend_back(l, j):
        key_grad = jnp.zeros((s.nr * s.qc, s.dc), F32)
        value_grad = jnp.zeros((s.nr * s.qc, s.dc), F32)
        for n, i in QUERIES_OF[j]:
            prob = m.probs[l, n]
            prob_grad = dot_nt(m.do2[i], keys(l, j, True))
            score_grad = (prob.astype(F32) * (prob_grad - m.delta[i])).astype(BF16)
            m.dq2[i] += dot(score_grad, keys(l, j, False))
            key_grad = key_grad + dot_tn(score_grad, m.q2[l, i])
            value_grad = value_grad + dot_tn(prob, m.do2[i])
        shape = (s.nzx, 2, s.qc, s.dc)
        place = pl.ds(j % 2 * s.qc, s.qc)
        m.dkv[j // 2, :, :, place, pl.ds(0, s.dc)] = key_grad.astype(BF16).reshape(shape)
        m.dkv[j // 2, :, :, place, pl.ds(s.dc, s.dc)] = value_grad.astype(BF16).reshape(shape)

    wait(m.recv, (COTAN, 0, 0), m.cot.at[:, :, pl.ds(0, few * s.dc)])
    for l in reversed(range(L)):
        at = l * VEC_ROWS
        own = l * 2 * VEC_ROWS
        for a in range(2):
            if l + 1 < L:
                grad = scattered(a, (DX, l + 1, a)) + m.carry[a]
            else:
                grad = m.cot[a].astype(F32)
            dz = norm_back(grad, l, a, GAIN2, SHIFT2, m.n2, m.r2)
            m.carry[a] = dz
            low = dz.astype(BF16)
            share(m.dff.at[l, a], low, (DF, l, a))
            add_row(m.vec, at + DOWN_B, low.astype(F32))
        if l + 1 == L:
            each_col(lambda cc: remote(
                m.act_out.at[:, :, rows(cc, s.dc)], m.act_in.at[:, rows(c, s.t)], (ACT, 0, 0), r, cc).start())
            m.act_in[:, rows(c, s.t), :] = m.act_out[:, :, rows(c, s.dc)]
        else:
            reduce_mid(GQ, l + 1)
            reduce_turn(GP, l + 1)
        for a in range(2):
            shared(m.dff.at[l, a], (DF, l, a))
            de = (dot_nt(m.dff[l, a], m.wdown[l]) * m.slope[l, a]).astype(BF16)
            m.de[a] = de
            scatter(a, dot_nt(de, m.wup[l].reshape(s.d, s.fc)), (DN, l, a))
            sums = jnp.sum(de.astype(F32), axis=0, keepdims=True)
            for i in range(s.fc // LANES):
                m.own[own + i : own + i + 1, :] += sums[:, i * LANES : (i + 1) * LANES]
        if l + 1 < L:
            reduce_turn(GQ, l + 1)
            swap_back(l + 1, GP, reduce_end(GP, l + 1))
            sent_half(GD, l + 1)
            sent_half(GU, l + 1)
        m.gdown[...] = dot_tn(m.gate[l].reshape(s.tok, s.fc), m.dff[l].reshape(s.tok, s.d)).astype(BF16)
        reduce_start(GD, l)
        for a in range(2):
            grad = scattered(a, (DN, l, a)) + m.carry[a]
            du = norm_back(grad, l, a, GAIN1, SHIFT1, m.n1, m.r1)
            m.carry[a] = du
            low = du.astype(BF16)
            share(m.drf.at[l, a], low, (DR, l, a))
            add_row(m.vec, at + PROJ_B, low.astype(F32))
        m.gup[...] = dot_tn(m.x1[l].reshape(s.tok, s.d), m.de[...].reshape(s.tok, s.fc)).astype(BF16).reshape(m.gup.shape)
        reduce_start(GU, l)
        reduce_mid(GD, l)
        if l == 0:
            each_col(lambda cc: remote(m.vec.at[:, rows(cc, s.dc)], m.vec_in.at[c], (VEC, 0, 0), r, cc).start())
            m.vec_in[c] = m.vec[:, rows(c, s.dc)]
        if l + 1 < L:
            sent_half(DKVA, l + 1)
            sent_half(DKVB, l + 1)
        for a in range(2):
            shared(m.drf.at[l, a], (DR, l, a))
            dout = dot_nt(m.drf[l, a], m.wproj[l]).astype(BF16)
            for b in range(2):
                i = 2 * a + b
                block = two_heads(dout[b * s.qc : (b + 1) * s.qc, :])
                kept = m.att[l, i * s.qc : (i + 1) * s.qc, :]
                m.do2[i] = block.astype(BF16)
                m.delta[i] = jnp.sum(block * jnp.concatenate([kept, kept], axis=0), axis=1, keepdims=True)
                m.dq2[i] = jnp.zeros((2 * s.qc, s.dc), F32)
            if a == 0:
                attend_back(l, 0)
                reduce_mid(GU, l)
        attend_back(l, 1)
        reduce_start(DKVA, l)
        attend_back(l, 2)
        reduce_mid(DKVA, l)
        attend_back(l, 3)
        reduce_start(DKVB, l)
        for i in range(4):
            m.dqkv[i * s.qc : (i + 1) * s.qc, : s.dc] = (one_block(m.dq2[i]) * HEAD_DIM ** (-0.5)).astype(BF16)
        reduce_mid(DKVB, l)
        reduce_turn(GD, l)
        if l + 1 < L:
            sent_half(GP, l + 1)
            sent_half(GQ, l + 1)
        m.gproj[...] = dot_tn(m.att[l].astype(BF16), m.drf[l].reshape(s.tok, s.d)).astype(BF16)
        reduce_start(GP, l)
        reduce_turn(GU, l)
        if l == 0:
            wait(m.recv, (VEC, 0, 0), m.vec_in.at[pl.ds(0, few)])
            total = m.vec_in[0]
            for i in range(1, s.nc):
                total = total + m.vec_in[i]
            for i in range(L):
                to = i * 2 * VEC_ROWS + VEC_ROWS
                m.own[to : to + VEC_ROWS, :] = total[i * VEC_ROWS : (i + 1) * VEC_ROWS]
        for a in range(2):
            m.dqkv[span(a), s.dc :] = reduce_end(DKVA if a == 0 else DKVB, l).astype(BF16)
            back = dot_nt(m.dqkv[span(a), :], m.wqkv[l].reshape(s.d, 3 * s.dc))
            if l:
                scatter(a, back, (DX, l, a))
            else:
                m.part[a] = back.astype(BF16)
                mine = m.part[a, rows(c, s.t), :].astype(F32) + m.carry[a]
                m.part[a, rows(c, s.t), :] = mine.astype(BF16)
                each_col(lambda cc: remote(m.part.at[a, :, rows(cc, s.dc)], m.got_in.at[a, c], (DX, 0, a), r, cc).start())
                m.got_in[a, c] = m.part[a, :, rows(c, s.dc)]
        m.gqkv[...] = dot_tn(m.xf[l].reshape(s.tok, s.d), m.dqkv[...]).astype(BF16).reshape(m.gqkv.shape)
        reduce_start(GQ, l)
        sums = jnp.sum(m.dqkv[...].astype(F32), axis=0, keepdims=True)
        m.own[own + 4 : own + 5, :] = sums[:, : s.dc]
        m.own[own + 5 : own + 6, :] = sums[:, 2 * s.dc :]
        reduce_mid(GP, l)
        swap_back(l, GD, reduce_end(GD, l))
        m.o_up[l] = reduce_end(GU, l)
        if l + 1 < L:
            swap_end(l + 1, GD, m.o_down)
            swap_end(l + 1, GP, m.o_proj)
            total = reduce_end(GQ, l + 1)
            for which, out in enumerate((m.o_q, m.o_k, m.o_v)):
                out[l + 1] = total[:, which * s.dc : (which + 1) * s.dc]

    m.own_in[r] = m.own[...]
    each_row(lambda rr: remote(m.own, m.own_in.at[r], (OWN, 0, 0), rr, c).start())
    reduce_mid(GQ, 0)
    reduce_turn(GP, 0)
    swap_end(0, GD, m.o_down)
    wait(m.recv, (ACT, 0, 0), m.act_in.at[:, pl.ds(0, few * s.t)])
    m.o_act[...] = m.act_in[...]
    for a in range(2):
        wait(m.recv, (DX, 0, a), m.got_in.at[a, pl.ds(0, few)])
        total = m.got_in[a, 0].astype(F32)
        for i in range(1, s.nc):
            total = total + m.got_in[a, i].astype(F32)
        m.o_in[a] = total
    swap_back(0, GP, reduce_end(GP, 0))
    wait(m.recv, (OWN, 0, 0), m.own_in.at[pl.ds(0, s.nr - 1)])
    total = m.own_in[0]
    for i in range(1, s.nr):
        total = total + m.own_in[i]
    m.o_vec[...] = total
    total = reduce_end(GQ, 0)
    for which, out in enumerate((m.o_q, m.o_k, m.o_v)):
        out[0] = total[:, which * s.dc : (which + 1) * s.dc]
    swap_end(0, GP, m.o_proj)

    wait(m.send, (X_IN, 0, 0), m.xf.at[0, :, :, pl.ds(0, few * s.dc)])
    wait(m.send, (PVEC, 0, 0), m.pv.at[:, pl.ds(0, few * s.dc)])
    wait(m.send, (COTAN, 0, 0), m.cot.at[:, :, pl.ds(0, few * s.dc)])
    wait(m.send, (ACT, 0, 0), m.act_in.at[:, pl.ds(0, few * s.t)])
    for a in range(2):
        wait(m.send, (DX, 0, a), m.got_in.at[a, pl.ds(0, few)])
    wait(m.send, (VEC, 0, 0), m.vec_in.at[pl.ds(0, few)])
    wait(m.send, (OWN, 0, 0), m.own_in.at[pl.ds(0, s.nr - 1)])

    @pl.when(jnp.logical_not(at_home))
    def _():
        wait(m.send, (WPT, 0, 0), m.wp_own)
        wait(m.send, (WDT, 0, 0), m.wd_own)
        for l in range(L):
            wait(m.send, (GPT, l, 0), m.gproj_fin.at[l])
            wait(m.send, (GDT, l, 0), m.gdown_fin.at[l])
    for l in range(L):
        for name in (WQ, WP, WU, WD, KVA, KVB):
            sent_gather(name, l)
        for name in (GQ, GP, GU, GD, DKVA, DKVB):
            sent_pieces(name, l)
    for name in (GQ, GP, GU, GD, DKVA, DKVB):
        sent_half(name, 0)


def body(s, layer_input, query_weight, key_weight, value_weight, proj_weight, up_weight, down_weight, query_shift,
         value_shift, proj_shift, up_shift, down_shift, first_gain, first_shift, second_gain, second_shift, segment_ids,
         cotangent):
    L = LAYERS
    places = jnp.tile(segment_ids[: s.tok].reshape(4, s.qc), (1, LANES // s.qc))
    shapes = scratch_of(s)
    halves = (2, s.half, s.dc)
    square = jax.ShapeDtypeStruct((L, s.dr, s.dc), F32)
    out_shape = (
        jax.ShapeDtypeStruct((2, s.half, s.dc), BF16),
        jax.ShapeDtypeStruct((2, s.half, s.dc), F32),
        square, square, square, square,
        jax.ShapeDtypeStruct((L, s.dr, s.fc), F32),
        jax.ShapeDtypeStruct((L, s.fr, s.dc), F32),
        jax.ShapeDtypeStruct((L * 2 * VEC_ROWS, s.dc), F32),
    )
    vmem = pl.BlockSpec(memory_space=pltpu.VMEM)
    results = pl.pallas_call(
        functools.partial(kernel, s),
        out_shape=out_shape,
        in_specs=[vmem] * len(INPUTS),
        out_specs=[vmem] * len(OUTPUTS),
        scratch_shapes=[pltpu.VMEM(shape, dtype) for shape, dtype in shapes.values()]
        + [pltpu.SemaphoreType.DMA((len(KEYS),))] * 2,
        compiler_params=pltpu.CompilerParams(
            collective_id=0, has_side_effects=True, vmem_limit_bytes=60 * 2**20),
        name="encoder",
    )(layer_input.reshape(halves), cotangent.reshape(halves), query_weight, key_weight, value_weight, proj_weight, up_weight,
      down_weight, query_shift, value_shift, proj_shift, up_shift, down_shift, first_gain, first_shift, second_gain,
      second_shift, places)
    narrow, wide = jax.ShapeDtypeStruct((L, s.dc), F32), jax.ShapeDtypeStruct((L, s.fc), F32)
    o_act, o_in, *others = pl.pallas_call(
        functools.partial(hand_out, s),
        out_shape=out_shape[:-1] + (narrow,) * 3 + (wide,) + (narrow,) * 5,
        in_specs=[vmem] * len(OUTPUTS),
        out_specs=[vmem] * 17,
        name="results",
    )(*results)
    return (o_act.reshape(s.tok, s.dc), o_in.reshape(s.tok, s.dc), *others)


def hand_out(s, *refs):
    count = len(OUTPUTS)
    arrays, packed, outs = refs[: count - 1], refs[count - 1], refs[count:]
    for array, out in zip(arrays, outs):
        out[...] = array[...]
    qs, vs, ps, us, ds, fg, fs, sg, ss = outs[count - 1 :]
    for l in range(LAYERS):
        own = l * 2 * VEC_ROWS
        rows = [(qs, 4), (vs, 5)]
        rows += [(ref, VEC_ROWS + which) for ref, which in
                 ((ps, PROJ_B), (ds, DOWN_B), (fg, GAIN1), (fs, SHIFT1), (sg, GAIN2), (ss, SHIFT2))]
        for ref, at in rows:
            ref[l : l + 1, :] = packed[own + at : own + at + 1, :]
        for i in range(s.fc // LANES):
            us[l : l + 1, i * LANES : (i + 1) * LANES] = packed[own + i : own + i + 1, :]


def build(mesh, tok, d, ff):
    s = Sizes(mesh.shape["row"], mesh.shape["col"], tok, d, ff)
    return jax.shard_map(
        functools.partial(body, s),
        mesh=mesh,
        in_specs=(P("row", "col"),) + (P(None, "row", "col"),) * 6 + (P(None, "col"),) * 9 + (P(), P("row", "col")),
        out_specs=(P("row", "col"),) * 2 + (P(None, "row", "col"),) * 6 + (P(None, "col"),) * 9,
        check_vma=False,
    )


def solution(mesh):
    return build(mesh, 256, 1024, 4096)
```

time: 241 us -> 229 us (0.950); the launches traced: 241 us -> 226 us
  local copies, waits for them, and re-layouts: 12 us -> 1.42 us
  Pallas kernels: 228 us -> 224 us
    unnamed x24 -> x0, local copies, waits for them, and re-layouts: 8.14 us -> none
    pallas_call x1, Pallas kernels: 228 us -> 221 us  [body(): pl.pallas_call(functools.partial(kernel, s), out_shape=out_shape, in_spec...]
where the time goes in v4:
time: 229 us; the launch traced here: 226 us
  Pallas kernels  224 us (98%)
    pallas_call x1, Pallas kernels, body(): pl.pallas_call(functools.partial(kernel, s), out_shape=out_shape, in_spec...  221 us

profile of v4, /device:TPU:2, one launch (start us, length us, event | category | flops | bytes accessed | tf_op | source)
XLA Modules:
  0.0 225.8 jit_solution(6897601010852394133)
XLA Ops:
  0.7 0.0 slice-start
  0.7 0.7 slice-done
  1.3 0.1 tile.10
  1.4 0.7 tile.12.refs_17_
  2.1 221.3 %encoder.1 = (bf16[2,128,128]{2,1,0:T(8,128)(2,1)}, f32[2,128,128]{2,1,0:T(8,128)}, f32[2,64,128]{2,1,0:T(8,128)}, f32[2,64,128]{2,1,0:T(8,128)}, f32[2,64,128]{...) custom-call(bf16[2,128,128]{2,1,0:T(8,128)(2,1)} %bitcast.4, ...), custom_call_target="tpu_custom_call" | custom-call | tf_op jit(solution)/shard_map/encoder/pallas_call | solution.py:759
  223.4 2.2 results.1
  (1 shorter events, 0.0 us)
Async XLA Ops:
  0.7 0.7 slice-start

commit v5 on v4

--- a/solution.py
+++ b/solution.py
@@ -61,9 +61,9 @@
     v.cot = ((2, s.t, s.d), BF16)
     v.pv = ((L * VEC_ROWS, s.d), F32)
     v.kv = ((L, s.nzx, 2, s.tok, 2 * s.dc), BF16)
-    v.dkv = ((2, s.nzx, 2, s.half, 2 * s.dc), BF16)
-    v.dkv_c = ((L, 2, s.nzx, s.half, 2 * s.dc), BF16)
-    v.dkv_in = ((L, 2, s.nzx, s.half, 2 * s.dc), BF16)
+    v.dkv = ((4, s.nzx, 2, s.qc, 2 * s.dc), BF16)
+    v.dkv_c = ((L, 4, s.nzx, s.qc, 2 * s.dc), BF16)
+    v.dkv_in = ((L, 4, s.nzx, s.qc, 2 * s.dc), BF16)
     v.probs = ((L, len(PAIRS), 2 * s.qc, s.nr * s.qc), BF16)
     v.q2 = ((L, 4, 2 * s.qc, s.dc), BF16)
     v.do2 = ((4, 2 * s.qc, s.dc), BF16)
@@ -112,6 +112,8 @@
     v.segq = ((4, 2 * s.qc, 1), jnp.int32)
     v.segk = ((4, s.nr * s.qc), jnp.int32)
     v.own = ((L * 2 * VEC_ROWS, s.dc), F32)
+    v.late = ((VEC_ROWS, s.dc), F32)
+    v.late_in = ((s.nr, VEC_ROWS, s.dc), F32)
     v.own_in = ((s.nr, L * 2 * VEC_ROWS, s.dc), F32)
     return vars(v)
 
@@ -121,13 +123,13 @@
 OUTPUTS = tuple(dict(o_act=0, o_in=0, o_q=0, o_k=0, o_v=0, o_proj=0, o_up=0, o_down=0, o_vec=0))
 
 (X_IN, COTAN, PVEC, ACT, VEC, OWN, WPT, WDT, GPT, GDT, PR, N1, FR, H, DF, DN, DR, DX,
- WQ, WP, WU, WD, KVA, KVB, DKVA, DKVB, GQ, GP, GU, GD) = range(30)
+ WQ, WP, WU, WD, KV0, KV1, KV2, KV3, DKV0, DKV1, DKV2, DKV3, GQ, GP, GU, GD) = range(34)
 CORE, ACROSS = 1, 2
-IN_STEPS = {(n, l) for n in (WP, WU, WD, KVA, KVB, GP, GU, GD) for l in range(LAYERS)} | {(WQ, 1), (GQ, 1)}
-KV = {KVA: 0, KVB: 1}
-DKV = {DKVA: 0, DKVB: 1}
+IN_STEPS = {(n, l) for n in (WP, WU, WD, KV0, KV1, KV2, KV3, GP, GU, GD) for l in range(LAYERS)} | {(WQ, 1), (GQ, 0), (GQ, 1)}
+KV = {KV0: 0, KV1: 1, KV2: 2, KV3: 3}
+DKV = {DKV0: 0, DKV1: 1, DKV2: 2, DKV3: 3}
 KEYS = (
-    [(n, 0, 0) for n in range(X_IN, GPT)]
+    [(X_IN, 0, 1), (OWN, 0, 1)] + [(n, 0, 0) for n in range(X_IN, GPT)]
     + [(n, l, 0) for n in range(GPT, PR) for l in range(LAYERS)]
     + [(n, l, a) for n in range(PR, WQ) for l in range(LAYERS) for a in range(2)]
     + [(n, l, step) for n in range(WQ, GD + 1) for l in range(LAYERS) for step in range(3)]
@@ -198,7 +200,7 @@
     def weight(name, l):
         chips = s.nzx - (2 if (name, l) in IN_STEPS else 1)
         if name in KV:
-            span = pl.ds(KV[name] * s.half, s.half)
+            span = pl.ds(KV[name] * s.qc, s.qc)
             return ((lambda i, kk: m.kv.at[l, i, kk, span]), (lambda kk: m.kv.at[l, :, kk, span]),
                     m.kv.at[l, pl.ds(0, chips), 0, span] if chips else None)
         if name in (WQ, WU):
@@ -337,8 +339,12 @@
 
     pl.semaphore_wait(barrier, s.nc - 1 + s.nr - 1 + 1 - at_home.astype(jnp.int32))
 
+    def send_x(a):
+        each_col(lambda cc: remote(m.x.at[a], m.xf.at[0, a, :, rows(c, s.dc)], (X_IN, 0, a), r, cc).start())
+
+    send_x(0)
     gather(WQ, 0)
-    each_col(lambda cc: remote(m.x, m.xf.at[0, :, :, rows(c, s.dc)], (X_IN, 0, 0), r, cc).start())
+    send_x(1)
 
     @pl.when(jnp.logical_not(at_home))
     def _():
@@ -357,26 +363,35 @@
         m.segk[i : i + 1, :] = jnp.concatenate([numbers] * (s.nr * s.qc // numbers.shape[1]), axis=1)
     m.vec[...] = jnp.zeros(m.vec.shape, F32)
     m.own[...] = jnp.zeros(m.own.shape, F32)
+    m.late[...] = jnp.zeros(m.late.shape, F32)
 
     def vector(l, which):
         return m.pv[l * VEC_ROWS + which : l * VEC_ROWS + which + 1, :]
+
+    unwaited = []
+    in_flight = [None, None]
+
+    def part_free(a):
+        if in_flight[a] is not None:
+            wait(m.send, in_flight[a], m.got.at[a, pl.ds(0, few)])
 
     def share(buf, value, phase):
         buf[rows(c, s.t), :] = value
         each_col(lambda cc: remote(buf.at[rows(c, s.t)], buf.at[rows(c, s.t)], phase, r, cc).start())
 
     def shared(buf, phase):
-        for sems in (m.recv, m.send):
-            wait(sems, phase, buf.at[pl.ds(0, few * s.t)])
+        wait(m.recv, phase, buf.at[pl.ds(0, few * s.t)])
+        unwaited.append((phase, buf.at[pl.ds(0, few * s.t)]))
 
     def scatter(a, value, phase):
+        part_free(a)
+        in_flight[a] = phase
         m.part[a] = value.astype(BF16)
         each_col(lambda cc: remote(m.part.at[a, rows(cc, s.t)], m.got.at[a, c], phase, r, cc).start())
         m.got[a, c] = m.part[a, rows(c, s.t), :]
 
     def scattered(a, phase):
-        for sems in (m.recv, m.send):
-            wait(sems, phase, m.got.at[a, pl.ds(0, few)])
+        wait(m.recv, phase, m.got.at[a, pl.ds(0, few)])
         total = m.got[a, 0].astype(F32)
         for i in range(1, s.nc):
             total = total + m.got[a, i].astype(F32)
@@ -421,19 +436,6 @@
         m.wdown[l, rows(k, s.fr), rows(zx, s.dc)] = m.wd_own[l]
 
     pass_on(WQ, 0)
-    wait(m.recv, (X_IN, 0, 0), m.xf.at[0, :, :, pl.ds(0, few * s.dc)])
-    wait(m.recv, (PVEC, 0, 0), m.pv.at[:, pl.ds(0, few * s.dc)])
-
-    @pl.when(at_home)
-    def _():
-        m.wp_own[...] = m.wp[...]
-        m.wd_own[...] = m.wd[...]
-
-    @pl.when(jnp.logical_not(at_home))
-    def _():
-        wait(m.recv, (WPT, 0, 0), m.wp_own)
-        wait(m.recv, (WDT, 0, 0), m.wd_own)
-    swapped(0)
 
     def attend(l, i):
         queries = m.q2[l, i]
@@ -459,28 +461,38 @@
         for a in range(2):
             if l:
                 shared(m.xf.at[l, a], (H, l - 1, a))
-            elif a == 0:
-                gathered(WQ, 0)
-                for b in range(2):
-                    m.carry[b] = m.xf[0, b, rows(c, s.t), :].astype(F32)
-            if l and a == 0:
+            else:
+                wait(m.recv, (X_IN, 0, a), m.xf.at[0, a, :, pl.ds(0, few * s.dc)])
+                m.carry[a] = m.xf[0, a, rows(c, s.t), :].astype(F32)
+            if a == 0:
                 gathered(WQ, l)
             qkv = dot(m.xf[l, a], m.wqkv[l].reshape(s.d, 3 * s.dc))
             keep = (qkv[:, 2 * s.dc :] + m.vb[l : l + 1, :].astype(F32)).astype(BF16)
             m.kv[l, zx, k, span(a), : s.dc] = qkv[:, s.dc : 2 * s.dc].astype(BF16)
             m.kv[l, zx, k, span(a), s.dc :] = keep
-            gather(KVA if a == 0 else KVB, l)
+            gather(KV0 + 2 * a, l)
+            gather(KV1 + 2 * a, l)
             for i in range(2):
                 block = (qkv[i * s.qc : (i + 1) * s.qc, : s.dc] + m.qb[l : l + 1, :].astype(F32)).astype(BF16)
                 m.q2[l, 2 * a + i] = (two_heads(block) * HEAD_DIM ** (-0.5)).astype(BF16)
         if l == 0:
+            @pl.when(at_home)
+            def _():
+                m.wp_own[...] = m.wp[...]
+                m.wd_own[...] = m.wd[...]
+
+            @pl.when(jnp.logical_not(at_home))
+            def _():
+                wait(m.recv, (WPT, 0, 0), m.wp_own)
+                wait(m.recv, (WDT, 0, 0), m.wd_own)
+            swapped(0)
             gather(WP, 0)
+        for name in KV:
+            forward(name, l)
         if l == 0:
             forward(WP, 0)
-        forward(KVA, l)
-        forward(KVB, l)
-        pass_on(KVA, l)
-        pass_on(KVB, l)
+        for name in KV:
+            pass_on(name, l)
         if l == 0:
             gather(WU, 0)
             gather(WD, 0)
@@ -488,10 +500,12 @@
         else:
             pass_on(WU, 1)
             pass_on(WD, 1)
-        gathered(KVA, l)
+        gathered(KV0, l)
         attend(l, 0)
-        gathered(KVB, l)
+        gathered(KV1, l)
+        gathered(KV2, l)
         attend(l, 1)
+        gathered(KV3, l)
         gathered(WP, l)
         scatter(0, dot(m.att[l, span(0), :].astype(BF16), m.wproj[l]), (PR, l, 0))
         attend(l, 2)
@@ -501,6 +515,8 @@
             forward(WU, 0)
             forward(WD, 0)
             swapped(1)
+        if l == 0:
+            wait(m.recv, (PVEC, 0, 0), m.pv.at[:, pl.ds(0, few * s.dc)])
         for a in range(2):
             u = scattered(a, (PR, l, a)) + vector(l, PROJ_B) + m.carry[a]
             first_out = norm(u, l, a, GAIN1, SHIFT1, m.n1, m.r1)
@@ -571,9 +587,8 @@
             key_grad = key_grad + dot_tn(score_grad, m.q2[l, i])
             value_grad = value_grad + dot_tn(prob, m.do2[i])
         shape = (s.nzx, 2, s.qc, s.dc)
-        place = pl.ds(j % 2 * s.qc, s.qc)
-        m.dkv[j // 2, :, :, place, pl.ds(0, s.dc)] = key_grad.astype(BF16).reshape(shape)
-        m.dkv[j // 2, :, :, place, pl.ds(s.dc, s.dc)] = value_grad.astype(BF16).reshape(shape)
+        m.dkv[j, :, :, :, pl.ds(0, s.dc)] = key_grad.astype(BF16).reshape(shape)
+        m.dkv[j, :, :, :, pl.ds(s.dc, s.dc)] = value_grad.astype(BF16).reshape(shape)
 
     wait(m.recv, (COTAN, 0, 0), m.cot.at[:, :, pl.ds(0, few * s.dc)])
     for l in reversed(range(L)):
@@ -595,7 +610,9 @@
             m.act_in[:, rows(c, s.t), :] = m.act_out[:, :, rows(c, s.dc)]
         else:
             reduce_mid(GQ, l + 1)
-            reduce_turn(GP, l + 1)
+            reduce_turn(GU, l + 1)
+            swap_back(l + 1, GD, reduce_end(GD, l + 1))
+            swap_back(l + 1, GP, reduce_end(GP, l + 1))
         for a in range(2):
             shared(m.dff.at[l, a], (DF, l, a))
             de = (dot_nt(m.dff[l, a], m.wdown[l]) * m.slope[l, a]).astype(BF16)
@@ -606,7 +623,7 @@
                 m.own[own + i : own + i + 1, :] += sums[:, i * LANES : (i + 1) * LANES]
         if l + 1 < L:
             reduce_turn(GQ, l + 1)
-            swap_back(l + 1, GP, reduce_end(GP, l + 1))
+            m.o_up[l + 1] = reduce_end(GU, l + 1)
             sent_half(GD, l + 1)
             sent_half(GU, l + 1)
         m.gdown[...] = dot_tn(m.gate[l].reshape(s.tok, s.fc), m.dff[l].reshape(s.tok, s.d)).astype(BF16)
@@ -621,12 +638,18 @@
         m.gup[...] = dot_tn(m.x1[l].reshape(s.tok, s.d), m.de[...].reshape(s.tok, s.fc)).astype(BF16).reshape(m.gup.shape)
         reduce_start(GU, l)
         reduce_mid(GD, l)
+        if l + 1 < L:
+            swap_end(l + 1, GD, m.o_down)
+            swap_end(l + 1, GP, m.o_proj)
+            total = reduce_end(GQ, l + 1)
+            for which, out in enumerate((m.o_q, m.o_k, m.o_v)):
+                out[l + 1] = total[:, which * s.dc : (which + 1) * s.dc]
         if l == 0:
             each_col(lambda cc: remote(m.vec.at[:, rows(cc, s.dc)], m.vec_in.at[c], (VEC, 0, 0), r, cc).start())
             m.vec_in[c] = m.vec[:, rows(c, s.dc)]
         if l + 1 < L:
-            sent_half(DKVA, l + 1)
-            sent_half(DKVB, l + 1)
+            for name in DKV:
+                sent_half(name, l + 1)
         for a in range(2):
             shared(m.drf.at[l, a], (DR, l, a))
             dout = dot_nt(m.drf[l, a], m.wproj[l]).astype(BF16)
@@ -639,23 +662,41 @@
                 m.dq2[i] = jnp.zeros((2 * s.qc, s.dc), F32)
             if a == 0:
                 attend_back(l, 0)
-                reduce_mid(GU, l)
+                reduce_start(DKV0, l)
+        if l + 1 < L:
+            sent_half(GP, l + 1)
+        m.gproj[...] = dot_tn(m.att[l].astype(BF16), m.drf[l].reshape(s.tok, s.d)).astype(BF16)
+        reduce_start(GP, l)
         attend_back(l, 1)
-        reduce_start(DKVA, l)
+        reduce_start(DKV1, l)
+        reduce_mid(DKV0, l)
         attend_back(l, 2)
-        reduce_mid(DKVA, l)
+        reduce_start(DKV2, l)
+        reduce_mid(DKV1, l)
+        reduce_mid(GP, l)
         attend_back(l, 3)
-        reduce_start(DKVB, l)
+        reduce_start(DKV3, l)
+        reduce_mid(DKV2, l)
         for i in range(4):
             m.dqkv[i * s.qc : (i + 1) * s.qc, : s.dc] = (one_block(m.dq2[i]) * HEAD_DIM ** (-0.5)).astype(BF16)
-        reduce_mid(DKVB, l)
+        reduce_mid(DKV3, l)
+        reduce_mid(GU, l)
         reduce_turn(GD, l)
+        for a in range(2):
+            for j in (2 * a, 2 * a + 1):
+                m.dqkv[j * s.qc : (j + 1) * s.qc, s.dc :] = reduce_end(DKV0 + j, l).astype(BF16)
+            back = dot_nt(m.dqkv[span(a), :], m.wqkv[l].reshape(s.d, 3 * s.dc))
+            if l:
+                scatter(a, back, (DX, l, a))
+            else:
+                part_free(a)
+                m.part[a] = back.astype(BF16)
+                mine = m.part[a, rows(c, s.t), :].astype(F32) + m.carry[a]
+                m.part[a, rows(c, s.t), :] = mine.astype(BF16)
+                each_col(lambda cc: remote(m.part.at[a, :, rows(cc, s.dc)], m.got_in.at[a, c], (DX, 0, a), r, cc).start())
+                m.got_in[a, c] = m.part[a, :, rows(c, s.dc)]
         if l + 1 < L:
-            sent_half(GP, l + 1)
             sent_half(GQ, l + 1)
-        m.gproj[...] = dot_tn(m.att[l].astype(BF16), m.drf[l].reshape(s.tok, s.d)).astype(BF16)
-        reduce_start(GP, l)
-        reduce_turn(GU, l)
         if l == 0:
             wait(m.recv, (VEC, 0, 0), m.vec_in.at[pl.ds(0, few)])
             total = m.vec_in[0]
@@ -664,57 +705,53 @@
             for i in range(L):
                 to = i * 2 * VEC_ROWS + VEC_ROWS
                 m.own[to : to + VEC_ROWS, :] = total[i * VEC_ROWS : (i + 1) * VEC_ROWS]
-        for a in range(2):
-            m.dqkv[span(a), s.dc :] = reduce_end(DKVA if a == 0 else DKVB, l).astype(BF16)
-            back = dot_nt(m.dqkv[span(a), :], m.wqkv[l].reshape(s.d, 3 * s.dc))
-            if l:
-                scatter(a, back, (DX, l, a))
-            else:
-                m.part[a] = back.astype(BF16)
-                mine = m.part[a, rows(c, s.t), :].astype(F32) + m.carry[a]
-                m.part[a, rows(c, s.t), :] = mine.astype(BF16)
-                each_col(lambda cc: remote(m.part.at[a, :, rows(cc, s.dc)], m.got_in.at[a, c], (DX, 0, a), r, cc).start())
-                m.got_in[a, c] = m.part[a, :, rows(c, s.dc)]
+            m.own_in[r] = m.own[...]
+            each_row(lambda rr: remote(m.own, m.own_in.at[r], (OWN, 0, 0), rr, c).start())
         m.gqkv[...] = dot_tn(m.xf[l].reshape(s.tok, s.d), m.dqkv[...]).astype(BF16).reshape(m.gqkv.shape)
         reduce_start(GQ, l)
         sums = jnp.sum(m.dqkv[...].astype(F32), axis=0, keepdims=True)
-        m.own[own + 4 : own + 5, :] = sums[:, : s.dc]
-        m.own[own + 5 : own + 6, :] = sums[:, 2 * s.dc :]
-        reduce_mid(GP, l)
-        swap_back(l, GD, reduce_end(GD, l))
-        m.o_up[l] = reduce_end(GU, l)
-        if l + 1 < L:
-            swap_end(l + 1, GD, m.o_down)
-            swap_end(l + 1, GP, m.o_proj)
-            total = reduce_end(GQ, l + 1)
-            for which, out in enumerate((m.o_q, m.o_k, m.o_v)):
-                out[l + 1] = total[:, which * s.dc : (which + 1) * s.dc]
-
-    m.own_in[r] = m.own[...]
-    each_row(lambda rr: remote(m.own, m.own_in.at[r], (OWN, 0, 0), rr, c).start())
+        late, to = (m.own, own + 4) if l else (m.late, 0)
+        late[to : to + 1, :] = sums[:, : s.dc]
+        late[to + 1 : to + 2, :] = sums[:, 2 * s.dc :]
+        reduce_turn(GP, l)
+        if l == 0:
+            reduce_turn(GU, l)
+            swap_back(l, GD, reduce_end(GD, l))
+
+    m.late_in[r] = m.late[...]
+    each_row(lambda rr: remote(m.late, m.late_in.at[r], (OWN, 0, 1), rr, c).start())
     reduce_mid(GQ, 0)
-    reduce_turn(GP, 0)
-    swap_end(0, GD, m.o_down)
     wait(m.recv, (ACT, 0, 0), m.act_in.at[:, pl.ds(0, few * s.t)])
     m.o_act[...] = m.act_in[...]
+    swap_back(0, GP, reduce_end(GP, 0))
+    m.o_up[0] = reduce_end(GU, 0)
+    reduce_turn(GQ, 0)
+    swap_end(0, GD, m.o_down)
     for a in range(2):
         wait(m.recv, (DX, 0, a), m.got_in.at[a, pl.ds(0, few)])
         total = m.got_in[a, 0].astype(F32)
         for i in range(1, s.nc):
             total = total + m.got_in[a, i].astype(F32)
         m.o_in[a] = total
-    swap_back(0, GP, reduce_end(GP, 0))
     wait(m.recv, (OWN, 0, 0), m.own_in.at[pl.ds(0, s.nr - 1)])
     total = m.own_in[0]
     for i in range(1, s.nr):
         total = total + m.own_in[i]
     m.o_vec[...] = total
+    wait(m.recv, (OWN, 0, 1), m.late_in.at[pl.ds(0, s.nr - 1)])
+    total = m.late_in[0]
+    for i in range(1, s.nr):
+        total = total + m.late_in[i]
+    m.o_vec[4:6, :] = total[:2]
     total = reduce_end(GQ, 0)
     for which, out in enumerate((m.o_q, m.o_k, m.o_v)):
         out[0] = total[:, which * s.dc : (which + 1) * s.dc]
     swap_end(0, GP, m.o_proj)
 
-    wait(m.send, (X_IN, 0, 0), m.xf.at[0, :, :, pl.ds(0, few * s.dc)])
+    for phase, ref in unwaited:
+        wait(m.send, phase, ref)
+    for a in range(2):
+        wait(m.send, (X_IN, 0, a), m.xf.at[0, a, :, pl.ds(0, few * s.dc)])
     wait(m.send, (PVEC, 0, 0), m.pv.at[:, pl.ds(0, few * s.dc)])
     wait(m.send, (COTAN, 0, 0), m.cot.at[:, :, pl.ds(0, few * s.dc)])
     wait(m.send, (ACT, 0, 0), m.act_in.at[:, pl.ds(0, few * s.t)])
@@ -722,6 +759,7 @@
         wait(m.send, (DX, 0, a), m.got_in.at[a, pl.ds(0, few)])
     wait(m.send, (VEC, 0, 0), m.vec_in.at[pl.ds(0, few)])
     wait(m.send, (OWN, 0, 0), m.own_in.at[pl.ds(0, s.nr - 1)])
+    wait(m.send, (OWN, 0, 1), m.late_in.at[pl.ds(0, s.nr - 1)])
 
     @pl.when(jnp.logical_not(at_home))
     def _():
@@ -731,11 +769,11 @@
             wait(m.send, (GPT, l, 0), m.gproj_fin.at[l])
             wait(m.send, (GDT, l, 0), m.gdown_fin.at[l])
     for l in range(L):
-        for name in (WQ, WP, WU, WD, KVA, KVB):
+        for name in (WQ, WP, WU, WD, *KV):
             sent_gather(name, l)
-        for name in (GQ, GP, GU, GD, DKVA, DKVB):
+        for name in (GQ, GP, GU, GD, *DKV):
             sent_pieces(name, l)
-    for name in (GQ, GP, GU, GD, DKVA, DKVB):
+    for name in (GQ, GP, GU, GD, *DKV):
         sent_half(name, 0)
 
 

time: 229 us -> 220 us (0.961); the launches traced: 226 us -> 220 us
  Pallas kernels: 224 us -> 218 us
    pallas_call x1, Pallas kernels: 221 us -> 215 us  [body(): pl.pallas_call(functools.partial(kernel, s), out_shape=out_shape, in_spec...]
where the time goes in v5:
time: 220 us
  Pallas kernels  218 us (99%)
    pallas_call x1, Pallas kernels, body(): pl.pallas_call(functools.partial(kernel, s), out_shape=out_shape, in_spec...  215 us

profile of v5, /device:TPU:2, one launch (start us, length us, event | category | flops | bytes accessed | tf_op | source)
XLA Modules:
  0.0 219.9 jit_solution(10894419997369689056)
XLA Ops:
  0.7 0.0 slice-start
  0.7 0.7 slice-done
  1.3 0.1 tile.10
  1.4 0.7 tile.12.refs_17_
  2.1 215.5 %encoder.1 = (bf16[2,128,128]{2,1,0:T(8,128)(2,1)}, f32[2,128,128]{2,1,0:T(8,128)}, f32[2,64,128]{2,1,0:T(8,128)}, f32[2,64,128]{2,1,0:T(8,128)}, f32[2,64,128]{...) custom-call(bf16[2,128,128]{2,1,0:T(8,128)(2,1)} %bitcast.4, ...), custom_call_target="tpu_custom_call" | custom-call | tf_op jit(solution)/shard_map/encoder/pallas_call | solution.py:797
  217.6 2.2 %results.1 = (bf16[2,128,128]{2,1,0:T(8,128)(2,1)}, f32[2,128,128]{2,1,0:T(8,128)}, f32[2,64,128]{2,1,0:T(8,128)}, f32[2,64,128]{2,1,0:T(8,128)}, f32[2,64,128]{...) custom-call(bf16[2,128,128]{2,1,0:T(8,128)(2,1)} %get-tuple-element., ...), custom_call_target="tpu_custom_call" | custom-call | tf_op jit(solution)/shard_map/results/pallas_call | solution.py:811
  (1 shorter events, 0.0 us)
Async XLA Ops:
  0.7 0.7 slice-start

commit v6 on v5

--- a/solution.py
+++ b/solution.py
@@ -352,8 +352,6 @@
         remote(m.wd, m.wd_own, (WDT, 0, 0), swap_row, swap_col).start()
     mine = m.pv.at[:, rows(c, s.dc)]
     each_col(lambda cc: remote(mine, mine, (PVEC, 0, 0), r, cc).start())
-    each_col(lambda cc: remote(
-        m.cotan.at[:, rows(cc, s.t)], m.cot.at[:, :, rows(c, s.dc)], (COTAN, 0, 0), r, cc).start())
     square = (s.qc, s.qc)
     diagonal = lax.broadcasted_iota(jnp.int32, square, 0) == lax.broadcasted_iota(jnp.int32, square, 1)
     for i in range(4):
@@ -498,8 +496,8 @@
             gather(WD, 0)
             pass_on(WP, 0)
         else:
-            pass_on(WU, 1)
-            pass_on(WD, 1)
+            forward(WU, 1)
+            forward(WD, 1)
         gathered(KV0, l)
         attend(l, 0)
         gathered(KV1, l)
@@ -522,11 +520,14 @@
             first_out = norm(u, l, a, GAIN1, SHIFT1, m.n1, m.r1)
             share(m.x1.at[l, a], first_out.astype(BF16), (N1, l, a))
             m.carry[a] = first_out
-        if l == 0:
-            pass_on(WU, 0)
-            pass_on(WD, 0)
+        pass_on(WU, l)
+        pass_on(WD, l)
+        if l == 0:
             gather(WQ, 1)
             gather(WP, 1)
+        else:
+            each_col(lambda cc: remote(
+                m.cotan.at[:, rows(cc, s.t)], m.cot.at[:, :, rows(c, s.dc)], (COTAN, 0, 0), r, cc).start())
         gathered(WU, l)
         for a in range(2):
             shared(m.x1.at[l, a], (N1, l, a))
@@ -553,8 +554,6 @@
         if l == 0:
             pass_on(WQ, 1)
             pass_on(WP, 1)
-            forward(WU, 1)
-            forward(WD, 1)
 
     def swap_back(l, name, total):
         out, fin, phase = {GP: (m.gproj_out, m.gproj_fin, (GPT, l, 0)), GD: (m.gdown_out, m.gdown_fin, (GDT, l, 0))}[name]

time: 220 us -> 220 us (level)
  no operation moved by 1% of the time
where the time goes in v6:
time: 220 us
  Pallas kernels  217 us (99%)
    pallas_call x1, Pallas kernels, body(): pl.pallas_call(functools.partial(kernel, s), out_shape=out_shape, in_spec...  215 us

profile of v6, /device:TPU:2, one launch (start us, length us, event | category | flops | bytes accessed | tf_op | source)
XLA Modules:
  0.0 219.6 jit_solution(14451278045821899167)
XLA Ops:
  0.7 0.0 slice-start
  0.7 0.7 slice-done
  1.3 0.1 tile.10
  1.4 0.7 tile.12.refs_17_
  2.1 215.2 %encoder.1 = (bf16[2,128,128]{2,1,0:T(8,128)(2,1)}, f32[2,128,128]{2,1,0:T(8,128)}, f32[2,64,128]{2,1,0:T(8,128)}, f32[2,64,128]{2,1,0:T(8,128)}, f32[2,64,128]{...) custom-call(bf16[2,128,128]{2,1,0:T(8,128)(2,1)} %bitcast.4, ...), custom_call_target="tpu_custom_call" | custom-call | tf_op jit(solution)/shard_map/encoder/pallas_call | solution.py:796
  217.3 2.2 %results.1 = (bf16[2,128,128]{2,1,0:T(8,128)(2,1)}, f32[2,128,128]{2,1,0:T(8,128)}, f32[2,64,128]{2,1,0:T(8,128)}, f32[2,64,128]{2,1,0:T(8,128)}, f32[2,64,128]{...) custom-call(bf16[2,128,128]{2,1,0:T(8,128)(2,1)} %get-tuple-element., ...), custom_call_target="tpu_custom_call" | custom-call | tf_op jit(solution)/shard_map/results/pallas_call | solution.py:810
  (1 shorter events, 0.0 us)
Async XLA Ops:
  0.7 0.7 slice-start
